TPU v7x, 32 devices: a whole 2x2x4 slice. The times are simulated.
32 devices in a mesh: fsdp: 2 (over y), ctx: 4 (over z), tp: 4 (over x, core).
Axes of the slice: x: 2, y: 2, z: 4, core: 2. Of those that a mesh axis runs over, the one named last changes fastest.
Arguments:
- block_in: bfloat16 [8, 2048, 768], P('fsdp', ('ctx', 'tp')), may hold values from -6 to 6
- segments: int32 [8, 2048], P('fsdp'), may hold values from 0 to 10, as said below
- ln1_gain: bfloat16 [768], P('fsdp'), may hold values from 0.5 to 1.5
- ln1_shift: bfloat16 [768], P('fsdp'), may hold values from -1 to 1
- w_qkv: bfloat16 [3, 768, 768], P(None, ('tp', 'fsdp')), may hold values from -0.21875 to 0.21875
- b_qv: bfloat16 [12, 128], P('tp', 'fsdp'), may hold values from -1.796875 to 1.796875
- w_out: bfloat16 [768, 768], P(('tp', 'fsdp')), may hold values from -0.875 to 0.875
- b_out: bfloat16 [768], P('fsdp'), may hold values from -1 to 1
- ln2_gain: bfloat16 [768], P('fsdp'), may hold values from 0.5 to 1.5
- ln2_shift: bfloat16 [768], P('fsdp'), may hold values from -1 to 1
- w_up: bfloat16 [768, 3072], P('fsdp', 'tp'), may hold values from -0.21875 to 0.21875
- b_up: bfloat16 [12, 256], P('tp', 'fsdp'), may hold values from -1.796875 to 1.796875
- w_down: bfloat16 [3072, 768], P(('tp', 'fsdp')), may hold values from -0.109375 to 0.109375
- b_down: bfloat16 [768], P('fsdp'), may hold values from -1 to 1
- cotangent: bfloat16 [8, 2048, 768], P('fsdp', ('ctx', 'tp')), may hold values from -6 to 6
Outputs:
- block_out: bfloat16 [8, 2048, 768], P('fsdp', ('ctx', 'tp'))
- grad_x: bfloat16 [8, 2048, 768], P('fsdp', ('ctx', 'tp'))
- grad_ln1_gain: float32 [768], P('fsdp')
- grad_ln1_shift: float32 [768], P('fsdp')
- grad_w_qkv: float32 [3, 768, 768], P(None, ('tp', 'fsdp'))
- grad_b_qv: float32 [12, 128], P('tp', 'fsdp')
- grad_w_out: float32 [768, 768], P(('tp', 'fsdp'))
- grad_b_out: float32 [768], P('fsdp')
- grad_ln2_gain: float32 [768], P('fsdp')
- grad_ln2_shift: float32 [768], P('fsdp')
- grad_w_up: float32 [768, 3072], P('fsdp', 'tp')
- grad_b_up: float32 [12, 256], P('tp', 'fsdp')
- grad_w_down: float32 [3072, 768], P(('tp', 'fsdp'))
- grad_b_down: float32 [768], P('fsdp')
Inputs may be any that keep to these rules, and one draw needn't show every extreme that they name: `segments`: within each sequence the numbers start at 0 and never fall; positions with one number form one document. In each aligned block of 4 sequences, one sequence's first document covers at least its first 1793 positions; other documents are at least 204 long except a sequence's last one.
All inputs are finite; a program needn't handle non-finite values.
Results may differ from a plain program's by a relative error of at most 0.02.
Values may be sent and summed in bfloat16 or wider, within the bound.
No kernel may reach another device: no remote copies, remote signals or barrier semaphores. Data moves between devices by JAX's collectives and lax.ppermute only.
A program may use at most 256 MiB of HBM per device.

v0:
```python
import jax
import jax.numpy as jnp
from jax import lax
from jax.sharding import PartitionSpec as P

EPS = 1e-05


def layer_norm(values, ln_gain, ln_shift):
    center = values - jnp.mean(values, axis=-1, keepdims=True)
    spread = jnp.mean(center * center, axis=-1, keepdims=True)
    return center * lax.rsqrt(spread + EPS) * ln_gain + ln_shift


def gelu_tanh(inputs):
    return jax.nn.gelu(inputs, approximate=True)


def contract_rows(left, right):
    return lax.dot_general(
        left, right, (((0,), (0,)), ((), ())), preferred_element_type=jnp.float32
    )


def contract_cols(left, right):
    return lax.dot_general(
        left, right, (((1,), (1,)), ((), ())), preferred_element_type=jnp.float32
    )


def on_device(
    block_in,
    segments,
    ln1_gain,
    ln1_shift,
    w_qkv,
    b_qv,
    w_out,
    b_out,
    ln2_gain,
    ln2_shift,
    w_up,
    b_up,
    w_down,
    b_down,
    cotangent,
):
    sub_len = block_in.shape[1]
    whole_x, whole_cot = (
        lax.all_gather(block_in, "tp", axis=1, tiled=True),
        lax.all_gather(cotangent, "tp", axis=1, tiled=True),
    )
    seq_local, group_len, width = whole_x.shape
    token_count = seq_local * group_len
    (
        gain_one,
        shift_one,
        qkv_mat,
        qv_bias,
        out_mat,
        out_bias,
        gain_two,
        shift_two,
        up_mat,
        up_bias,
        down_mat,
        down_bias,
    ) = (
        lax.all_gather(ln1_gain, "fsdp", axis=0, tiled=True),
        lax.all_gather(ln1_shift, "fsdp", axis=0, tiled=True),
        lax.all_gather(w_qkv, "fsdp", axis=1, tiled=True),
        lax.all_gather(b_qv, "fsdp", axis=1, tiled=True),
        lax.all_gather(w_out, "fsdp", axis=0, tiled=True),
        lax.all_gather(b_out, "fsdp", axis=0, tiled=True),
        lax.all_gather(ln2_gain, "fsdp", axis=0, tiled=True),
        lax.all_gather(ln2_shift, "fsdp", axis=0, tiled=True),
        lax.all_gather(w_up, "fsdp", axis=0, tiled=True),
        lax.all_gather(b_up, "fsdp", axis=1, tiled=True),
        lax.all_gather(w_down, "fsdp", axis=0, tiled=True),
        lax.all_gather(b_down, "fsdp", axis=0, tiled=True),
    )
    head_count = qv_bias.shape[0]
    head_size = qv_bias.shape[1] // 2
    local_width = head_count * head_size
    tp_rank = lax.axis_index("tp")
    ctx_rank = lax.axis_index("ctx")
    ctx_count = lax.axis_size("ctx")
    scaling = head_size ** (-0.5)
    x_float = whole_x.reshape(token_count, width).astype(jnp.float32)
    normed_one, ln1_pull = jax.vjp(
        layer_norm, x_float, gain_one.astype(jnp.float32), shift_one.astype(jnp.float32)
    )
    normed_one = normed_one.astype(jnp.bfloat16)
    projected = contract_cols(normed_one, qkv_mat.reshape(3 * local_width, width))
    projected = projected.reshape(seq_local, group_len, 3, head_count, head_size)
    bias_float = qv_bias.astype(jnp.float32)
    queries = (projected[:, :, 0] + bias_float[:, :head_size]).astype(jnp.bfloat16)
    keys_local = projected[:, :, 1].astype(jnp.bfloat16)
    values_local = (projected[:, :, 2] + bias_float[:, head_size:]).astype(jnp.bfloat16)
    key_all, value_all = (
        lax.all_gather(keys_local, "ctx", axis=1, tiled=True),
        lax.all_gather(values_local, "ctx", axis=1, tiled=True),
    )
    query_place = ctx_rank * group_len + jnp.arange(group_len)
    key_place = jnp.arange(group_len * ctx_count)
    query_segs = lax.dynamic_slice_in_dim(segments, ctx_rank * group_len, group_len, 1)

    def allowed_of(query_seg, key_seg):
        return (query_seg[:, None] == key_seg[None, :]) & (
            key_place[None, :] <= query_place[:, None]
        )

    def attend(blocks):
        query_blk, key_blk, value_blk, query_seg, key_seg = blocks
        allowed = allowed_of(query_seg, key_seg)[None]
        scores = (
            jnp.einsum("chd,khd->hck", query_blk, key_blk, preferred_element_type=jnp.float32)
            * scaling
        )
        scores = jnp.where(allowed, scores, -1e30)
        peak_score = jnp.max(scores, axis=-1, keepdims=True)
        exponent = jnp.exp(scores - peak_score)
        row_total = jnp.sum(exponent, axis=-1, keepdims=True)
        weights = (exponent / row_total).astype(jnp.bfloat16)
        mixed_out = jnp.einsum(
            "hck,khd->chd", weights, value_blk, preferred_element_type=jnp.float32
        )
        return (mixed_out, (peak_score + jnp.log(row_total))[..., 0])

    attended, log_total = lax.map(attend, (queries, key_all, value_all, query_segs, segments))
    merged = attended.reshape(token_count, local_width).astype(jnp.bfloat16)
    attn_full = lax.psum(
        jnp.dot(merged, out_mat, preferred_element_type=jnp.float32).astype(jnp.bfloat16), "tp"
    ).astype(jnp.float32)
    hidden = x_float + attn_full + out_bias.astype(jnp.float32)
    normed_two, ln2_pull = jax.vjp(
        layer_norm, hidden, gain_two.astype(jnp.float32), shift_two.astype(jnp.float32)
    )
    normed_two = normed_two.astype(jnp.bfloat16)
    pre_act = jnp.dot(normed_two, up_mat, preferred_element_type=jnp.float32) + up_bias.reshape(
        -1
    ).astype(jnp.float32)
    activ, gelu_pull = jax.vjp(gelu_tanh, pre_act)
    activ = activ.astype(jnp.bfloat16)
    down_part = jnp.dot(activ, down_mat, preferred_element_type=jnp.float32).reshape(
        seq_local, group_len, width
    )
    mlp_share = lax.psum_scatter(
        down_part.astype(jnp.bfloat16), "tp", scatter_dimension=1, tiled=True
    ).astype(jnp.float32)
    hidden_share = lax.dynamic_slice_in_dim(
        hidden.reshape(seq_local, group_len, width), tp_rank * sub_len, sub_len, 1
    )
    block_out = (hidden_share + mlp_share + down_bias.astype(jnp.float32)).astype(jnp.bfloat16)
    qkv_back, out_back, up_back, down_back = (
        lax.all_gather(w_qkv, "fsdp", axis=1, tiled=True),
        lax.all_gather(w_out, "fsdp", axis=0, tiled=True),
        lax.all_gather(w_up, "fsdp", axis=0, tiled=True),
        lax.all_gather(w_down, "fsdp", axis=0, tiled=True),
    )
    key_back, value_back = (
        lax.all_gather(keys_local, "ctx", axis=1, tiled=True),
        lax.all_gather(values_local, "ctx", axis=1, tiled=True),
    )
    cot_rows = whole_cot.reshape(token_count, width)
    cot_float = cot_rows.astype(jnp.float32)
    grad_down_bias = jnp.sum(cot_float, axis=0)
    grad_down = contract_rows(activ, cot_rows)
    grad_activ = contract_cols(cot_rows, down_back)
    grad_pre = gelu_pull(grad_activ)[0].astype(jnp.bfloat16)
    grad_up_bias = jnp.sum(grad_pre.astype(jnp.float32), axis=0).reshape(up_bias.shape)
    grad_up = contract_rows(normed_two, grad_pre)
    grad_normed_two = lax.psum(contract_cols(grad_pre, up_back).astype(jnp.bfloat16), "tp").astype(
        jnp.float32
    )
    grad_hidden_norm, grad_gain_two, grad_shift_two = ln2_pull(grad_normed_two)
    grad_hidden = cot_float + grad_hidden_norm
    grad_out_bias = jnp.sum(grad_hidden, axis=0)
    grad_branch = grad_hidden.astype(jnp.bfloat16)
    grad_out = contract_rows(merged, grad_branch)
    grad_merged = contract_cols(grad_branch, out_back).astype(jnp.bfloat16)
    grad_merged = grad_merged.reshape(seq_local, group_len, head_count, head_size)

    def attend_back(blocks):
        query_blk, key_blk, value_blk, grad_blk, log_blk, query_seg, key_seg = blocks
        allowed = allowed_of(query_seg, key_seg)[None]
        scores = (
            jnp.einsum("chd,khd->hck", query_blk, key_blk, preferred_element_type=jnp.float32)
            * scaling
        )
        probs = jnp.where(allowed, jnp.exp(scores - log_blk[..., None]), 0.0)
        grad_probs = jnp.einsum(
            "chd,khd->hck", grad_blk, value_blk, preferred_element_type=jnp.float32
        )
        centred = jnp.sum(probs * grad_probs, axis=-1, keepdims=True)
        grad_scores = (probs * (grad_probs - centred)).astype(jnp.bfloat16)
        grad_query = (
            jnp.einsum("hck,khd->chd", grad_scores, key_blk, preferred_element_type=jnp.float32)
            * scaling
        )
        grad_key = (
            jnp.einsum("hck,chd->khd", grad_scores, query_blk, preferred_element_type=jnp.float32)
            * scaling
        )
        grad_value = jnp.einsum(
            "hck,chd->khd", probs.astype(jnp.bfloat16), grad_blk, preferred_element_type=jnp.float32
        )
        return (grad_query, grad_key, grad_value)

    grad_queries, grad_keys_all, grad_values_all = lax.map(
        attend_back, (queries, key_back, value_back, grad_merged, log_total, query_segs, segments)
    )
    grad_keys, grad_values = (
        lax.psum_scatter(
            grad_keys_all.astype(jnp.bfloat16), "ctx", scatter_dimension=1, tiled=True
        ).astype(jnp.float32),
        lax.psum_scatter(
            grad_values_all.astype(jnp.bfloat16), "ctx", scatter_dimension=1, tiled=True
        ).astype(jnp.float32),
    )
    query_low = grad_queries.astype(jnp.bfloat16)
    key_low = grad_keys.astype(jnp.bfloat16)
    value_low = grad_values.astype(jnp.bfloat16)
    grad_qv_bias = jnp.concatenate(
        [
            jnp.sum(query_low.astype(jnp.float32), axis=(0, 1)),
            jnp.sum(value_low.astype(jnp.float32), axis=(0, 1)),
        ],
        axis=-1,
    )
    grad_proj = jnp.stack([query_low, key_low, value_low], axis=2).reshape(
        token_count, 3 * local_width
    )
    grad_qkv = contract_rows(grad_proj, normed_one).reshape(3, local_width, width)
    grad_normed_one = lax.psum(
        jnp.dot(
            grad_proj, qkv_back.reshape(3 * local_width, width), preferred_element_type=jnp.float32
        ).astype(jnp.bfloat16),
        "tp",
    ).astype(jnp.float32)
    grad_x_norm, grad_gain_one, grad_shift_one = ln1_pull(grad_normed_one)
    grad_x_full = (grad_hidden + grad_x_norm).reshape(seq_local, group_len, width)
    grad_input = lax.dynamic_slice_in_dim(grad_x_full, tp_rank * sub_len, sub_len, 1).astype(
        jnp.bfloat16
    )
    (
        sum_gain_one,
        sum_shift_one,
        sum_qkv,
        sum_qv_bias,
        sum_out,
        sum_out_bias,
        sum_gain_two,
        sum_shift_two,
        sum_up,
        sum_up_bias,
        sum_down,
        sum_down_bias,
    ) = (
        lax.psum(grad_gain_one.astype(jnp.bfloat16), "ctx").astype(jnp.float32),
        lax.psum(grad_shift_one.astype(jnp.bfloat16), "ctx").astype(jnp.float32),
        lax.psum(grad_qkv.astype(jnp.bfloat16), "ctx").astype(jnp.float32),
        lax.psum(grad_qv_bias.astype(jnp.bfloat16), "ctx").astype(jnp.float32),
        lax.psum(grad_out.astype(jnp.bfloat16), "ctx").astype(jnp.float32),
        lax.psum(grad_out_bias.astype(jnp.bfloat16), "ctx").astype(jnp.float32),
        lax.psum(grad_gain_two.astype(jnp.bfloat16), "ctx").astype(jnp.float32),
        lax.psum(grad_shift_two.astype(jnp.bfloat16), "ctx").astype(jnp.float32),
        lax.psum(grad_up.astype(jnp.bfloat16), "ctx").astype(jnp.float32),
        lax.psum(grad_up_bias.astype(jnp.bfloat16), "ctx").astype(jnp.float32),
        lax.psum(grad_down.astype(jnp.bfloat16), "ctx").astype(jnp.float32),
        lax.psum(grad_down_bias.astype(jnp.bfloat16), "ctx").astype(jnp.float32),
    )
    owned = (
        lax.psum_scatter(
            sum_gain_one.astype(jnp.bfloat16), "fsdp", scatter_dimension=0, tiled=True
        ).astype(jnp.float32),
        lax.psum_scatter(
            sum_shift_one.astype(jnp.bfloat16), "fsdp", scatter_dimension=0, tiled=True
        ).astype(jnp.float32),
        lax.psum_scatter(
            sum_qkv.astype(jnp.bfloat16), "fsdp", scatter_dimension=1, tiled=True
        ).astype(jnp.float32),
        lax.psum_scatter(
            sum_qv_bias.astype(jnp.bfloat16), "fsdp", scatter_dimension=1, tiled=True
        ).astype(jnp.float32),
        lax.psum_scatter(
            sum_out.astype(jnp.bfloat16), "fsdp", scatter_dimension=0, tiled=True
        ).astype(jnp.float32),
        lax.psum_scatter(
            sum_out_bias.astype(jnp.bfloat16), "fsdp", scatter_dimension=0, tiled=True
        ).astype(jnp.float32),
        lax.psum_scatter(
            sum_gain_two.astype(jnp.bfloat16), "fsdp", scatter_dimension=0, tiled=True
        ).astype(jnp.float32),
        lax.psum_scatter(
            sum_shift_two.astype(jnp.bfloat16), "fsdp", scatter_dimension=0, tiled=True
        ).astype(jnp.float32),
        lax.psum_scatter(
            sum_up.astype(jnp.bfloat16), "fsdp", scatter_dimension=0, tiled=True
        ).astype(jnp.float32),
        lax.psum_scatter(
            sum_up_bias.astype(jnp.bfloat16), "fsdp", scatter_dimension=1, tiled=True
        ).astype(jnp.float32),
        lax.psum_scatter(
            sum_down.astype(jnp.bfloat16), "fsdp", scatter_dimension=0, tiled=True
        ).astype(jnp.float32),
        lax.psum_scatter(
            sum_down_bias.astype(jnp.bfloat16), "fsdp", scatter_dimension=0, tiled=True
        ).astype(jnp.float32),
    )
    return (block_out, grad_input) + tuple(owned)


def solution(mesh):
    in_specs = (
        P("fsdp", ("ctx", "tp"), None),
        P("fsdp", None),
        P("fsdp"),
        P("fsdp"),
        P(None, ("tp", "fsdp"), None),
        P("tp", "fsdp"),
        P(("tp", "fsdp"), None),
        P("fsdp"),
        P("fsdp"),
        P("fsdp"),
        P("fsdp", "tp"),
        P("tp", "fsdp"),
        P(("tp", "fsdp"), None),
        P("fsdp"),
        P("fsdp", ("ctx", "tp"), None),
    )
    out_specs = (
        P("fsdp", ("ctx", "tp"), None),
        P("fsdp", ("ctx", "tp"), None),
        P("fsdp"),
        P("fsdp"),
        P(None, ("tp", "fsdp"), None),
        P("tp", "fsdp"),
        P(("tp", "fsdp"), None),
        P("fsdp"),
        P("fsdp"),
        P("fsdp"),
        P("fsdp", "tp"),
        P("tp", "fsdp"),
        P(("tp", "fsdp"), None),
        P("fsdp"),
    )
    return jax.shard_map(
        on_device, mesh=mesh, in_specs=in_specs, out_specs=out_specs, check_vma=False
    )
```

profile of v0, /device:TPU:0, one launch (start us, length us, event | category | flops | bytes accessed | tf_op | source)
XLA Modules:
  0.0 970.9 jit_solution(9225734149338524849)
XLA Ops:
  9.5 5.2 all-gather.1
  15.4 4.3 all-gather.2
  19.8 4.5 all-gather.3
  24.4 12.3 %all_gather.57 = bf16[3,192,768]{2,1,0:T(8,128)(2,1)} all-gather(bf16[3,96,768]{2,1,0:T(8,128)(2,1)} %param.23), channel_id=1, replica_groups=mesh['fsdp'=2,'ctx'=4,'tp'=4] {'fsdp'}, dimensions={1}, use_global_device_ids=true | all-gather | bytes 1327104 | tf_op jit(solution)/shard_map/all_gather | solution.py:71
  36.8 4.9 all-gather.15.cloned.1.call-done
  57.8 7.2 all_gather.61
  65.0 53.9 %all-gather.17.cloned.1.call-done = bf16[4,2048,3,64]{1,3,2,0:T(8,128)(2,1)} async-done(((bf16[4,512,3,64]{1,3,2,0:T(8,128)(2,1)}), bf16[4,2048,3,64]{1,3,2,0:T(8,128)(2,1)}) %all-gather.17.cloned.1.call-update) | async-done | bytes 3145744 | tf_op jit(solution)/shard_map/all_gather | solution.py:102
  118.9 64.3 %all-gather.25.cloned.1.call-done = bf16[4,2048,1,3,64]{1,4,3,2,0:T(8,128)(2,1)} async-done(((bf16[4,512,1,3,64]{1,4,3,2,0:T(8,128)(2,1)}), bf16[4,2048,1,3,64]{1,4,3,2,0:T(8,128)(2,1)}) %all-gather.25.cloned.1.call-update) | async-done | bytes 3145744 | tf_op jit(solution)/shard_map/all_gather | solution.py:101
  184.1 96.9 %while.28 = (s32[]{:T(128)}, bf16[4,512,3,64]{1,3,2,0:T(8,128)(2,1)}, f32[4,3,512]{2,1,0:T(4,128)S(1)}, bf16[4,2048,3,64]{1,3,2,0:T(8,128)(2,1)}, s32[4,512]{1,0...) while((s32[]{:T(128)}, ...), condition=%wide.region_5.6_spmd.clone, body=%wide.region_2.5_spmd.clone.sunk | while | flops 846199808 | bytes 50493620 | solution.py:130
  185.4 8.3 fusion.154
  193.7 6.8 fusion.155
  200.5 7.0 fusion.156
  209.6 8.3 fusion.154
  217.9 6.8 fusion.155
  224.8 7.0 fusion.156
  233.8 8.3 fusion.154
  242.1 6.8 fusion.155
  249.0 7.0 fusion.156
  258.1 8.3 fusion.154
  266.4 6.8 fusion.155
  273.2 7.0 fusion.156
  288.4 4.3 all-gather.4
  292.8 4.3 all-gather.5
  297.2 4.3 all-gather.6
  301.6 4.8 all_gather.66
  306.4 64.4 %all-reduce.14.cloned.1.call-done = bf16[2048,768]{1,0:T(8,128)(2,1)} async-done(((bf16[2048,768]{1,0:T(8,128)(2,1)}), bf16[2048,768]{1,0:T(8,128)(2,1)}) %all-reduce.14.cloned.1.call-update) | async-done | bytes 3145744 | tf_op jit(solution)/shard_map/psum | solution.py:132
  377.6 6.6 fusion.112
  384.2 9.9 %fusion.105 = (bf16[768]{0:T(1024)(128)(2,1)}, bf16[2048,768]{1,0:T(8,128)(2,1)S(1)}) fusion(f32[2048,768]{1,0:T(8,128)} %fusion.112, f32[768]{0:T(1024)S(1)} %reshape.348, bf16[2048,768]{1,0:T(8,128)(2,1)} %bitcast.225, bf16[768,768]{1,0:T(8,128)(2,1)} %all-gather.21.cloned.1.call-done), kind=kOutput, calls=%fused_computation.161 | convolution fusion | flops 2450521344 | bytes 13767168 | tf_op jit(solution)/shard_map/dot_general | solution.py:26
  395.9 4.0 convolution_convert_fusion
  400.0 68.4 %all-reduce.16.cloned.1.call-done = bf16[2048,768]{1,0:T(8,128)(2,1)} async-done(((bf16[2048,768]{1,0:T(8,128)(2,1)}), bf16[2048,768]{1,0:T(8,128)(2,1)}) %all-reduce.16.cloned.1.call-update) | async-done | bytes 3145744 | tf_op jit(solution)/shard_map/psum | solution.py:173
  468.4 4.6 fusion.68
  473.1 5.9 fusion.69
  488.3 107.1 %while.29 = (s32[]{:T(128)}, bf16[4,512,3,64]{1,3,2,0:T(8,128)(2,1)}, bf16[4,2048,3,64]{1,3,2,0:T(8,128)(2,1)}, bf16[4,2048,3,64]{1,3,2,0:T(8,128)(2,1)}, bf16[4...) while((s32[]{:T(128)}, ...), condition=%wide.region_15.16_spmd.clone, body=%wide.region_13.15_spmd.clone.sunk | while | flops 2064088064 | bytes 147279216 | solution.py:210
  493.2 3.8 fusion.169
  497.0 5.8 multiply_reduce_fusion.3
  502.8 4.8 multiply_convert_fusion.5
  519.9 3.8 fusion.169
  523.7 5.8 multiply_reduce_fusion.3
  529.4 4.8 multiply_convert_fusion.5
  546.5 3.8 fusion.169
  550.3 5.8 multiply_reduce_fusion.3
  556.1 4.8 multiply_convert_fusion.5
  577.0 5.8 multiply_reduce_fusion.3
  582.8 4.8 multiply_convert_fusion.5
  596.9 8.6 convolution_convert_fusion.1
  605.8 50.2 %reduce-scatter.18.cloned.1.call-done = bf16[4,512,3,64]{1,3,2,0:T(8,128)(2,1)} async-done(((bf16[4,2048,3,64]{1,3,2,0:T(8,128)(2,1)}), bf16[4,512,3,64]{1,3,2,0:T(8,128)(2,1)}) %reduce-scatter.18.cloned.1.call-update) | async-done | bytes 786448 | tf_op jit(solution)/shard_map/reduce_scatter | solution.py:217
  658.1 60.3 %reduce-scatter.16.cloned.1.call-done = bf16[4,512,3,64]{1,3,2,0:T(8,128)(2,1)} async-done(((bf16[4,2048,3,64]{1,3,2,0:T(8,128)(2,1)}), bf16[4,512,3,64]{1,3,2,0:T(8,128)(2,1)}) %reduce-scatter.16.cloned.1.call-update) | async-done | bytes 786448 | tf_op jit(solution)/shard_map/reduce_scatter | solution.py:214
  724.1 4.0 convolution_convert_fusion.2
  728.2 4.7 fusion.97
  733.4 7.4 convolution_convert_fusion.5
  740.9 7.5 convolution_convert_fusion.6
  748.5 4.6 convolution_convert_fusion.7
  753.2 4.6 all-gather.7
  764.9 12.4 %reduce-scatter.14.cloned.1.call-done = bf16[4,128,768]{2,1,0:T(8,128)(2,1)} async-done(((bf16[4,512,768]{2,1,0:T(8,128)(2,1)}), bf16[4,128,768]{2,1,0:T(8,128)(2,1)}) %reduce-scatter.14.cloned.1.call-update) | async-done | bytes 786448 | tf_op jit(solution)/shard_map/reduce_scatter | solution.py:148
  780.0 10.0 %reduce-scatter.28.cloned.1.call-done = bf16[64,3]{1,0:T(8,128)(2,1)} async-done(((bf16[128,3]{1,0:T(8,128)(2,1)}), bf16[64,3]{1,0:T(8,128)(2,1)}) %reduce-scatter.28.cloned.1.call-update) | async-done | bytes 400
  790.8 22.6 %all-reduce.18.cloned.1.call-done = bf16[2048,768]{1,0:T(8,128)(2,1)} async-done(((bf16[2048,768]{1,0:T(8,128)(2,1)}), bf16[2048,768]{1,0:T(8,128)(2,1)}) %all-reduce.18.cloned.1.call-update) | async-done | bytes 3145744 | tf_op jit(solution)/shard_map/psum | solution.py:235
  816.7 12.9 %reduce-scatter.26.cloned.1.call-done = bf16[384,768]{1,0:T(8,128)(2,1)} async-done(((bf16[768,768]{1,0:T(8,128)(2,1)}), bf16[384,768]{1,0:T(8,128)(2,1)}) %reduce-scatter.26.cloned.1.call-update) | async-done | bytes 589840 | tf_op jit(solution)/shard_map/reduce_scatter | solution.py:304
  829.6 24.5 %reduce-scatter.24.cloned.1.call-done = bf16[384,768]{1,0:T(8,128)(2,1)} async-done(((bf16[768,768]{1,0:T(8,128)(2,1)}), bf16[384,768]{1,0:T(8,128)(2,1)}) %reduce-scatter.24.cloned.1.call-update) | async-done | bytes 589840 | tf_op jit(solution)/shard_map/reduce_scatter | solution.py:298
  854.0 21.5 %reduce-scatter.20.cloned.1.call-done = bf16[3,96,768]{2,1,0:T(8,128)(2,1)} async-done(((bf16[3,192,768]{2,1,0:T(8,128)(2,1)}), bf16[3,96,768]{2,1,0:T(8,128)(2,1)}) %reduce-scatter.20.cloned.1.call-update) | async-done | bytes 442384 | tf_op jit(solution)/shard_map/reduce_scatter | solution.py:280
  875.5 5.1 fusion.70
  880.7 5.8 fusion.110
  886.5 6.9 all-reduce.8
  893.9 13.1 %all-reduce.6 = (bf16[384]{0:T(512)(128)(2,1)S(1)}, bf16[384]{0:T(512)(128)(2,1)S(1)}, bf16[3,64]{1,0:T(4,128)(2,1)S(1)}, bf16[384]{0:T(512)(128)(2,1)S(1)}, bf1...) all-reduce(bf16[384]{0:T(512)(128)(2,1)S(1)} %dynamic-slice.1, ...), channel_id=1, replica_groups=mesh['fsdp'=2,'ctx'=4,'tp'=4] {'ctx'}, use_global_device_ids=true, to_apply=%region_22.23 | all-reduce | flops 2880 | bytes 11520 | tf_op jit(solution)/shard_map/psum | solution.py:260
  913.7 41.7 %all-reduce.20.cloned.1.call-done = (bf16[3,96,768]{2,1,0:T(8,128)(2,1)}, bf16[96,768]{1,0:T(8,128)(2,1)}, bf16[384,768]{1,0:T(8,128)(2,1)}, bf16[384,768]{1,0:T(8,128)(2,1)}) async-done(((bf16[3,96,768]{2,1,0:T(8,128)(2,1)}, bf16[96,768]{1,0:T(8,128)(2,1)}, bf16[384,768]{1,0:T(8,128)(2,1)}, bf16[384,768]{1,0:T(8,128)(2,1)}), (bf16[3,96,768]{2,1,0:T(8,128)(2,1)}, bf16[96,768]{1,0:T(8,128)(2,1)}, ...) | async-done | bytes 1769488 | tf_op jit(solution)/shard_map/psum | solution.py:262
  (334 shorter events, 143.8 us)
Async XLA Ops:
  8.0 33.7 %all-gather.15.cloned.1.call-start = ((), (), s32[]{:S(2)}) async-start(), calls=%async_computation.9 | async-start | bytes 3932160 | tf_op jit(solution)/shard_map/all_gather | solution.py:50
  8.7 110.1 %all-gather.17.cloned.1.call-start = ((), (), s32[]{:S(2)}) async-start(), calls=%async_computation.10 | async-start | bytes 3932160 | tf_op jit(solution)/shard_map/all_gather | solution.py:102
  14.7 34.9 %copy-start.27 = (f32[768]{0:T(1024)}, f32[768]{0:T(1024)S(1)}, u32[]{:S(2)}) copy-start(f32[768]{0:T(1024)S(1)} %reshape.364) | copy-start | bytes 9220
  41.7 6.7 copy-start.2
  41.7 8.0 copy-start.24
  49.7 5.6 copy-start.16
  51.7 13.2 %copy-start.26 = (s32[4,2048]{1,0:T(4,128)S(1)}, s32[4,2048]{1,0:T(4,128)}, u32[]{:S(2)}) copy-start(s32[4,2048]{1,0:T(4,128)} %param.20) | copy-start | bytes 98308
  55.2 128.0 %all-gather.25.cloned.1.call-start = ((), (), s32[]{:S(2)}) async-start(), calls=%async_computation.20 | async-start | bytes 3932160 | tf_op jit(solution)/shard_map/all_gather | solution.py:101
  57.7 313.0 %all-reduce.14.cloned.1.call-start = ((), (), s32[]{:S(2)}) async-start(), calls=%async_computation.11 | async-start | bytes 6291456 | tf_op jit(solution)/shard_map/psum | solution.py:132
  193.7 6.8 copy-start.20
  217.9 6.8 copy-start.20
  242.1 6.8 copy-start.20
  266.4 6.8 copy-start.20
  283.9 4.5 copy-start.37
  283.9 8.9 copy-start.38
  283.9 13.3 %copy-start.39 = (bf16[384]{0:T(512)(128)(2,1)S(1)}, bf16[384]{0:T(512)(128)(2,1)}, u32[]{:S(2)}) copy-start(bf16[384]{0:T(512)(128)(2,1)} %param.28) | copy-start | bytes 2308
  283.9 17.7 %copy-start.36 = (bf16[3,128]{1,0:T(4,128)(2,1)S(1)}, bf16[3,128]{1,0:T(4,128)(2,1)}, u32[]{:S(2)}) copy-start(bf16[3,128]{1,0:T(4,128)(2,1)} %param.30) | copy-start | bytes 2308
  286.6 90.9 %all-gather.19.cloned.1.call-start = ((), (), s32[]{:S(2)}) async-start(), calls=%async_computation.12 | async-start | bytes 1769472 | tf_op jit(solution)/shard_map/all_gather | solution.py:77
  287.2 97.0 %all-gather.21.cloned.1.call-start = ((), (), s32[]{:S(2)}) async-start(), calls=%async_computation.13 | async-start | bytes 1769472 | tf_op jit(solution)/shard_map/all_gather | solution.py:79
  287.8 96.4 %all-gather.23.cloned.1.call-start = ((), (), s32[]{:S(2)}) async-start(), calls=%async_computation.15 | async-start | bytes 3932160 | tf_op jit(solution)/shard_map/all_gather | solution.py:51
  288.4 180.0 %all-reduce.16.cloned.1.call-start = ((), (), s32[]{:S(2)}) async-start(), calls=%async_computation.16 | async-start | bytes 6291456 | tf_op jit(solution)/shard_map/psum | solution.py:173
  306.4 77.8 %copy-start.33 = (f32[768]{0:T(1024)}, f32[768]{0:T(1024)S(1)}, u32[]{:S(2)}) copy-start(f32[768]{0:T(1024)S(1)} %reshape.348) | copy-start | bytes 9220
  377.5 6.7 copy-start.22
  384.2 11.7 %copy-start.42 = (bf16[768,768]{1,0:T(8,128)(2,1)S(1)}, bf16[768,768]{1,0:T(8,128)(2,1)}, u32[]{:S(2)}) copy-start(bf16[768,768]{1,0:T(8,128)(2,1)} %all-gather.19.cloned.1.call-done) | copy-start | bytes 3538948
  399.9 256.1 %reduce-scatter.18.cloned.1.call-start = ((), (), s32[]{:S(2)}) async-start(), calls=%async_computation.18 | async-start | bytes 3932160 | tf_op jit(solution)/shard_map/reduce_scatter | solution.py:217
  468.4 4.7 copy-start.5
  468.4 10.7 %slice-start = ((s8[6291456]{0:T(1024)(128)(4,1)}), s8[4194304]{0:T(1024)(128)(4,1)S(1)}, s32[]{:S(2)}) async-start(s8[6291456]{0:T(1024)(128)(4,1)} %bitcast.222), calls=%async_computation.28 | async-start | bytes 8388608
  473.0 6.0 copy-start.7
  473.0 6.0 slice-start.1
  488.4 4.7 copy-start.13
  502.8 4.8 copy-start.10
  507.6 7.5 copy-start.14
  515.1 4.7 copy-start.13
  529.4 4.8 copy-start.10
  534.3 7.5 copy-start.14
  541.8 4.7 copy-start.13
  556.1 4.8 copy-start.10
  561.0 7.5 copy-start.14
  568.5 4.7 copy-start.13
  582.8 4.8 copy-start.10
  587.6 7.5 copy-start.14
  595.4 123.0 %reduce-scatter.16.cloned.1.call-start = ((), (), s32[]{:S(2)}) async-start(), calls=%async_computation.17 | async-start | bytes 3932160 | tf_op jit(solution)/shard_map/reduce_scatter | solution.py:214
  596.0 165.6 %reduce-scatter.30.cloned.1.call-start = ((), (), s32[]{:S(2)}) async-start(), calls=%async_computation.26 | async-start | bytes 98304
  596.9 8.7 copy-start.12
  596.9 180.4 %reduce-scatter.14.cloned.1.call-start = ((), (), s32[]{:S(2)}) async-start(), calls=%async_computation.14 | async-start | bytes 3932160 | tf_op jit(solution)/shard_map/reduce_scatter | solution.py:148
  605.5 184.5 %reduce-scatter.28.cloned.1.call-start = ((), (), s32[]{:S(2)}) async-start(), calls=%async_computation.25 | async-start | bytes 49152
  718.4 5.6 copy-start.25
  722.7 90.6 %all-reduce.18.cloned.1.call-start = ((), (), s32[]{:S(2)}) async-start(), calls=%async_computation.19 | async-start | bytes 6291456 | tf_op jit(solution)/shard_map/psum | solution.py:235
  728.1 5.2 copy-start.8
  728.2 88.5 %reduce-scatter.22.cloned.1.call-start = ((), (), s32[]{:S(2)}) async-start(), calls=%async_computation.22 | async-start | bytes 442368 | tf_op jit(solution)/shard_map/reduce_scatter | solution.py:286
  732.9 96.6 %reduce-scatter.26.cloned.1.call-start = ((), (), s32[]{:S(2)}) async-start(), calls=%async_computation.24 | async-start | bytes 1769472 | tf_op jit(solution)/shard_map/reduce_scatter | solution.py:304
  740.8 7.6 copy-start.17
  740.8 113.2 %reduce-scatter.24.cloned.1.call-start = ((), (), s32[]{:S(2)}) async-start(), calls=%async_computation.23 | async-start | bytes 1769472 | tf_op jit(solution)/shard_map/reduce_scatter | solution.py:298
  748.4 127.1 %reduce-scatter.20.cloned.1.call-start = ((), (), s32[]{:S(2)}) async-start(), calls=%async_computation.21 | async-start | bytes 1327104 | tf_op jit(solution)/shard_map/reduce_scatter | solution.py:280
  748.5 4.7 copy-start.40
  748.5 9.4 copy-start.43
  748.5 10.7 %copy-start.29 = (f32[1,4,4,128]{3,2,1,0:T(4,128)S(1)}, f32[1,4,4,128]{3,2,1,0:T(4,128)}, u32[]{:S(2)}) copy-start(f32[1,4,4,128]{3,2,1,0:T(4,128)} %get-tuple-element.309) | copy-start | bytes 24580
  748.5 10.7 %copy-start.30 = (f32[1,4,4,128]{3,2,1,0:T(4,128)S(1)}, f32[1,4,4,128]{3,2,1,0:T(4,128)}, u32[]{:S(2)}) copy-start(f32[1,4,4,128]{3,2,1,0:T(4,128)} %get-tuple-element.307) | copy-start | bytes 24580
  753.1 60.2 %copy-start.3 = (bf16[4,512,768]{2,1,0:T(8,128)(2,1)S(1)}, bf16[4,512,768]{2,1,0:T(8,128)(2,1)}, u32[]{:S(2)}) copy-start(bf16[4,512,768]{2,1,0:T(8,128)(2,1)} %all-gather.15.cloned.1.call-done) | copy-start | bytes 9437188
  753.1 60.2 %copy-start.28 = (f32[768]{0:T(1024)S(1)}, f32[768]{0:T(1024)}, u32[]{:S(2)}) copy-start(f32[768]{0:T(1024)} %copy-done.27) | copy-start | bytes 9220
  753.1 202.2 %all-reduce.20.cloned.1.call-start = ((), (), s32[]{:S(2)}) async-start(), calls=%async_computation.27 | async-start | bytes 3538944 | tf_op jit(solution)/shard_map/psum | solution.py:262
  875.5 5.2 copy-start.6
  880.7 5.8 copy-start.31
  880.7 5.8 copy-start.32
  (29 other events, 62.7 us)
Sparse Core Ops, SparseCore 0:
  10.4 31.2 all-gather.14
  55.4 63.4 all-gather.16
  121.0 62.1 all-gather.24
  286.7 83.9 all-reduce.13
  595.5 60.3 reduce-scatter.17
  658.1 60.2 reduce-scatter.15
  721.2 9.8 reduce-scatter.29
  733.7 43.5 reduce-scatter.13
  780.1 9.8 reduce-scatter.27
  792.7 12.1 reduce-scatter.21
  807.8 21.7 reduce-scatter.25
  832.2 21.7 reduce-scatter.23
  857.0 18.4 reduce-scatter.19
  878.2 77.1 all-reduce.19
Sparse Core Ops, SparseCore 1:
  288.6 21.3 all-gather.18
  311.4 22.6 all-gather.20
  335.5 35.8 all-gather.22
  400.0 68.3 all-reduce.15
  728.2 85.0 all-reduce.17
where the time goes:
time: 977 us; the launch traced here: 971 us
  waiting for transfers between devices  515 us (53%)
  matrix products  199 us (20%)
  other arithmetic  123 us (13%)
  blocking collectives  75.9 us (8%)
  local copies, waits for them, and re-layouts  38.5 us (4%)
  between operations  17.2 us (2%)
    psum x1, waiting for transfers between devices, on_device(): lax.psum(contract_cols(grad_pre, up_back).astype(jnp.bfloat16), 'tp')  68.4 us
    psum x1, waiting for transfers between devices, on_device(): lax.psum(jnp.dot(merged, out_mat, preferred_element_type=jnp.float32).ast...  64.4 us
    all_gather x1, waiting for transfers between devices, on_device(): lax.all_gather(keys_local, 'ctx', axis=1, tiled=True)  64.3 us
    reduce_scatter x1, waiting for transfers between devices, on_device(): lax.psum_scatter(grad_keys_all.astype(jnp.bfloat16), 'ctx', scatter_dimen...  60.3 us
    all_gather x1, waiting for transfers between devices, on_device(): lax.all_gather(values_local, 'ctx', axis=1, tiled=True)  53.9 us
    reduce_scatter x1, waiting for transfers between devices, on_device(): lax.psum_scatter(grad_values_all.astype(jnp.bfloat16), 'ctx', scatter_dim...  50.2 us
    psum x1, waiting for transfers between devices, on_device(): lax.psum(grad_qkv.astype(jnp.bfloat16), 'ctx').astype(jnp.float32)  41.7 us
    dot_general x4, matrix products, attend(): jnp.einsum('chd,khd->hck', query_blk, key_blk, preferred_element_type=jnp...  33.2 us
  transfers between devices with their start and end apart: 19, of which 14 were waited for; matrix products, arithmetic and copies ran while one was open for 9% of the time, Pallas kernels for 0%

commit v1 on v0

v1 whole, which is shorter than its diff:
```python
import functools

import jax
import jax.numpy as jnp
from jax import lax
from jax.experimental import pallas as pl
from jax.experimental.pallas import tpu as pltpu
from jax.sharding import PartitionSpec as P

EPS = 1e-05
NEG = -1e30
BF = jnp.bfloat16
F32 = jnp.float32
LANES = 128
HEAD_PAD = 256
BQ = 256
BK = 256
VMEM_BYTES = 48 * 1024 * 1024


def dot_nn(left, right):
    return lax.dot_general(left, right, (((1,), (0,)), ((), ())), preferred_element_type=F32)


def dot_nt(left, right):
    return lax.dot_general(left, right, (((1,), (1,)), ((), ())), preferred_element_type=F32)


def dot_tn(left, right):
    return lax.dot_general(left, right, (((0,), (0,)), ((), ())), preferred_element_type=F32)


def swap(value, axis, bit):
    size = lax.axis_size(axis)
    return lax.ppermute(value, axis, [(i, i ^ bit) for i in range(size)])


def tree_sum(items):
    items = [item.astype(F32) for item in items]
    while len(items) > 1:
        items = [items[i] + items[i + 1] for i in range(0, len(items), 2)]
    return items[0]


def butterfly(value, axis):
    size = lax.axis_size(axis)
    if size & (size - 1):
        return lax.psum(value, axis)
    return tree_sum([value] + [swap(value, axis, bit) for bit in range(1, size)])


def gather_fsdp(value):
    if lax.axis_size("fsdp") != 2:
        return lax.all_gather(value, "fsdp", axis=0, tiled=False)
    other = swap(value, "fsdp", 1)
    first = lax.axis_index("fsdp") == 0
    return jnp.stack([jnp.where(first, value, other), jnp.where(first, other, value)])


def scatter_fsdp(value):
    if lax.axis_size("fsdp") != 2:
        return lax.psum_scatter(value, "fsdp", scatter_dimension=0, tiled=False)
    rank = lax.axis_index("fsdp")
    mine = lax.dynamic_index_in_dim(value, rank, 0, keepdims=False)
    theirs = lax.dynamic_index_in_dim(value, 1 - rank, 0, keepdims=False)
    return (mine.astype(F32) + swap(theirs, "fsdp", 1).astype(F32)).astype(value.dtype)


def sum_ctx(value):
    size = lax.axis_size("ctx")
    rows = value.shape[0]
    if size != 4 or rows % (8 * size):
        return lax.psum(value, "ctx").astype(F32)
    rank = lax.axis_index("ctx")
    parts = value.reshape((size, rows // size) + value.shape[1:])

    def part(index):
        return lax.dynamic_index_in_dim(parts, index, 0, keepdims=False)

    got = [part(rank)] + [
        lax.ppermute(part(rank ^ s), "ctx", [(i, i ^ s) for i in range(size)])
        for s in range(1, size)
    ]
    mine = tree_sum(got).astype(value.dtype)
    slots = jnp.stack([mine] + [swap(mine, "ctx", s) for s in range(1, size)])
    out = [lax.dynamic_index_in_dim(slots, rank ^ i, 0, keepdims=False) for i in range(size)]
    return jnp.concatenate(out, axis=0).astype(F32)


def gather_tp(value):
    far = swap(value, "tp", 2)
    return [value, swap(value, "tp", 1), far, swap(far, "tp", 1)]


def scatter_tp(slots):
    near = [slots[0].astype(F32) + swap(slots[1], "tp", 1).astype(F32)]
    far = slots[2].astype(F32) + swap(slots[3], "tp", 1).astype(F32)
    return near[0] + swap(far.astype(BF), "tp", 2).astype(F32)


def seq_steps(seqs):
    size = lax.axis_size("ctx")
    groups = size // seqs
    return [
        [(src, ((src % seqs + step) % seqs) * groups + src // seqs) for src in range(size)]
        for step in range(seqs)
    ]


def send(value, pairs):
    if all(src == dst for src, dst in pairs):
        return value
    return lax.ppermute(value, "ctx", pairs)


def to_sequence(value):
    seqs = value.shape[0]
    base = lax.axis_index("ctx") % seqs
    return [
        send(lax.dynamic_index_in_dim(value, (base + step) % seqs, 0, keepdims=False), pairs)
        for step, pairs in enumerate(seq_steps(seqs))
    ]


def from_sequence(blocks):
    seqs = len(blocks)
    base = lax.axis_index("ctx") % seqs
    got = [
        send(block, [(dst, src) for src, dst in pairs])
        for block, pairs in zip(blocks, seq_steps(seqs))
    ]
    twice = jnp.stack(got + got)
    return lax.dynamic_slice_in_dim(twice, (seqs - base) % seqs, seqs, 0)


def lane_is_low(rows):
    return lax.broadcasted_iota(jnp.int32, (rows, LANES), 1) < LANES // 2


def pieces(dims):
    ranks, steps = dims
    return [(j * ranks + rank, j, rank) for j in range(steps) for rank in range(ranks)]


def allowed_block(seg_row, seg_col, q_axis, q_start, k_start, shape):
    q_at = q_start + lax.broadcasted_iota(jnp.int32, shape, q_axis)
    k_at = k_start + lax.broadcasted_iota(jnp.int32, shape, 1 - q_axis)
    return (seg_row == seg_col) & (k_at <= q_at)


def attend_kernel(where_ref, low_ref, full_ref, seg_q_ref, seg_k_ref, q_ref, kv_ref, o_ref, lse_ref, qs, ks, vs):
    ranks, steps, sub, _ = q_ref.shape
    parts = kv_ref.shape[0]
    tp_rank, seq_rank, part = where_ref[0], where_ref[1], where_ref[2]
    q_len = ranks * steps * sub
    scale = 64 ** (-0.5)
    low = lane_is_low(sub)
    for block, j, rank in pieces((ranks, steps)):
        slot, step = tp_rank ^ rank, lax.rem(seq_rank - j + steps, steps)
        rows = slice(block * sub, (block + 1) * sub)
        tile = q_ref[slot, step]
        tile = (tile.astype(F32) * scale).astype(BF)
        head_pair = tile[:, :LANES]
        zero = jnp.zeros_like(head_pair)
        qs[rows, 0:128] = jnp.where(low, head_pair, zero)
        qs[rows, 128:256] = jnp.where(low, zero, head_pair)
        qs[rows, 256:384] = tile[:, LANES:]
        for p in range(parts):
            at = slice(p * q_len + block * sub, p * q_len + (block + 1) * sub)
            ks[at, :] = kv_ref[p, slot, step, :, :HEAD_PAD]
            vs[at, :] = kv_ref[p, slot, step, :, HEAD_PAD:]

    def q_block(i, _):
        q_row = pl.multiple_of(i * BQ, BQ)
        q_first = part * q_len + q_row
        seg_q = seg_q_ref[pl.ds(q_row, BQ), :]

        def step(masked, kk, carry):
            k_row = pl.multiple_of(kk * BK, BK)
            keys = ks[pl.ds(k_row, BK), :]
            vals = vs[pl.ds(k_row, BK), :]
            if masked:
                ok = allowed_block(seg_q, seg_k_ref[:, pl.ds(k_row, BK)], 0, q_first, k_row, (BQ, BK))
            out = []
            for h in range(3):
                top, total, acc = carry[h]
                lanes = slice((h // 2) * LANES, (h // 2 + 1) * LANES)
                scores = dot_nt(qs[pl.ds(q_row, BQ), h * LANES : (h + 1) * LANES], keys[:, lanes])
                if masked:
                    scores = jnp.where(ok, scores, NEG)
                new_top = jnp.maximum(top, jnp.max(scores, axis=1, keepdims=True))
                probs = jnp.exp(scores - new_top)
                shrink = jnp.exp(top - new_top)
                total = total * shrink + jnp.sum(probs, axis=1, keepdims=True)
                acc = acc * shrink + dot_nn(probs.astype(BF), vals[:, lanes])
                out.append((new_top, total, acc))
            return tuple(out)

        start = tuple(
            (jnp.full((BQ, 1), NEG, F32), jnp.zeros((BQ, 1), F32), jnp.zeros((BQ, LANES), F32))
            for _ in range(3)
        )
        first, full = low_ref[i], full_ref[i]
        last = q_first // BK
        carry = lax.fori_loop(first, full, functools.partial(step, True), start)
        carry = lax.fori_loop(full, last, functools.partial(step, False), carry)
        carry = lax.fori_loop(last, last + BQ // BK, functools.partial(step, True), carry)
        heads = [acc / total for _, total, acc in carry]
        pair = jnp.where(lane_is_low(BQ), heads[0], heads[1]).astype(BF)
        third = heads[2].astype(BF)
        for n in range(BQ // sub):
            block = i * (BQ // sub) + n
            j, rank = block // ranks, lax.rem(block, ranks)
            slot, at = tp_rank ^ rank, lax.rem(seq_rank - j + steps, steps)
            o_ref[slot, at, :, 0:128] = pair[n * sub : (n + 1) * sub]
            o_ref[slot, at, :, 128:256] = third[n * sub : (n + 1) * sub]
        for h in range(3):
            top, total, _ = carry[h]
            column = jnp.broadcast_to(top + jnp.log(total), (BQ, LANES))
            lse_ref[h : h + 1, pl.ds(q_row, BQ)] = column.T[0:1]
        return 0

    lax.fori_loop(0, q_len // BQ, q_block, 0)


def attend_back_kernel(
    where_ref, full_ref, high_ref, seg_q_ref, seg_k_ref, q_ref, kv_ref, o_ref, do_ref, lse_ref, dq_ref, dkv_ref, qs, ks, vs, dos, dqs, delta
):
    ranks, steps, sub, _ = q_ref.shape
    parts = kv_ref.shape[0]
    tp_rank, seq_rank, part = where_ref[0], where_ref[1], where_ref[2]
    q_len = ranks * steps * sub
    scale = 64 ** (-0.5)
    low = lane_is_low(sub)

    def place(rank, j):
        return tp_rank ^ rank, lax.rem(seq_rank - j + steps, steps)

    for block, j, rank in pieces((ranks, steps)):
        slot, step = place(rank, j)
        rows = slice(block * sub, (block + 1) * sub)
        tile = (q_ref[slot, step].astype(F32) * scale).astype(BF)
        grad = do_ref[slot, step]
        for source, target in ((tile, qs), (grad, dos)):
            head_pair = source[:, :LANES]
            zero = jnp.zeros_like(head_pair)
            target[rows, 0:128] = jnp.where(low, head_pair, zero)
            target[rows, 128:256] = jnp.where(low, zero, head_pair)
            target[rows, 256:384] = source[:, LANES:]
        product = grad.astype(F32) * o_ref[slot, step].astype(F32)
        pair = product[:, :LANES].T
        third = product[:, LANES:].T
        delta[0:1, rows] = jnp.sum(pair[:64], axis=0, keepdims=True)
        delta[1:2, rows] = jnp.sum(pair[64:], axis=0, keepdims=True)
        delta[2:3, rows] = jnp.sum(third[:64], axis=0, keepdims=True)
        for p in range(parts):
            at = slice(p * q_len + block * sub, p * q_len + (block + 1) * sub)
            ks[at, :] = kv_ref[p, slot, step, :, :HEAD_PAD]
            vs[at, :] = kv_ref[p, slot, step, :, HEAD_PAD:]
    dqs[...] = jnp.zeros_like(dqs)
    q_count = q_len // BQ
    low_q = lane_is_low(BQ)

    def k_block(kk, _):
        k_row = pl.multiple_of(kk * BK, BK)
        keys = ks[pl.ds(k_row, BK), :]
        vals = vs[pl.ds(k_row, BK), :]
        seg_k = seg_k_ref[pl.ds(k_row, BK), :]

        def step(masked, i, carry):
            q_row = pl.multiple_of(i * BQ, BQ)
            at = pl.ds(q_row, BQ)
            if masked:
                ok = allowed_block(
                    seg_q_ref[:, at], seg_k, 1, part * q_len + q_row, k_row, (BK, BQ)
                )
            dk, dv = list(carry[0]), list(carry[1])
            dq = []
            for h in range(3):
                t = h // 2
                lanes = slice(t * LANES, (t + 1) * LANES)
                mine = slice(h * LANES, (h + 1) * LANES)
                q_head, do_head = qs[at, mine], dos[at, mine]
                scores = dot_nt(keys[:, lanes], q_head)
                probs = jnp.exp(scores - lse_ref[h : h + 1, at])
                if masked:
                    probs = jnp.where(ok, probs, 0.0)
                grad_probs = dot_nt(vals[:, lanes], do_head)
                grad_scores = (probs * (grad_probs - delta[h : h + 1, at])).astype(BF)
                dv[t] = dv[t] + dot_nn(probs.astype(BF), do_head)
                dk[t] = dk[t] + dot_nn(grad_scores, q_head)
                dq.append(dot_tn(grad_scores, keys[:, lanes]))
            dqs[at, 0:128] += jnp.where(low_q, dq[0], dq[1])
            dqs[at, 128:256] += dq[2]
            return tuple(dk), tuple(dv)

        zero = jnp.zeros((BK, LANES), F32)
        carry = ((zero, zero), (zero, zero))
        first = jnp.maximum(kk * BK // BQ - part * q_count, 0)
        diagonal = jnp.where(kk * BK >= part * q_len, first + 1, first)
        diagonal = jnp.where(kk * BK >= (part + 1) * q_len, first, diagonal)
        first = jnp.minimum(first, q_count)
        diagonal = jnp.minimum(diagonal, q_count)
        full = jnp.maximum(full_ref[kk], diagonal)
        high = jnp.maximum(high_ref[kk], full)
        carry = lax.fori_loop(first, diagonal, functools.partial(step, True), carry)
        carry = lax.fori_loop(diagonal, full, functools.partial(step, False), carry)
        carry = lax.fori_loop(full, high, functools.partial(step, True), carry)
        dk, dv = carry
        p = kk // (q_len // BK)
        for n in range(BK // sub):
            block = lax.rem(kk, q_len // BK) * (BK // sub) + n
            slot, step_at = place(lax.rem(block, ranks), block // ranks)
            rows = slice(n * sub, (n + 1) * sub)
            for t in range(2):
                dkv_ref[p, slot, step_at, :, t * 128 : (t + 1) * 128] = dk[t][rows].astype(BF)
                dkv_ref[p, slot, step_at, :, 256 + t * 128 : 256 + (t + 1) * 128] = dv[t][rows].astype(BF)
        return 0

    lax.fori_loop(0, parts * q_len // BK, k_block, 0)
    for block, j, rank in pieces((ranks, steps)):
        slot, step = place(rank, j)
        dq_ref[slot, step] = (dqs[block * sub : (block + 1) * sub, :] * scale).astype(BF)


SMEM = pl.BlockSpec(memory_space=pltpu.SMEM)
VMEM = pl.BlockSpec(memory_space=pltpu.VMEM)
PARAMS = pltpu.CompilerParams(vmem_limit_bytes=VMEM_BYTES)


def attend(where, seg_q, seg_k, queries, keyvals):
    ranks, steps, sub, _ = queries.shape
    q_len, k_len = ranks * steps * sub, keyvals.shape[0] * ranks * steps * sub
    q_first, q_last = seg_q[::BQ], seg_q[BQ - 1 :: BQ]
    k_first, k_last = seg_k[::BK], seg_k[BK - 1 :: BK]
    k_index = jnp.arange(k_len // BK)
    bound = where[2] * (q_len // BK) + jnp.arange(q_len // BQ) * (BQ // BK)
    before = k_index[None, :] < bound[:, None]
    first = jnp.sum(before & (k_last[None, :] < q_first[:, None]), axis=1).astype(jnp.int32)
    full = jnp.sum(before & (k_first[None, :] != q_last[:, None]), axis=1).astype(jnp.int32)
    return pl.pallas_call(
        attend_kernel,
        out_shape=(
            jax.ShapeDtypeStruct((ranks, steps, sub, HEAD_PAD), BF),
            jax.ShapeDtypeStruct((8, q_len), F32),
        ),
        in_specs=[SMEM, SMEM, SMEM, VMEM, VMEM, VMEM, VMEM],
        out_specs=(VMEM, VMEM),
        scratch_shapes=[
            pltpu.VMEM((q_len, 3 * LANES), BF),
            pltpu.VMEM((k_len, HEAD_PAD), BF),
            pltpu.VMEM((k_len, HEAD_PAD), BF),
        ],
        compiler_params=PARAMS,
        cost_estimate=pl.CostEstimate(
            flops=6 * q_len * k_len * 256, bytes_accessed=8 * q_len * 1024, transcendentals=3 * q_len * k_len // 2
        ),
        name="attend",
    )(where, first, jnp.maximum(full, first), seg_q[:, None], seg_k[None, :], queries, keyvals)


def attend_back(where, seg_q, seg_k, queries, keyvals, attended, grad, lse):
    ranks, steps, sub, _ = queries.shape
    q_len, k_len = ranks * steps * sub, keyvals.shape[0] * ranks * steps * sub
    q_first, q_last = seg_q[::BQ], seg_q[BQ - 1 :: BQ]
    k_first, k_last = seg_k[::BK], seg_k[BK - 1 :: BK]
    full = jnp.sum(q_last[None, :] <= k_first[:, None], axis=1).astype(jnp.int32)
    high = jnp.sum(q_first[None, :] <= k_last[:, None], axis=1).astype(jnp.int32)
    return pl.pallas_call(
        attend_back_kernel,
        out_shape=(
            jax.ShapeDtypeStruct(queries.shape, BF),
            jax.ShapeDtypeStruct(keyvals.shape, BF),
        ),
        in_specs=[SMEM, SMEM, SMEM] + [VMEM] * 7,
        out_specs=(VMEM, VMEM),
        scratch_shapes=[
            pltpu.VMEM((q_len, 3 * LANES), BF),
            pltpu.VMEM((k_len, HEAD_PAD), BF),
            pltpu.VMEM((k_len, HEAD_PAD), BF),
            pltpu.VMEM((q_len, 3 * LANES), BF),
            pltpu.VMEM((q_len, HEAD_PAD), F32),
            pltpu.VMEM((8, q_len), F32),
        ],
        compiler_params=PARAMS,
        cost_estimate=pl.CostEstimate(
            flops=15 * q_len * k_len * 256, bytes_accessed=16 * q_len * 1024, transcendentals=3 * q_len * k_len // 2
        ),
        name="attend_back",
    )(where, full, high, seg_q[None, :], seg_k[:, None], queries, keyvals, attended, grad, lse)


def norm_parts(values):
    center = values - jnp.mean(values, axis=-1, keepdims=True)
    rstd = lax.rsqrt(jnp.mean(center * center, axis=-1, keepdims=True) + EPS)
    return center * rstd, rstd


def norm_back(xhat, rstd, gain, grad):
    gg = grad * gain
    inner = gg - jnp.mean(gg, axis=-1, keepdims=True)
    return rstd * (inner - xhat * jnp.mean(gg * xhat, axis=-1, keepdims=True))


def gelu_tanh(inputs):
    return jax.nn.gelu(inputs, approximate=True)


def on_device(
    block_in, segments, ln1_gain, ln1_shift, w_qkv, b_qv, w_out, b_out, ln2_gain, ln2_shift, w_up, b_up, w_down, b_down, cotangent
):
    seqs, sub, width = block_in.shape
    ranks = lax.axis_size("tp")
    ctx_size = lax.axis_size("ctx")
    parts = ctx_size // seqs
    tp_rank, ctx_rank = lax.axis_index("tp"), lax.axis_index("ctx")
    heads = b_qv.shape[0]
    head_width = heads * 64
    own = seqs * sub
    tokens = ranks * own

    x_own = jnp.concatenate(to_sequence(block_in), axis=0)

    small = [ln1_gain, ln1_shift, b_out, ln2_gain, ln2_shift, b_down]
    flat = jnp.concatenate([*small, b_qv.reshape(-1), b_up.reshape(-1)])
    packed = gather_fsdp(flat)
    shard = ln1_gain.shape[0]
    gain_one, shift_one, out_bias, gain_two, shift_two, down_bias = (
        packed[:, n * shard : (n + 1) * shard].reshape(-1).astype(F32) for n in range(6)
    )
    rest = packed[:, 6 * shard :]
    qv_bias = rest[:, : b_qv.size].reshape((-1,) + b_qv.shape).transpose(1, 0, 2).reshape(heads, -1)
    up_bias = rest[:, b_qv.size :].reshape((-1,) + b_up.shape).transpose(1, 0, 2).reshape(-1)

    qkv_mat = gather_fsdp(w_qkv).transpose(1, 0, 2, 3).reshape(3, head_width, width)
    qkv_pad = jnp.pad(qkv_mat, ((0, 0), (0, HEAD_PAD - head_width), (0, 0)))
    q_mat, kv_mat = qkv_pad[0], qkv_pad[1:].reshape(2 * HEAD_PAD, width)
    bias_float = qv_bias.astype(F32)

    def pad_bias(bias):
        return jnp.pad(bias.reshape(-1), (0, HEAD_PAD - head_width))

    q_bias = pad_bias(bias_float[:, :64])
    kv_bias = jnp.concatenate([jnp.zeros((HEAD_PAD,), F32), pad_bias(bias_float[:, 64:])])

    x_float = x_own.astype(F32)
    xhat_one, rstd_one = norm_parts(x_float)
    normed_own = (xhat_one * gain_one + shift_one).astype(BF)
    normed_one = jnp.concatenate(gather_tp(normed_own), axis=0)

    queries = (dot_nt(normed_one, q_mat) + q_bias).astype(BF).reshape(ranks, seqs, sub, HEAD_PAD)
    keyvals = (dot_nt(normed_one, kv_mat) + kv_bias).astype(BF)
    keyvals = keyvals.reshape(1, ranks, seqs, sub, 2 * HEAD_PAD)
    groups = [[g * parts + p for p in range(parts)] for g in range(ctx_size // parts)]
    if parts > 1:
        keyvals = lax.all_gather(keyvals, "ctx", axis=0, tiled=True, axis_index_groups=groups)
    seq_rank, part = ctx_rank // parts, ctx_rank % parts
    where = jnp.stack([tp_rank, seq_rank, part]).astype(jnp.int32)
    seg_k = lax.dynamic_index_in_dim(segments, seq_rank, 0, keepdims=False)
    seg_q = lax.dynamic_slice_in_dim(seg_k, part * tokens, tokens, 0)
    attended, lse = attend(where, seg_q, seg_k, queries, keyvals)

    out_mats = gather_tp(gather_fsdp(w_out).reshape(head_width, width))
    up_mats = gather_tp(gather_fsdp(w_up).reshape(width, -1))
    down_far = gather_fsdp(jnp.stack([w_down, swap(w_down, "tp", 2)]))
    down_far = down_far.transpose(1, 0, 2, 3).reshape(2, -1, width)
    down_mats = [down_far[0], swap(down_far[0], "tp", 1), down_far[1], swap(down_far[1], "tp", 1)]
    up_biases = [up_bias] + [swap(up_bias, "tp", s) for s in range(1, ranks)]
    blank = jnp.zeros((HEAD_PAD - head_width, width), BF)
    out_mat = jnp.concatenate([piece for mat in out_mats for piece in (mat, blank)], axis=0)

    attended_slots = attended.reshape(ranks, own, HEAD_PAD)
    merged = jnp.concatenate(
        [attended_slots[0]] + [swap(attended_slots[s], "tp", s) for s in range(1, ranks)], axis=1
    )
    hidden = x_float + dot_nn(merged, out_mat) + out_bias
    xhat_two, rstd_two = norm_parts(hidden)
    normed_two = (xhat_two * gain_two + shift_two).astype(BF)

    cot_rows = jnp.concatenate(to_sequence(cotangent), axis=0)
    cot_float = cot_rows.astype(F32)

    mlp_out = down_bias
    grad_normed_two = 0.0
    grad_up, grad_down, grad_up_bias = [], [], []
    for s in range(ranks):
        pre = dot_nn(normed_two, up_mats[s]) + up_biases[s].astype(F32)
        activ, pull = jax.vjp(gelu_tanh, pre)
        activ = activ.astype(BF)
        mlp_out = mlp_out + dot_nn(activ, down_mats[s])
        grad_pre = pull(dot_nt(cot_rows, down_mats[s]))[0].astype(BF)
        grad_normed_two = grad_normed_two + dot_nt(grad_pre, up_mats[s])
        grad_down.append(dot_tn(activ, cot_rows).astype(BF))
        grad_up.append(dot_tn(normed_two, grad_pre).astype(BF))
        grad_up_bias.append(jnp.sum(grad_pre.astype(F32), axis=0))
    block_out = (hidden + mlp_out).astype(BF)
    out_blocks = from_sequence([block_out[n * sub : (n + 1) * sub] for n in range(seqs)])

    grad_hidden = cot_float + norm_back(xhat_two, rstd_two, gain_two, grad_normed_two)
    grad_branch = grad_hidden.astype(BF)
    grad_merged = dot_nt(grad_branch, out_mat).astype(BF)
    grad_slots = [grad_merged[:, s * HEAD_PAD : (s + 1) * HEAD_PAD] for s in range(ranks)]
    grad_slots = [grad_slots[0]] + [swap(grad_slots[s], "tp", s) for s in range(1, ranks)]
    grad_attended = jnp.stack(grad_slots).reshape(ranks, seqs, sub, HEAD_PAD)
    grad_out = dot_tn(merged, grad_branch).astype(BF)

    fsdp = lax.axis_size("fsdp")
    near_down = [
        (grad_down[n].astype(F32) + swap(grad_down[n + 1], "tp", 1).astype(F32)).astype(BF)
        for n in (0, 2)
    ]
    near_down = jnp.stack(near_down, axis=0).reshape(2, fsdp, -1, width).transpose(1, 0, 2, 3)
    near_down = scatter_fsdp(near_down)
    down_shard = near_down[0].astype(F32) + swap(near_down[1], "tp", 2).astype(F32)
    sum_down = sum_ctx(down_shard.astype(BF))
    up_shard = scatter_tp(grad_up).astype(BF).reshape(fsdp, -1, grad_up[0].shape[1])
    sum_up = sum_ctx(scatter_fsdp(up_shard))
    out_shard = scatter_tp(
        [grad_out[s * HEAD_PAD : s * HEAD_PAD + head_width] for s in range(ranks)]
    )
    sum_out = sum_ctx(scatter_fsdp(out_shard.astype(BF).reshape(fsdp, -1, width)))

    early = [
        jnp.sum(grad_normed_two * xhat_two, axis=0),
        jnp.sum(grad_normed_two, axis=0),
        jnp.sum(grad_hidden, axis=0),
        jnp.sum(cot_float, axis=0),
    ]
    up_bias_all = jnp.take(jnp.stack(grad_up_bias), tp_rank ^ jnp.arange(ranks), axis=0)
    early = jnp.concatenate(early + [up_bias_all.reshape(-1)]).reshape(-1, LANES)
    early = lax.psum(early, ("fsdp", "ctx", "tp")).reshape(-1)

    dq, dkv = attend_back(where, seg_q, seg_k, queries, keyvals, attended, grad_attended, lse)
    if parts > 1:
        dkv = lax.psum_scatter(
            dkv, "ctx", scatter_dimension=0, tiled=True, axis_index_groups=groups
        )
    dq = dq.reshape(tokens, HEAD_PAD)
    dkv = dkv.reshape(tokens, 2 * HEAD_PAD)
    grad_normed = (dot_nn(dq, q_mat) + dot_nn(dkv, kv_mat)).astype(BF).reshape(ranks, own, width)
    grad_normed_one = scatter_tp([grad_normed[s] for s in range(ranks)])
    grad_x = grad_hidden + norm_back(xhat_one, rstd_one, gain_one, grad_normed_one)
    grad_x = grad_x.astype(BF)
    grad_blocks = from_sequence([grad_x[n * sub : (n + 1) * sub] for n in range(seqs)])

    grad_qkv = jnp.concatenate(
        [
            dot_tn(dq, normed_one)[:head_width],
            dot_tn(dkv, normed_one).reshape(2, HEAD_PAD, width)[:, :head_width].reshape(-1, width),
        ]
    ).astype(BF)
    grad_qkv = grad_qkv.reshape(3, fsdp, -1, width).transpose(1, 0, 2, 3)
    qkv_shard = scatter_fsdp(grad_qkv)
    sum_qkv = sum_ctx(qkv_shard.reshape(-1, width)).reshape(w_qkv.shape)

    bias_q = jnp.sum(dq.astype(F32), axis=0)[:head_width].reshape(heads, 64)
    bias_v = jnp.sum(dkv[:, HEAD_PAD:].astype(F32), axis=0)[:head_width].reshape(heads, 64)
    bias_rows = jnp.concatenate([bias_q, bias_v], axis=1)
    bias_all = lax.dynamic_update_slice(
        jnp.zeros((ranks * heads, 128), F32), bias_rows, (tp_rank * heads, 0)
    )
    late = [jnp.sum(grad_normed_one * xhat_one, axis=0), jnp.sum(grad_normed_one, axis=0)]
    late = jnp.concatenate(late + [bias_all.reshape(-1)]).reshape(-1, LANES)
    for axis in ("tp", "ctx", "fsdp"):
        late = butterfly(late, axis)
    late = late.reshape(-1)

    fsdp_rank = lax.axis_index("fsdp")

    def mine(vector):
        return lax.dynamic_slice_in_dim(vector, fsdp_rank * shard, shard, 0)

    def mine_bias(rows, like):
        rows = lax.dynamic_slice_in_dim(rows, tp_rank * like.shape[0], like.shape[0], 0)
        return lax.dynamic_slice_in_dim(rows, fsdp_rank * like.shape[1], like.shape[1], 1)

    sum_qv_bias = mine_bias(late[2 * width :].reshape(ranks * heads, 128), b_qv)
    sum_up_bias = mine_bias(early[4 * width :].reshape(ranks * b_up.shape[0], -1), b_up)
    return (
        out_blocks,
        grad_blocks,
        mine(late[:width]),
        mine(late[width : 2 * width]),
        sum_qkv,
        sum_qv_bias,
        sum_out,
        mine(early[2 * width : 3 * width]),
        mine(early[:width]),
        mine(early[width : 2 * width]),
        sum_up,
        sum_up_bias,
        sum_down,
        mine(early[3 * width : 4 * width]),
    )


def solution(mesh):
    rows = P("fsdp", ("ctx", "tp"), None)
    vector = P("fsdp")
    out_rows = P(("tp", "fsdp"), None)
    qkv_rows = P(None, ("tp", "fsdp"), None)
    bias = P("tp", "fsdp")
    weights = (
        vector, vector, qkv_rows, bias, out_rows, vector, vector, vector, P("fsdp", "tp"), bias, out_rows, vector,
    )
    return jax.shard_map(
        on_device,
        mesh=mesh,
        in_specs=(rows, P("fsdp", None)) + weights + (rows,),
        out_specs=(rows, rows) + weights,
        check_vma=False,
    )
```

time: 977 us -> 567 us (0.58)
  waiting for transfers between devices: 515 us -> 193 us
  starting transfers between devices: 1.19 us -> 144 us
  matrix products: 199 us -> 68.3 us
  other arithmetic: 123 us -> 26.9 us
  Pallas kernels: 0 us -> 44.8 us
  blocking collectives: 75.9 us -> 44.5 us
  between operations: 17.2 us -> 2.77 us
    psum x4 -> x0, waiting for transfers between devices: 197 us -> none  [the longest x1 68.4 us: on_device(): lax.psum(contract_cols(grad_pre, up_back).astype(jnp.bfloat16), 'tp')]
    ppermute x0 -> x85, waiting for transfers between devices: none -> 193 us  [the longest x61 152 us: swap(): return lax.ppermute(value, axis, [(i, i ^ bit) for i in range(size)])]
    reduce_scatter x7 -> x0, waiting for transfers between devices: 182 us -> none  [the longest x1 60.3 us: on_device(): lax.psum_scatter(grad_keys_all.astype(jnp.bfloat16), 'ctx', scatter_dimen...]
    ppermute x0 -> x85, starting transfers between devices: none -> 144 us  [the longest x61 86.6 us: swap(): return lax.ppermute(value, axis, [(i, i ^ bit) for i in range(size)])]
    dot_general x40 -> x33, matrix products: 199 us -> 68.3 us  [the longest x11 25.6 us: dot_tn(): lax.dot_general(left, right, (((0,), (0,)), ((), ())), preferred_element_...]
    all_gather x6 -> x0, waiting for transfers between devices: 123 us -> none  [the longest x1 64.3 us: on_device(): lax.all_gather(keys_local, 'ctx', axis=1, tiled=True)]
    reduce_sum x18 -> x8, other arithmetic: 71.5 us -> 4.91 us  [the longest x1 2.23 us: on_device(): jnp.sum(grad_hidden, axis=0)]
    all_gather x10 -> x0, blocking collectives: 56 us -> none  [the longest x1 12.3 us: on_device(): lax.all_gather(w_qkv, 'fsdp', axis=1, tiled=True)]
  transfers between devices with their start and end apart: 19 -> 85, of which waited for: 14 -> 32; matrix products, arithmetic and copies ran while one was open for 9% -> 21% of each run, Pallas kernels for 0% -> 8%
where the time goes in v1:
time: 567 us; the launch traced here: 563 us
  waiting for transfers between devices  193 us (34%)
  starting transfers between devices  144 us (25%)
  matrix products  68.3 us (12%)
  Pallas kernels  44.8 us (8%)
  blocking collectives  44.5 us (8%)
  local copies, waits for them, and re-layouts  38.3 us (7%)
  other arithmetic  26.9 us (5%)
    ppermute x61, waiting for transfers between devices, swap(): return lax.ppermute(value, axis, [(i, i ^ bit) for i in range(size)])  152 us
    ppermute x61, starting transfers between devices, swap(): return lax.ppermute(value, axis, [(i, i ^ bit) for i in range(size)])  86.6 us
    psum x1, blocking collectives, on_device(): early = lax.psum(early, ('fsdp', 'ctx', 'tp')).reshape(-1)  44.5 us
    ppermute x12, starting transfers between devices, send(): return lax.ppermute(value, 'ctx', pairs)  34.4 us
    dot_general x11, matrix products, dot_tn(): lax.dot_general(left, right, (((0,), (0,)), ((), ())), preferred_element_...  25.6 us
    dot_general x11, matrix products, dot_nt(): lax.dot_general(left, right, (((1,), (1,)), ((), ())), preferred_element_...  23.9 us
    pallas_call x1, Pallas kernels, attend_back(): pl.pallas_call(attend_back_kernel, out_shape=(jax.ShapeDtypeStruct(querie...  23.6 us
    ppermute x12, starting transfers between devices, sum_ctx(): lax.ppermute(part(rank ^ s), 'ctx', [(i, i ^ s) for i in range(size)])  23 us
  transfers between devices with their start and end apart: 85, of which 32 were waited for; matrix products, arithmetic and copies ran while one was open for 21% of the time, Pallas kernels for 8%

profile of v1, /device:TPU:0, one launch (start us, length us, event | category | flops | bytes accessed | tf_op | source)
XLA Modules:
  0.0 562.9 jit_solution(9961877900675771452)
XLA Ops:
  1.5 4.9 concatenate.49
  6.4 3.0 collective-permute-start.3
  18.6 3.6 collective-permute-start.2
  28.1 10.1 %collective-permute-done.1 = bf16[128,768]{1,0:T(8,128)(2,1)S(1)} collective-permute-done((bf16[128,768]{1,0:T(8,128)(2,1)S(1)}, bf16[128,768]{1,0:T(8,128)(2,1)S(1)}, u32[]{:S(2)}, u32[]{:S(2)}) %collective-permute-start.1) | collective-permute-done | bytes 196640 | tf_op jit(solution)/shard_map/ppermute | solution.py:113
  41.4 6.7 %collective-permute-done.13 = bf16[192,768]{1,0:T(8,128)(2,1)S(1)} collective-permute-done((bf16[192,768]{1,0:T(8,128)(2,1)S(1)}, bf16[192,768]{1,0:T(8,128)(2,1)S(1)}, u32[]{:S(2)}, u32[]{:S(2)}) %collective-permute-start.13) | collective-permute-done | bytes 294944 | tf_op jit(solution)/shard_map/ppermute | solution.py:35
  51.4 13.1 %collective-permute-done.5 = bf16[512,768]{1,0:T(8,128)(2,1)S(1)} collective-permute-done((bf16[512,768]{1,0:T(8,128)(2,1)S(1)}, bf16[512,768]{1,0:T(8,128)(2,1)S(1)}, u32[]{:S(2)}, u32[]{:S(2)}) %collective-permute-start.5) | collective-permute-done | bytes 786464 | tf_op jit(solution)/shard_map/ppermute | solution.py:35
  70.6 5.1 add_convert_fusion.1
  75.8 4.1 fusion.2
  80.0 21.2 %attend.1 = (bf16[4,4,128,256]{3,2,1,0:T(8,128)(2,1)S(1)}, f32[8,2048]{1,0:T(8,128)S(1)}) custom-call(s32[3]{0:T(128)S(1)} %pad_add_fusion.where_ref, s32[8]{0:T(128)S(1)} %get-tuple-element.33.low_ref, s32[8]{0:T(128)S(1)} %max.3.full_ref, s32[2048,1]{1,0:T(8,128)S(1)} %copy.38.seg_q_ref.seg_k_ref, ...), custom_call_target="tpu_custom_call" | custom-call | flops 6442450944 | bytes 16777216 | tf_op jit(solution)/shard_map/attend/pallas_call | solution.py:341
  105.0 5.0 collective-permute-done.10
  109.9 18.0 %collective-permute-start.29 = (bf16[128,768]{1,0:T(8,128)(2,1)S(1)}, bf16[128,768]{1,0:T(8,128)(2,1)S(1)}, u32[]{:S(2)}, u32[]{:S(2)}) collective-permute-start(bf16[128,768]{1,0:T(8,128)(2,1)S(1)} %copy-done.58), channel_id=1, source_target_pairs={{0,4},{4,8},{8,12},{12,0},{1,5},{5,9},{9,13},{13,1},{2,6},{6,10},{... | collective-permute-start | bytes 589832 | tf_op jit(solution)/shard_map/ppermute | solution.py:113
  132.6 23.0 %collective-permute-done.21 = bf16[768,768]{1,0:T(8,128)(2,1)S(1)} collective-permute-done((bf16[768,768]{1,0:T(8,128)(2,1)S(1)}, bf16[768,768]{1,0:T(8,128)(2,1)S(1)}, u32[]{:S(2)}, u32[]{:S(2)}) %collective-permute-start.21) | collective-permute-done | bytes 1179680 | tf_op jit(solution)/shard_map/ppermute | solution.py:35
  156.4 2.2 fusion.82
  160.3 2.0 convolution_convert_fusion.3
  165.7 2.0 convolution_convert_fusion.4
  167.7 2.0 convolution_convert_fusion.2
  169.7 2.1 fusion.99
  173.6 2.1 fusion.101
  175.8 2.2 fusion.80
  180.7 2.4 convert_reduce_fusion.6
  183.9 3.1 convolution_convert_fusion.5
  192.3 2.2 fusion.89
  194.6 44.5 %psum.7 = f32[48,128]{1,0:T(8,128)S(1)} all-reduce(f32[48,128]{1,0:T(8,128)S(1)} %bitcast.371), channel_id=1, replica_groups=mesh['fsdp'=2,'ctx'=4,'tp'=4] {'fsdp','ctx','tp'}, use_global_device_ids=true, to_apply=%region_24.25 | all-reduce | flops 6144 | bytes 49152 | tf_op jit(solution)/shard_map/psum | solution.py:531
  239.2 3.0 fusion.81
  242.7 2.8 add_convert_fusion.7
  246.3 2.3 collective-permute-start.26
  259.8 3.6 convolution_convert_fusion.1
  263.4 2.3 collective-permute-start.33
  273.2 2.6 add_convert_fusion.3
  277.4 23.6 %attend_back.1 = (bf16[4,4,128,256]{3,2,1,0:T(8,128)(2,1)S(1)}, bf16[1,4,4,128,512]{4,3,2,1,0:T(8,128)(2,1)}) custom-call(s32[3]{0:T(128)S(1)} %pad_add_fusion.where_ref, s32[8]{0:T(128)S(1)} %get-tuple-element.31.full_ref, s32[8]{0:T(128)S(1)} %get-tuple-element.30.high_ref, s32[1,2048]{1,0:T(1,128)S(1)} %constant_dynamic-slice_fusion.2.seg_k_ref.seg_q_ref, ...), custom_call_target="tpu_custom_call" | custom-call | flops 16106127360 | bytes 33554432 | tf_op jit(solution)/shard_map/attend_back/pallas_call | solution.py:369
  301.0 3.5 fusion.102
  308.6 2.5 copy.41
  311.1 4.4 fusion
  320.4 7.2 %collective-permute-done.57 = bf16[192,768]{1,0:T(8,128)(2,1)S(1)} collective-permute-done((bf16[192,768]{1,0:T(8,128)(2,1)S(1)}, bf16[192,768]{1,0:T(8,128)(2,1)S(1)}, u32[]{:S(2)}, u32[]{:S(2)}) %collective-permute-start.57) | collective-permute-done | bytes 294944 | tf_op jit(solution)/shard_map/ppermute | solution.py:35
  328.9 25.9 %collective-permute-start.58 = (bf16[96,768]{1,0:T(8,128)(2,1)S(1)}, bf16[96,768]{1,0:T(8,128)(2,1)S(1)}, u32[]{:S(2)}, u32[]{:S(2)}) collective-permute-start(bf16[96,768]{1,0:T(8,128)(2,1)S(1)} %dynamic-slice_bitcast_fusion.24), channel_id=1, source_target_pairs={{0,16},{16,0},{1,17},{17,1},{2,18},{18,2},{3,19},{19,3},{4,20},{20... | collective-permute-start | bytes 442376 | tf_op jit(solution)/shard_map/ppermute | solution.py:35
  355.3 4.2 collective-permute-done.58
  359.6 3.7 collective-permute-start.61
  363.3 4.3 collective-permute-done.48
  369.4 2.1 collective-permute-done.59
  371.6 3.4 collective-permute-start.64
  377.6 3.2 collective-permute-start.51
  382.0 2.2 collective-permute-done.51
  384.2 3.2 collective-permute-done.50
  387.7 2.1 collective-permute-start.54
  389.9 4.5 collective-permute-done.54
  394.4 3.3 collective-permute-start.52
  404.4 2.2 add_convert_fusion.5
  408.0 14.3 %collective-permute-done.37 = bf16[512,768]{1,0:T(8,128)(2,1)S(1)} collective-permute-done((bf16[512,768]{1,0:T(8,128)(2,1)S(1)}, bf16[512,768]{1,0:T(8,128)(2,1)S(1)}, u32[]{:S(2)}, u32[]{:S(2)}) %collective-permute-start.37) | collective-permute-done | bytes 786464 | tf_op jit(solution)/shard_map/ppermute | solution.py:35
  427.1 20.5 %collective-permute-done.42 = f32[24,128]{1,0:T(8,128)S(1)} collective-permute-done((f32[24,128]{1,0:T(8,128)S(1)}, f32[24,128]{1,0:T(8,128)S(1)}, u32[]{:S(2)}, u32[]{:S(2)}) %collective-permute-start.42) | collective-permute-done | bytes 12320 | tf_op jit(solution)/shard_map/ppermute | solution.py:35
  447.6 3.1 collective-permute-start.45
  454.2 2.0 collective-permute-done.46
  458.8 21.1 %collective-permute-done.47 = f32[24,128]{1,0:T(8,128)S(1)} collective-permute-done((f32[24,128]{1,0:T(8,128)S(1)}, f32[24,128]{1,0:T(8,128)S(1)}, u32[]{:S(2)}, u32[]{:S(2)}) %collective-permute-start.47) | collective-permute-done | bytes 12320 | tf_op jit(solution)/shard_map/ppermute | solution.py:35
  479.9 2.7 collective-permute-start.39
  484.9 9.6 %collective-permute-done.39 = bf16[128,768]{1,0:T(8,128)(2,1)S(1)} collective-permute-done((bf16[128,768]{1,0:T(8,128)(2,1)S(1)}, bf16[128,768]{1,0:T(8,128)(2,1)S(1)}, u32[]{:S(2)}, u32[]{:S(2)}) %collective-permute-start.39) | collective-permute-done | bytes 196640 | tf_op jit(solution)/shard_map/ppermute | solution.py:113
  498.9 10.6 %collective-permute-done.68 = bf16[384,768]{1,0:T(8,128)(2,1)S(1)} collective-permute-done((bf16[384,768]{1,0:T(8,128)(2,1)S(1)}, bf16[384,768]{1,0:T(8,128)(2,1)S(1)}, u32[]{:S(2)}, u32[]{:S(2)}) %collective-permute-start.68) | collective-permute-done | bytes 589856 | tf_op jit(solution)/shard_map/ppermute | solution.py:35
  511.5 2.7 collective-permute-start.69
  515.9 2.4 collective-permute-done.71
  518.4 8.1 %collective-permute-start.79 = (bf16[96,768]{1,0:T(8,128)(2,1)S(1)}, bf16[96,768]{1,0:T(8,128)(2,1)S(1)}, u32[]{:S(2)}, u32[]{:S(2)}) collective-permute-start(bf16[96,768]{1,0:T(8,128)(2,1)S(1)} %get-tuple-element.75), channel_id=1, source_target_pairs={{0,4},{4,0},{8,12},{12,8},{1,5},{5,1},{9,13},{13,9},{2,6},{6,2},{1... | collective-permute-start | bytes 442376 | tf_op jit(solution)/shard_map/ppermute | solution.py:81
  526.5 4.8 collective-permute-done.70
  531.8 7.3 %collective-permute-start.72 = (bf16[96,768]{1,0:T(8,128)(2,1)S(1)}, bf16[96,768]{1,0:T(8,128)(2,1)S(1)}, u32[]{:S(2)}, u32[]{:S(2)}) collective-permute-start(bf16[96,768]{1,0:T(8,128)(2,1)S(1)} %fusion.61), channel_id=1, source_target_pairs={{0,4},{4,0},{8,12},{12,8},{1,5},{5,1},{9,13},{13,9},{2,6},{6,2},{1... | collective-permute-start | bytes 442376 | tf_op jit(solution)/shard_map/ppermute | solution.py:35
  539.1 5.0 collective-permute-done.80
  544.5 7.1 %collective-permute-start.82 = (bf16[96,768]{1,0:T(8,128)(2,1)S(1)}, bf16[96,768]{1,0:T(8,128)(2,1)S(1)}, u32[]{:S(2)}, u32[]{:S(2)}) collective-permute-start(bf16[96,768]{1,0:T(8,128)(2,1)S(1)} %fusion.59), channel_id=1, source_target_pairs={{0,4},{4,0},{8,12},{12,8},{1,5},{5,1},{9,13},{13,9},{2,6},{6,2},{1... | collective-permute-start | bytes 442376 | tf_op jit(solution)/shard_map/ppermute | solution.py:35
  551.6 5.1 collective-permute-done.73
  556.9 4.1 collective-permute-done.83
  (493 shorter events, 122.5 us)
Async XLA Ops:
  9.4 13.8 %collective-permute-start.11 = (bf16[96,768]{1,0:T(8,128)(2,1)}, bf16[96,768]{1,0:T(8,128)(2,1)}, u32[]{:S(2)}, u32[]{:S(2)}) collective-permute-start(bf16[96,768]{1,0:T(8,128)(2,1)} %param.21), channel_id=1, source_target_pairs={{0,16},{16,0},{1,17},{17,1},{2,18},{18,2},{3,19},{19,3},{4,20},{20... | collective-permute-start | bytes 442376 | tf_op jit(solution)/shard_map/ppermute | solution.py:35
  9.5 39.3 %collective-permute-start.7 = (bf16[3,96,768]{2,1,0:T(8,128)(2,1)}, bf16[3,96,768]{2,1,0:T(8,128)(2,1)S(1)}, u32[]{:S(2)}, u32[]{:S(2)}) collective-permute-start(bf16[3,96,768]{2,1,0:T(8,128)(2,1)} %param.19), channel_id=1, source_target_pairs={{0,16},{16,0},{1,17},{17,1},{2,18},{18,2},{3,19},{19,3},{4,20},{20... | collective-permute-start | bytes 1327112 | tf_op jit(solution)/shard_map/ppermute | solution.py:35
  18.6 9.0 %collective-permute-start.2 = (bf16[128,768]{1,0:T(8,128)(2,1)S(1)}, bf16[128,768]{1,0:T(8,128)(2,1)S(1)}, u32[]{:S(2)}, u32[]{:S(2)}) collective-permute-start(bf16[128,768]{1,0:T(8,128)(2,1)S(1)} %get-tuple-element.69), channel_id=1, source_target_pairs={{0,12},{4,0},{8,4},{12,8},{1,13},{5,1},{9,5},{13,9},{2,14},{6,2},{... | collective-permute-start | bytes 589832 | tf_op jit(solution)/shard_map/ppermute | solution.py:113
  22.2 16.0 %collective-permute-start.1 = (bf16[128,768]{1,0:T(8,128)(2,1)S(1)}, bf16[128,768]{1,0:T(8,128)(2,1)S(1)}, u32[]{:S(2)}, u32[]{:S(2)}) collective-permute-start(bf16[128,768]{1,0:T(8,128)(2,1)S(1)} %get-tuple-element.70), channel_id=1, source_target_pairs={{0,8},{4,12},{8,0},{12,4},{1,9},{5,13},{9,1},{13,5},{2,10},{6,14},... | collective-permute-start | bytes 589832 | tf_op jit(solution)/shard_map/ppermute | solution.py:113
  22.2 16.0 %collective-permute-start = (bf16[128,768]{1,0:T(8,128)(2,1)S(1)}, bf16[128,768]{1,0:T(8,128)(2,1)S(1)}, u32[]{:S(2)}, u32[]{:S(2)}) collective-permute-start(bf16[128,768]{1,0:T(8,128)(2,1)S(1)} %get-tuple-element.68), channel_id=1, source_target_pairs={{0,4},{4,8},{8,12},{12,0},{1,5},{5,9},{9,13},{13,1},{2,6},{6,10},{... | collective-permute-start | bytes 589832 | tf_op jit(solution)/shard_map/ppermute | solution.py:113
  23.2 42.8 %collective-permute-start.16 = (bf16[384,768]{1,0:T(8,128)(2,1)}, bf16[384,768]{1,0:T(8,128)(2,1)S(1)}, u32[]{:S(2)}, u32[]{:S(2)}) collective-permute-start(bf16[384,768]{1,0:T(8,128)(2,1)} %param.27), channel_id=1, source_target_pairs={{0,2},{1,3},{2,0},{3,1},{4,6},{5,7},{6,4},{7,5},{8,10},{9,11},{10,... | collective-permute-start | bytes 1769480 | tf_op jit(solution)/shard_map/ppermute | solution.py:35
  27.6 23.2 %collective-permute-start.15 = (bf16[384,768]{1,0:T(8,128)(2,1)}, bf16[384,768]{1,0:T(8,128)(2,1)S(1)}, u32[]{:S(2)}, u32[]{:S(2)}) collective-permute-start(bf16[384,768]{1,0:T(8,128)(2,1)} %param.25), channel_id=1, source_target_pairs={{0,16},{16,0},{1,17},{17,1},{2,18},{18,2},{3,19},{19,3},{4,20},{20... | collective-permute-start | bytes 1769480 | tf_op jit(solution)/shard_map/ppermute | solution.py:35
  38.2 9.9 %collective-permute-start.13 = (bf16[192,768]{1,0:T(8,128)(2,1)S(1)}, bf16[192,768]{1,0:T(8,128)(2,1)S(1)}, u32[]{:S(2)}, u32[]{:S(2)}) collective-permute-start(bf16[192,768]{1,0:T(8,128)(2,1)S(1)} %bitcast.334), channel_id=1, source_target_pairs={{0,2},{1,3},{2,0},{3,1},{4,6},{5,7},{6,4},{7,5},{8,10},{9,11},{10,... | collective-permute-start | bytes 884744 | tf_op jit(solution)/shard_map/ppermute | solution.py:35
  40.7 23.8 %collective-permute-start.5 = (bf16[512,768]{1,0:T(8,128)(2,1)S(1)}, bf16[512,768]{1,0:T(8,128)(2,1)S(1)}, u32[]{:S(2)}, u32[]{:S(2)}) collective-permute-start(bf16[512,768]{1,0:T(8,128)(2,1)S(1)} %fusion.11), channel_id=1, source_target_pairs={{0,2},{1,3},{2,0},{3,1},{4,6},{5,7},{6,4},{7,5},{8,10},{9,11},{10,... | collective-permute-start | bytes 2359304 | tf_op jit(solution)/shard_map/ppermute | solution.py:35
  48.1 111.9 %collective-permute-start.31 = (bf16[128,768]{1,0:T(8,128)(2,1)}, bf16[128,768]{1,0:T(8,128)(2,1)S(1)}, u32[]{:S(2)}, u32[]{:S(2)}) collective-permute-start(bf16[128,768]{1,0:T(8,128)(2,1)} %get-tuple-element.62), channel_id=1, source_target_pairs={{0,12},{4,0},{8,4},{12,8},{1,13},{5,1},{9,5},{13,9},{2,14},{6,2},{... | collective-permute-start | bytes 589832 | tf_op jit(solution)/shard_map/ppermute | solution.py:113
  49.5 20.0 %collective-permute-start.4 = (bf16[512,768]{1,0:T(8,128)(2,1)S(1)}, bf16[512,768]{1,0:T(8,128)(2,1)S(1)}, u32[]{:S(2)}, u32[]{:S(2)}) collective-permute-start(bf16[512,768]{1,0:T(8,128)(2,1)S(1)} %fusion.11), channel_id=1, source_target_pairs={{0,1},{1,0},{2,3},{3,2},{4,5},{5,4},{6,7},{7,6},{8,9},{9,8},{10,11... | collective-permute-start | bytes 2359304 | tf_op jit(solution)/shard_map/ppermute | solution.py:35
  50.8 18.0 %collective-permute-start.14 = (bf16[192,768]{1,0:T(8,128)(2,1)S(1)}, bf16[192,768]{1,0:T(8,128)(2,1)S(1)}, u32[]{:S(2)}, u32[]{:S(2)}) collective-permute-start(bf16[192,768]{1,0:T(8,128)(2,1)S(1)} %collective-permute-done.13), channel_id=1, source_target_pairs={{0,1},{1,0},{2,3},{3,2},{4,5},{5,4},{6,7},{7,6},{8,9},{9,8},{10,11... | collective-permute-start | bytes 884744 | tf_op jit(solution)/shard_map/ppermute | solution.py:35
  66.0 94.3 %collective-permute-start.30 = (bf16[128,768]{1,0:T(8,128)(2,1)S(1)}, bf16[128,768]{1,0:T(8,128)(2,1)S(1)}, u32[]{:S(2)}, u32[]{:S(2)}) collective-permute-start(bf16[128,768]{1,0:T(8,128)(2,1)S(1)} %copy-done.59), channel_id=1, source_target_pairs={{0,8},{4,12},{8,0},{12,4},{1,9},{5,13},{9,1},{13,5},{2,10},{6,14},... | collective-permute-start | bytes 589832 | tf_op jit(solution)/shard_map/ppermute | solution.py:113
  68.9 34.1 %collective-permute-start.17 = (bf16[2,384,768]{2,1,0:T(8,128)(2,1)S(1)}, bf16[2,384,768]{2,1,0:T(8,128)(2,1)S(1)}, u32[]{:S(2)}, u32[]{:S(2)}) collective-permute-start(bf16[2,384,768]{2,1,0:T(8,128)(2,1)S(1)} %pad_maximum_fusion.2), channel_id=1, source_target_pairs={{0,16},{16,0},{1,17},{17,1},{2,18},{18,2},{3,19},{19,3},{4,20},{20... | collective-permute-start | bytes 3538952 | tf_op jit(solution)/shard_map/ppermute | solution.py:35
  102.2 25.7 %collective-permute-start.9 = (bf16[512,256]{1,0:T(8,128)(2,1)S(1)}, bf16[512,256]{1,0:T(8,128)(2,1)S(1)}, u32[]{:S(2)}, u32[]{:S(2)}) collective-permute-start(bf16[512,256]{1,0:T(8,128)(2,1)S(1)} %bitcast.354), channel_id=1, source_target_pairs={{0,2},{1,3},{2,0},{3,1},{4,6},{5,7},{6,4},{7,5},{8,10},{9,11},{10,... | collective-permute-start | bytes 786440 | tf_op jit(solution)/shard_map/ppermute | solution.py:35
  103.0 26.5 %collective-permute-start.8 = (bf16[512,256]{1,0:T(8,128)(2,1)S(1)}, bf16[512,256]{1,0:T(8,128)(2,1)S(1)}, u32[]{:S(2)}, u32[]{:S(2)}) collective-permute-start(bf16[512,256]{1,0:T(8,128)(2,1)S(1)} %bitcast.353), channel_id=1, source_target_pairs={{0,1},{1,0},{2,3},{3,2},{4,5},{5,4},{6,7},{7,6},{8,9},{9,8},{10,11... | collective-permute-start | bytes 786440 | tf_op jit(solution)/shard_map/ppermute | solution.py:35
  109.9 50.3 %collective-permute-start.29 = (bf16[128,768]{1,0:T(8,128)(2,1)S(1)}, bf16[128,768]{1,0:T(8,128)(2,1)S(1)}, u32[]{:S(2)}, u32[]{:S(2)}) collective-permute-start(bf16[128,768]{1,0:T(8,128)(2,1)S(1)} %copy-done.58), channel_id=1, source_target_pairs={{0,4},{4,8},{8,12},{12,0},{1,5},{5,9},{9,13},{13,1},{2,6},{6,10},{... | collective-permute-start | bytes 589832 | tf_op jit(solution)/shard_map/ppermute | solution.py:113
  127.9 27.7 %collective-permute-start.21 = (bf16[768,768]{1,0:T(8,128)(2,1)S(1)}, bf16[768,768]{1,0:T(8,128)(2,1)S(1)}, u32[]{:S(2)}, u32[]{:S(2)}) collective-permute-start(bf16[768,768]{1,0:T(8,128)(2,1)S(1)} %bitcast.328), channel_id=1, source_target_pairs={{0,2},{1,3},{2,0},{3,1},{4,6},{5,7},{6,4},{7,5},{8,10},{9,11},{10,... | collective-permute-start | bytes 3538952 | tf_op jit(solution)/shard_map/ppermute | solution.py:35
  129.5 29.2 %collective-permute-start.18 = (bf16[768,768]{1,0:T(8,128)(2,1)S(1)}, bf16[768,768]{1,0:T(8,128)(2,1)S(1)}, u32[]{:S(2)}, u32[]{:S(2)}) collective-permute-start(bf16[768,768]{1,0:T(8,128)(2,1)S(1)} %bitcast.329), channel_id=1, source_target_pairs={{0,1},{1,0},{2,3},{3,2},{4,5},{5,4},{6,7},{7,6},{8,9},{9,8},{10,11... | collective-permute-start | bytes 3538952 | tf_op jit(solution)/shard_map/ppermute | solution.py:35
  155.6 23.4 %collective-permute-start.25 = (bf16[768,768]{1,0:T(8,128)(2,1)S(1)}, bf16[768,768]{1,0:T(8,128)(2,1)S(1)}, u32[]{:S(2)}, u32[]{:S(2)}) collective-permute-start(bf16[768,768]{1,0:T(8,128)(2,1)S(1)} %bitcast.340), channel_id=1, source_target_pairs={{0,1},{1,0},{2,3},{3,2},{4,5},{5,4},{6,7},{7,6},{8,9},{9,8},{10,11... | collective-permute-start | bytes 3538952 | tf_op jit(solution)/shard_map/ppermute | solution.py:35
  158.6 22.0 %collective-permute-start.20 = (bf16[768,768]{1,0:T(8,128)(2,1)S(1)}, bf16[768,768]{1,0:T(8,128)(2,1)S(1)}, u32[]{:S(2)}, u32[]{:S(2)}) collective-permute-start(bf16[768,768]{1,0:T(8,128)(2,1)S(1)} %bitcast.337), channel_id=1, source_target_pairs={{0,1},{1,0},{2,3},{3,2},{4,5},{5,4},{6,7},{7,6},{8,9},{9,8},{10,11... | collective-permute-start | bytes 3538952 | tf_op jit(solution)/shard_map/ppermute | solution.py:35
  160.0 18.0 %collective-permute-start.23 = (bf16[768,768]{1,0:T(8,128)(2,1)S(1)}, bf16[768,768]{1,0:T(8,128)(2,1)S(1)}, u32[]{:S(2)}, u32[]{:S(2)}) collective-permute-start(bf16[768,768]{1,0:T(8,128)(2,1)S(1)} %collective-permute-done.21), channel_id=1, source_target_pairs={{0,1},{1,0},{2,3},{3,2},{4,5},{5,4},{6,7},{7,6},{8,9},{9,8},{10,11... | collective-permute-start | bytes 3538952 | tf_op jit(solution)/shard_map/ppermute | solution.py:35
  162.3 110.9 %collective-permute-start.75 = (bf16[768,768]{1,0:T(8,128)(2,1)}, bf16[768,768]{1,0:T(8,128)(2,1)}, u32[]{:S(2)}, u32[]{:S(2)}) collective-permute-start(bf16[768,768]{1,0:T(8,128)(2,1)} %convolution_convert_fusion.3), channel_id=1, source_target_pairs={{0,1},{1,0},{2,3},{3,2},{4,5},{5,4},{6,7},{7,6},{8,9},{9,8},{10,11... | collective-permute-start | bytes 3538952 | tf_op jit(solution)/shard_map/ppermute | solution.py:35
  246.3 17.1 %collective-permute-start.26 = (bf16[128,768]{1,0:T(8,128)(2,1)}, bf16[128,768]{1,0:T(8,128)(2,1)}, u32[]{:S(2)}, u32[]{:S(2)}) collective-permute-start(bf16[128,768]{1,0:T(8,128)(2,1)} %get-tuple-element.66), channel_id=1, source_target_pairs={{4,0},{8,4},{12,8},{0,12},{5,1},{9,5},{13,9},{1,13},{6,2},{10,6},{... | collective-permute-start | bytes 589832 | tf_op jit(solution)/shard_map/ppermute | solution.py:113
  248.6 18.2 %collective-permute-start.27 = (bf16[128,768]{1,0:T(8,128)(2,1)}, bf16[128,768]{1,0:T(8,128)(2,1)}, u32[]{:S(2)}, u32[]{:S(2)}) collective-permute-start(bf16[128,768]{1,0:T(8,128)(2,1)} %get-tuple-element.65), channel_id=1, source_target_pairs={{8,0},{12,4},{0,8},{4,12},{9,1},{13,5},{1,9},{5,13},{10,2},{14,6},... | collective-permute-start | bytes 589832 | tf_op jit(solution)/shard_map/ppermute | solution.py:113
  250.0 17.8 %collective-permute-start.28 = (bf16[128,768]{1,0:T(8,128)(2,1)}, bf16[128,768]{1,0:T(8,128)(2,1)}, u32[]{:S(2)}, u32[]{:S(2)}) collective-permute-start(bf16[128,768]{1,0:T(8,128)(2,1)} %get-tuple-element.64), channel_id=1, source_target_pairs={{12,0},{0,4},{4,8},{8,12},{13,1},{1,5},{5,9},{9,13},{14,2},{2,6},{... | collective-permute-start | bytes 589832 | tf_op jit(solution)/shard_map/ppermute | solution.py:113
  253.0 22.8 %collective-permute-start.34 = (bf16[512,256]{1,0:T(8,128)(2,1)}, bf16[512,256]{1,0:T(8,128)(2,1)}, u32[]{:S(2)}, u32[]{:S(2)}) collective-permute-start(bf16[512,256]{1,0:T(8,128)(2,1)} %get-tuple-element.47), channel_id=1, source_target_pairs={{0,3},{1,2},{2,1},{3,0},{4,7},{5,6},{6,5},{7,4},{8,11},{9,10},{10,... | collective-permute-start | bytes 786440 | tf_op jit(solution)/shard_map/ppermute | solution.py:35
  263.4 12.9 %collective-permute-start.33 = (bf16[512,256]{1,0:T(8,128)(2,1)S(1)}, bf16[512,256]{1,0:T(8,128)(2,1)S(1)}, u32[]{:S(2)}, u32[]{:S(2)}) collective-permute-start(bf16[512,256]{1,0:T(8,128)(2,1)S(1)} %copy-done.51), channel_id=1, source_target_pairs={{0,2},{1,3},{2,0},{3,1},{4,6},{5,7},{6,4},{7,5},{8,10},{9,11},{10,... | collective-permute-start | bytes 786440 | tf_op jit(solution)/shard_map/ppermute | solution.py:35
  266.8 9.5 %collective-permute-start.32 = (bf16[512,256]{1,0:T(8,128)(2,1)S(1)}, bf16[512,256]{1,0:T(8,128)(2,1)S(1)}, u32[]{:S(2)}, u32[]{:S(2)}) collective-permute-start(bf16[512,256]{1,0:T(8,128)(2,1)S(1)} %copy-done.50), channel_id=1, source_target_pairs={{0,1},{1,0},{2,3},{3,2},{4,5},{5,4},{6,7},{7,6},{8,9},{9,8},{10,11... | collective-permute-start | bytes 786440 | tf_op jit(solution)/shard_map/ppermute | solution.py:35
  267.8 49.6 %collective-permute-start.56 = (bf16[192,768]{1,0:T(8,128)(2,1)}, bf16[192,768]{1,0:T(8,128)(2,1)}, u32[]{:S(2)}, u32[]{:S(2)}) collective-permute-start(bf16[192,768]{1,0:T(8,128)(2,1)} %get-tuple-element.43), channel_id=1, source_target_pairs={{0,1},{1,0},{2,3},{3,2},{4,5},{5,4},{6,7},{7,6},{8,9},{9,8},{10,11... | collective-permute-start | bytes 884744 | tf_op jit(solution)/shard_map/ppermute | solution.py:35
  273.2 47.3 %collective-permute-start.55 = (bf16[192,768]{1,0:T(8,128)(2,1)}, bf16[192,768]{1,0:T(8,128)(2,1)}, u32[]{:S(2)}, u32[]{:S(2)}) collective-permute-start(bf16[192,768]{1,0:T(8,128)(2,1)} %get-tuple-element.42), channel_id=1, source_target_pairs={{0,1},{1,0},{2,3},{3,2},{4,5},{5,4},{6,7},{7,6},{8,9},{9,8},{10,11... | collective-permute-start | bytes 884744 | tf_op jit(solution)/shard_map/ppermute | solution.py:35
  275.8 128.6 %collective-permute-start.66 = (bf16[768,768]{1,0:T(8,128)(2,1)}, bf16[768,768]{1,0:T(8,128)(2,1)}, u32[]{:S(2)}, u32[]{:S(2)}) collective-permute-start(bf16[768,768]{1,0:T(8,128)(2,1)} %convolution_convert_fusion.5), channel_id=1, source_target_pairs={{0,1},{1,0},{2,3},{3,2},{4,5},{5,4},{6,7},{7,6},{8,9},{9,8},{10,11... | collective-permute-start | bytes 3538952 | tf_op jit(solution)/shard_map/ppermute | solution.py:35
  307.8 92.8 %collective-permute-start.36 = (bf16[512,768]{1,0:T(8,128)(2,1)}, bf16[512,768]{1,0:T(8,128)(2,1)}, u32[]{:S(2)}, u32[]{:S(2)}) collective-permute-start(bf16[512,768]{1,0:T(8,128)(2,1)} %get-tuple-element.37), channel_id=1, source_target_pairs={{0,1},{1,0},{2,3},{3,2},{4,5},{5,4},{6,7},{7,6},{8,9},{9,8},{10,11... | collective-permute-start | bytes 2359304 | tf_op jit(solution)/shard_map/ppermute | solution.py:35
  318.5 9.2 %collective-permute-start.57 = (bf16[192,768]{1,0:T(8,128)(2,1)S(1)}, bf16[192,768]{1,0:T(8,128)(2,1)S(1)}, u32[]{:S(2)}, u32[]{:S(2)}) collective-permute-start(bf16[192,768]{1,0:T(8,128)(2,1)S(1)} %add_convert_fusion.10), channel_id=1, source_target_pairs={{0,2},{1,3},{2,0},{3,1},{4,6},{5,7},{6,4},{7,5},{8,10},{9,11},{10,... | collective-permute-start | bytes 884744 | tf_op jit(solution)/shard_map/ppermute | solution.py:35
  328.9 30.6 %collective-permute-start.58 = (bf16[96,768]{1,0:T(8,128)(2,1)S(1)}, bf16[96,768]{1,0:T(8,128)(2,1)S(1)}, u32[]{:S(2)}, u32[]{:S(2)}) collective-permute-start(bf16[96,768]{1,0:T(8,128)(2,1)S(1)} %dynamic-slice_bitcast_fusion.24), channel_id=1, source_target_pairs={{0,16},{16,0},{1,17},{17,1},{2,18},{18,2},{3,19},{19,3},{4,20},{20... | collective-permute-start | bytes 442376 | tf_op jit(solution)/shard_map/ppermute | solution.py:35
  354.9 12.7 %collective-permute-start.48 = (bf16[3,96,768]{2,1,0:T(8,128)(2,1)S(1)}, bf16[3,96,768]{2,1,0:T(8,128)(2,1)S(1)}, u32[]{:S(2)}, u32[]{:S(2)}) collective-permute-start(bf16[3,96,768]{2,1,0:T(8,128)(2,1)S(1)} %dynamic-slice_bitcast_fusion.1), channel_id=1, source_target_pairs={{0,16},{16,0},{1,17},{17,1},{2,18},{18,2},{3,19},{19,3},{4,20},{20... | collective-permute-start | bytes 1327112 | tf_op jit(solution)/shard_map/ppermute | solution.py:35
  359.6 9.8 %collective-permute-start.61 = (bf16[24,768]{1,0:T(8,128)(2,1)S(1)}, bf16[24,768]{1,0:T(8,128)(2,1)S(1)}, u32[]{:S(2)}, u32[]{:S(2)}) collective-permute-start(bf16[24,768]{1,0:T(8,128)(2,1)S(1)} %get-tuple-element.99), channel_id=1, source_target_pairs={{0,12},{4,8},{8,4},{12,0},{1,13},{5,9},{9,5},{13,1},{2,14},{6,10},... | collective-permute-start | bytes 110600 | tf_op jit(solution)/shard_map/ppermute | solution.py:81
  384.2 23.1 %collective-permute-start.76 = (bf16[768,768]{1,0:T(8,128)(2,1)}, bf16[768,768]{1,0:T(8,128)(2,1)S(1)}, u32[]{:S(2)}, u32[]{:S(2)}) collective-permute-start(bf16[768,768]{1,0:T(8,128)(2,1)} %convolution_convert_fusion.1), channel_id=1, source_target_pairs={{0,1},{1,0},{2,3},{3,2},{4,5},{5,4},{6,7},{7,6},{8,9},{9,8},{10,11... | collective-permute-start | bytes 3538952 | tf_op jit(solution)/shard_map/ppermute | solution.py:35
  389.8 8.8 %collective-permute-start.53 = (bf16[72,768]{1,0:T(8,128)(2,1)S(1)}, bf16[72,768]{1,0:T(8,128)(2,1)S(1)}, u32[]{:S(2)}, u32[]{:S(2)}) collective-permute-start(bf16[72,768]{1,0:T(8,128)(2,1)S(1)} %fusion.64), channel_id=1, source_target_pairs={{0,8},{4,12},{8,0},{12,4},{1,9},{5,13},{9,1},{13,5},{2,10},{6,14},... | collective-permute-start | bytes 331784 | tf_op jit(solution)/shard_map/ppermute | solution.py:35
  398.6 96.0 %collective-permute-start.65 = (bf16[768,768]{1,0:T(8,128)(2,1)S(1)}, bf16[768,768]{1,0:T(8,128)(2,1)S(1)}, u32[]{:S(2)}, u32[]{:S(2)}) collective-permute-start(bf16[768,768]{1,0:T(8,128)(2,1)S(1)} %copy-done.65), channel_id=1, source_target_pairs={{0,1},{1,0},{2,3},{3,2},{4,5},{5,4},{6,7},{7,6},{8,9},{9,8},{10,11... | collective-permute-start | bytes 3538952 | tf_op jit(solution)/shard_map/ppermute | solution.py:35
  401.9 20.4 %collective-permute-start.37 = (bf16[512,768]{1,0:T(8,128)(2,1)S(1)}, bf16[512,768]{1,0:T(8,128)(2,1)S(1)}, u32[]{:S(2)}, u32[]{:S(2)}) collective-permute-start(bf16[512,768]{1,0:T(8,128)(2,1)S(1)} %add_convert_fusion.6), channel_id=1, source_target_pairs={{0,2},{1,3},{2,0},{3,1},{4,6},{5,7},{6,4},{7,5},{8,10},{9,11},{10,... | collective-permute-start | bytes 2359304 | tf_op jit(solution)/shard_map/ppermute | solution.py:35
  406.6 88.0 %collective-permute-start.67 = (bf16[768,768]{1,0:T(8,128)(2,1)S(1)}, bf16[768,768]{1,0:T(8,128)(2,1)S(1)}, u32[]{:S(2)}, u32[]{:S(2)}) collective-permute-start(bf16[768,768]{1,0:T(8,128)(2,1)S(1)} %add_convert_fusion.5), channel_id=1, source_target_pairs={{0,2},{1,3},{2,0},{3,1},{4,6},{5,7},{6,4},{7,5},{8,10},{9,11},{10,... | collective-permute-start | bytes 3538952 | tf_op jit(solution)/shard_map/ppermute | solution.py:35
  423.4 24.2 %collective-permute-start.42 = (f32[24,128]{1,0:T(8,128)S(1)}, f32[24,128]{1,0:T(8,128)S(1)}, u32[]{:S(2)}, u32[]{:S(2)}) collective-permute-start(f32[24,128]{1,0:T(8,128)S(1)} %maximum_bitcast_fusion.1), channel_id=1, source_target_pairs={{0,2},{1,3},{2,0},{3,1},{4,6},{5,7},{6,4},{7,5},{8,10},{9,11},{10,... | collective-permute-start | bytes 36872 | tf_op jit(solution)/shard_map/ppermute | solution.py:35
  424.9 22.7 %collective-permute-start.43 = (f32[24,128]{1,0:T(8,128)S(1)}, f32[24,128]{1,0:T(8,128)S(1)}, u32[]{:S(2)}, u32[]{:S(2)}) collective-permute-start(f32[24,128]{1,0:T(8,128)S(1)} %maximum_bitcast_fusion.1), channel_id=1, source_target_pairs={{0,3},{1,2},{2,1},{3,0},{4,7},{5,6},{6,5},{7,4},{8,11},{9,10},{10,... | collective-permute-start | bytes 36872 | tf_op jit(solution)/shard_map/ppermute | solution.py:35
  424.9 22.7 %collective-permute-start.41 = (f32[24,128]{1,0:T(8,128)S(1)}, f32[24,128]{1,0:T(8,128)S(1)}, u32[]{:S(2)}, u32[]{:S(2)}) collective-permute-start(f32[24,128]{1,0:T(8,128)S(1)} %maximum_bitcast_fusion.1), channel_id=1, source_target_pairs={{0,1},{1,0},{2,3},{3,2},{4,5},{5,4},{6,7},{7,6},{8,9},{9,8},{10,11... | collective-permute-start | bytes 36872 | tf_op jit(solution)/shard_map/ppermute | solution.py:35
  452.4 43.8 %collective-permute-start.77 = (bf16[2,384,768]{2,1,0:T(8,128)(2,1)S(1)}, bf16[2,384,768]{2,1,0:T(8,128)(2,1)S(1)}, u32[]{:S(2)}, u32[]{:S(2)}) collective-permute-start(bf16[2,384,768]{2,1,0:T(8,128)(2,1)S(1)} %fusion.49), channel_id=1, source_target_pairs={{0,16},{16,0},{1,17},{17,1},{2,18},{18,2},{3,19},{19,3},{4,20},{20... | collective-permute-start | bytes 3538952 | tf_op jit(solution)/shard_map/ppermute | solution.py:35
  456.2 23.7 %collective-permute-start.47 = (f32[24,128]{1,0:T(8,128)S(1)}, f32[24,128]{1,0:T(8,128)S(1)}, u32[]{:S(2)}, u32[]{:S(2)}) collective-permute-start(f32[24,128]{1,0:T(8,128)S(1)} %add_add_fusion.1), channel_id=1, source_target_pairs={{0,16},{16,0},{1,17},{17,1},{2,18},{18,2},{3,19},{19,3},{4,20},{20... | collective-permute-start | bytes 36872 | tf_op jit(solution)/shard_map/ppermute | solution.py:35
  456.8 27.8 %collective-permute-start.38 = (bf16[128,768]{1,0:T(8,128)(2,1)S(1)}, bf16[128,768]{1,0:T(8,128)(2,1)S(1)}, u32[]{:S(2)}, u32[]{:S(2)}) collective-permute-start(bf16[128,768]{1,0:T(8,128)(2,1)S(1)} %get-tuple-element.59), channel_id=1, source_target_pairs={{4,0},{8,4},{12,8},{0,12},{5,1},{9,5},{13,9},{1,13},{6,2},{10,6},{... | collective-permute-start | bytes 589832 | tf_op jit(solution)/shard_map/ppermute | solution.py:113
  479.9 14.6 %collective-permute-start.39 = (bf16[128,768]{1,0:T(8,128)(2,1)S(1)}, bf16[128,768]{1,0:T(8,128)(2,1)S(1)}, u32[]{:S(2)}, u32[]{:S(2)}) collective-permute-start(bf16[128,768]{1,0:T(8,128)(2,1)S(1)} %get-tuple-element.58), channel_id=1, source_target_pairs={{8,0},{12,4},{0,8},{4,12},{9,1},{13,5},{1,9},{5,13},{10,2},{14,6},... | collective-permute-start | bytes 589832 | tf_op jit(solution)/shard_map/ppermute | solution.py:113
  484.6 10.0 %collective-permute-start.40 = (bf16[128,768]{1,0:T(8,128)(2,1)S(1)}, bf16[128,768]{1,0:T(8,128)(2,1)S(1)}, u32[]{:S(2)}, u32[]{:S(2)}) collective-permute-start(bf16[128,768]{1,0:T(8,128)(2,1)S(1)} %get-tuple-element.57), channel_id=1, source_target_pairs={{12,0},{0,4},{4,8},{8,12},{13,1},{1,5},{5,9},{9,13},{14,2},{2,6},{... | collective-permute-start | bytes 589832 | tf_op jit(solution)/shard_map/ppermute | solution.py:113
  495.2 14.3 %collective-permute-start.68 = (bf16[384,768]{1,0:T(8,128)(2,1)S(1)}, bf16[384,768]{1,0:T(8,128)(2,1)S(1)}, u32[]{:S(2)}, u32[]{:S(2)}) collective-permute-start(bf16[384,768]{1,0:T(8,128)(2,1)S(1)} %dynamic-slice_bitcast_fusion), channel_id=1, source_target_pairs={{0,16},{16,0},{1,17},{17,1},{2,18},{18,2},{3,19},{19,3},{4,20},{20... | collective-permute-start | bytes 1769480 | tf_op jit(solution)/shard_map/ppermute | solution.py:35
  496.6 17.6 %collective-permute-start.78 = (bf16[384,768]{1,0:T(8,128)(2,1)S(1)}, bf16[384,768]{1,0:T(8,128)(2,1)S(1)}, u32[]{:S(2)}, u32[]{:S(2)}) collective-permute-start(bf16[384,768]{1,0:T(8,128)(2,1)S(1)} %slice_bitcast_fusion), channel_id=1, source_target_pairs={{0,2},{1,3},{2,0},{3,1},{4,6},{5,7},{6,4},{7,5},{8,10},{9,11},{10,... | collective-permute-start | bytes 1769480 | tf_op jit(solution)/shard_map/ppermute | solution.py:35
  509.7 8.7 %collective-permute-start.71 = (bf16[96,768]{1,0:T(8,128)(2,1)S(1)}, bf16[96,768]{1,0:T(8,128)(2,1)S(1)}, u32[]{:S(2)}, u32[]{:S(2)}) collective-permute-start(bf16[96,768]{1,0:T(8,128)(2,1)S(1)} %get-tuple-element.83), channel_id=1, source_target_pairs={{0,12},{4,8},{8,4},{12,0},{1,13},{5,9},{9,5},{13,1},{2,14},{6,10},... | collective-permute-start | bytes 442376 | tf_op jit(solution)/shard_map/ppermute | solution.py:81
  509.8 21.6 %collective-permute-start.70 = (bf16[96,768]{1,0:T(8,128)(2,1)S(1)}, bf16[96,768]{1,0:T(8,128)(2,1)S(1)}, u32[]{:S(2)}, u32[]{:S(2)}) collective-permute-start(bf16[96,768]{1,0:T(8,128)(2,1)S(1)} %get-tuple-element.84), channel_id=1, source_target_pairs={{0,8},{4,12},{8,0},{12,4},{1,9},{5,13},{9,1},{13,5},{2,10},{6,14},... | collective-permute-start | bytes 442376 | tf_op jit(solution)/shard_map/ppermute | solution.py:81
  511.5 19.9 %collective-permute-start.69 = (bf16[96,768]{1,0:T(8,128)(2,1)S(1)}, bf16[96,768]{1,0:T(8,128)(2,1)S(1)}, u32[]{:S(2)}, u32[]{:S(2)}) collective-permute-start(bf16[96,768]{1,0:T(8,128)(2,1)S(1)} %get-tuple-element.82), channel_id=1, source_target_pairs={{0,4},{4,0},{8,12},{12,8},{1,5},{5,1},{9,13},{13,9},{2,6},{6,2},{1... | collective-permute-start | bytes 442376 | tf_op jit(solution)/shard_map/ppermute | solution.py:81
  514.4 17.4 %collective-permute-start.81 = (bf16[96,768]{1,0:T(8,128)(2,1)S(1)}, bf16[96,768]{1,0:T(8,128)(2,1)S(1)}, u32[]{:S(2)}, u32[]{:S(2)}) collective-permute-start(bf16[96,768]{1,0:T(8,128)(2,1)S(1)} %get-tuple-element.76), channel_id=1, source_target_pairs={{0,12},{4,8},{8,4},{12,0},{1,13},{5,9},{9,5},{13,1},{2,14},{6,10},... | collective-permute-start | bytes 442376 | tf_op jit(solution)/shard_map/ppermute | solution.py:81
  514.6 29.5 %collective-permute-start.80 = (bf16[96,768]{1,0:T(8,128)(2,1)S(1)}, bf16[96,768]{1,0:T(8,128)(2,1)S(1)}, u32[]{:S(2)}, u32[]{:S(2)}) collective-permute-start(bf16[96,768]{1,0:T(8,128)(2,1)S(1)} %get-tuple-element.77), channel_id=1, source_target_pairs={{0,8},{4,12},{8,0},{12,4},{1,9},{5,13},{9,1},{13,5},{2,10},{6,14},... | collective-permute-start | bytes 442376 | tf_op jit(solution)/shard_map/ppermute | solution.py:81
  518.4 25.7 %collective-permute-start.79 = (bf16[96,768]{1,0:T(8,128)(2,1)S(1)}, bf16[96,768]{1,0:T(8,128)(2,1)S(1)}, u32[]{:S(2)}, u32[]{:S(2)}) collective-permute-start(bf16[96,768]{1,0:T(8,128)(2,1)S(1)} %get-tuple-element.75), channel_id=1, source_target_pairs={{0,4},{4,0},{8,12},{12,8},{1,5},{5,1},{9,13},{13,9},{2,6},{6,2},{1... | collective-permute-start | bytes 442376 | tf_op jit(solution)/shard_map/ppermute | solution.py:81
  531.4 13.1 %collective-permute-start.74 = (bf16[96,768]{1,0:T(8,128)(2,1)S(1)}, bf16[96,768]{1,0:T(8,128)(2,1)S(1)}, u32[]{:S(2)}, u32[]{:S(2)}) collective-permute-start(bf16[96,768]{1,0:T(8,128)(2,1)S(1)} %fusion.61), channel_id=1, source_target_pairs={{0,12},{4,8},{8,4},{12,0},{1,13},{5,9},{9,5},{13,1},{2,14},{6,10},... | collective-permute-start | bytes 442376 | tf_op jit(solution)/shard_map/ppermute | solution.py:35
  531.8 24.9 %collective-permute-start.73 = (bf16[96,768]{1,0:T(8,128)(2,1)S(1)}, bf16[96,768]{1,0:T(8,128)(2,1)S(1)}, u32[]{:S(2)}, u32[]{:S(2)}) collective-permute-start(bf16[96,768]{1,0:T(8,128)(2,1)S(1)} %fusion.61), channel_id=1, source_target_pairs={{0,8},{4,12},{8,0},{12,4},{1,9},{5,13},{9,1},{13,5},{2,10},{6,14},... | collective-permute-start | bytes 442376 | tf_op jit(solution)/shard_map/ppermute | solution.py:35
  531.8 24.9 %collective-permute-start.72 = (bf16[96,768]{1,0:T(8,128)(2,1)S(1)}, bf16[96,768]{1,0:T(8,128)(2,1)S(1)}, u32[]{:S(2)}, u32[]{:S(2)}) collective-permute-start(bf16[96,768]{1,0:T(8,128)(2,1)S(1)} %fusion.61), channel_id=1, source_target_pairs={{0,4},{4,0},{8,12},{12,8},{1,5},{5,1},{9,13},{13,9},{2,6},{6,2},{1... | collective-permute-start | bytes 442376 | tf_op jit(solution)/shard_map/ppermute | solution.py:35
  544.2 12.7 %collective-permute-start.84 = (bf16[96,768]{1,0:T(8,128)(2,1)S(1)}, bf16[96,768]{1,0:T(8,128)(2,1)S(1)}, u32[]{:S(2)}, u32[]{:S(2)}) collective-permute-start(bf16[96,768]{1,0:T(8,128)(2,1)S(1)} %fusion.59), channel_id=1, source_target_pairs={{0,12},{4,8},{8,4},{12,0},{1,13},{5,9},{9,5},{13,1},{2,14},{6,10},... | collective-permute-start | bytes 442376 | tf_op jit(solution)/shard_map/ppermute | solution.py:35
  544.5 16.4 %collective-permute-start.83 = (bf16[96,768]{1,0:T(8,128)(2,1)S(1)}, bf16[96,768]{1,0:T(8,128)(2,1)S(1)}, u32[]{:S(2)}, u32[]{:S(2)}) collective-permute-start(bf16[96,768]{1,0:T(8,128)(2,1)S(1)} %fusion.59), channel_id=1, source_target_pairs={{0,8},{4,12},{8,0},{12,4},{1,9},{5,13},{9,1},{13,5},{2,10},{6,14},... | collective-permute-start | bytes 442376 | tf_op jit(solution)/shard_map/ppermute | solution.py:35
  544.5 16.4 %collective-permute-start.82 = (bf16[96,768]{1,0:T(8,128)(2,1)S(1)}, bf16[96,768]{1,0:T(8,128)(2,1)S(1)}, u32[]{:S(2)}, u32[]{:S(2)}) collective-permute-start(bf16[96,768]{1,0:T(8,128)(2,1)S(1)} %fusion.59), channel_id=1, source_target_pairs={{0,4},{4,0},{8,12},{12,8},{1,5},{5,1},{9,13},{13,9},{2,6},{6,2},{1... | collective-permute-start | bytes 442376 | tf_op jit(solution)/shard_map/ppermute | solution.py:35
  (108 other events, 1163.7 us)

commit v2 on v1

v2 whole, which is shorter than its diff:
```python
import functools

import jax
import jax.numpy as jnp
from jax import lax
from jax.experimental import pallas as pl
from jax.experimental.pallas import tpu as pltpu
from jax.sharding import PartitionSpec as P

EPS = 1e-05
NEG = -1e30
BF = jnp.bfloat16
F32 = jnp.float32
LANES = 128
HEAD_PAD = 256
BQ = 512
BK = 512
VMEM_BYTES = 48 * 1024 * 1024


def dot_nn(left, right):
    return lax.dot_general(left, right, (((1,), (0,)), ((), ())), preferred_element_type=F32)


def dot_nt(left, right):
    return lax.dot_general(left, right, (((1,), (1,)), ((), ())), preferred_element_type=F32)


def dot_tn(left, right):
    return lax.dot_general(left, right, (((0,), (0,)), ((), ())), preferred_element_type=F32)


def swap(value, axis, bit):
    size = lax.axis_size(axis)
    return lax.ppermute(value, axis, [(i, i ^ bit) for i in range(size)])


def tree_sum(items):
    items = [item.astype(F32) for item in items]
    while len(items) > 1:
        items = [items[i] + items[i + 1] for i in range(0, len(items), 2)]
    return items[0]


def butterfly(value, axis):
    size = lax.axis_size(axis)
    if size & (size - 1):
        return lax.psum(value, axis)
    return tree_sum([value] + [swap(value, axis, bit) for bit in range(1, size)])


def gather_fsdp(values, axis):
    if lax.axis_size("fsdp") != 2:
        return [lax.all_gather(value, "fsdp", axis=axis, tiled=True) for value in values]
    whole = values[0] if len(values) == 1 else jnp.concatenate(values, axis=axis)
    other = swap(whole, "fsdp", 1)
    first = lax.axis_index("fsdp") == 0
    out, start = [], 0
    for value in values:
        size = value.shape[axis]
        theirs = lax.slice_in_dim(other, start, start + size, axis=axis)
        start += size
        pair = [jnp.where(first, value, theirs), jnp.where(first, theirs, value)]
        out.append(jnp.concatenate(pair, axis=axis))
    return out


def scatter_fsdp(value):
    if lax.axis_size("fsdp") != 2:
        return lax.psum_scatter(value, "fsdp", scatter_dimension=0, tiled=False)
    rank = lax.axis_index("fsdp")
    mine = lax.dynamic_index_in_dim(value, rank, 0, keepdims=False)
    theirs = lax.dynamic_index_in_dim(value, 1 - rank, 0, keepdims=False)
    return (mine.astype(F32) + swap(theirs, "fsdp", 1).astype(F32)).astype(value.dtype)


def sum_ctx(value):
    size = lax.axis_size("ctx")
    rows = value.shape[0]
    if size != 4 or rows % (8 * size):
        return lax.psum(value, "ctx").astype(F32)
    rank = lax.axis_index("ctx")
    near, far = rank % 2, rank // 2
    parts = value.reshape((2, 2, rows // size) + value.shape[1:])

    def halve(array, axis, bit, side):
        mine = lax.dynamic_index_in_dim(array, side, axis, keepdims=False)
        theirs = lax.dynamic_index_in_dim(array, 1 - side, axis, keepdims=False)
        return (mine.astype(F32) + swap(theirs, "ctx", bit).astype(F32)).astype(value.dtype)

    def double(array, axis, bit, side):
        other = swap(array, "ctx", bit)
        first = side == 0
        return jnp.stack(
            [jnp.where(first, array, other), jnp.where(first, other, array)], axis=axis
        )

    total = halve(halve(parts, 1, 1, near), 0, 2, far)
    total = double(double(total, 0, 2, far), 1, 1, near)
    return total.reshape(value.shape).astype(F32)


def gather_tp(value):
    far = swap(value, "tp", 2)
    return [value, swap(value, "tp", 1), far, swap(far, "tp", 1)]


def add_low(left, right):
    return (left.astype(F32) + right.astype(F32)).astype(BF)


def near_sums(slots):
    return [add_low(slots[n], swap(slots[n + 1], "tp", 1)) for n in (0, 2)]


def far_sum(near, far):
    return near.astype(F32) + swap(far, "tp", 2).astype(F32)


def seq_steps(seqs):
    size = lax.axis_size("ctx")
    groups = size // seqs
    return [
        [(src, ((src % seqs + step) % seqs) * groups + src // seqs) for src in range(size)]
        for step in range(seqs)
    ]


def send(value, pairs):
    if all(src == dst for src, dst in pairs):
        return value
    return lax.ppermute(value, "ctx", pairs)


def to_sequence(value):
    seqs = value.shape[0]
    size = lax.axis_size("ctx")
    base = lax.axis_index("ctx") % seqs
    owner = lax.axis_index("ctx") // (size // seqs)
    out = jnp.zeros_like(value)
    for step, pairs in enumerate(seq_steps(seqs)):
        block = lax.dynamic_index_in_dim(value, (base + step) % seqs, 0, keepdims=True)
        place = (owner - step + seqs) % seqs
        out = lax.dynamic_update_slice_in_dim(out, send(block, pairs), place, 0)
    return out


def from_sequence(value):
    seqs = value.shape[0]
    size = lax.axis_size("ctx")
    base = lax.axis_index("ctx") % seqs
    owner = lax.axis_index("ctx") // (size // seqs)
    out = jnp.zeros_like(value)
    for step, pairs in enumerate(seq_steps(seqs)):
        block = lax.dynamic_index_in_dim(value, (owner - step + seqs) % seqs, 0, keepdims=True)
        block = send(block, [(dst, src) for src, dst in pairs])
        out = lax.dynamic_update_slice_in_dim(out, block, (base + step) % seqs, 0)
    return out


def lane_is_low(rows):
    return lax.broadcasted_iota(jnp.int32, (rows, LANES), 1) < LANES // 2


def pieces(dims):
    ranks, steps = dims
    return [(j * ranks + rank, j, rank) for j in range(steps) for rank in range(ranks)]


def allowed_block(seg_row, seg_col, q_axis, q_start, k_start, shape):
    q_at = q_start + lax.broadcasted_iota(jnp.int32, shape, q_axis)
    k_at = k_start + lax.broadcasted_iota(jnp.int32, shape, 1 - q_axis)
    return (seg_row == seg_col) & (k_at <= q_at)


def split_heads(tile, target, rows, low):
    head_pair = tile[:, :LANES]
    zero = jnp.zeros_like(head_pair)
    target[rows, 0:128] = jnp.where(low, head_pair, zero)
    target[rows, 128:256] = jnp.where(low, zero, head_pair)
    target[rows, 256:384] = tile[:, LANES:]


def attend_kernel(gathered, where_ref, low_ref, full_ref, seg_q_ref, seg_k_ref, proj_ref, *refs):
    kv_ref = refs[0] if gathered else None
    o_ref, lse_ref, qs, ks, vs = refs[1:] if gathered else refs
    ranks, steps, sub, _ = proj_ref.shape
    parts = kv_ref.shape[0] if gathered else 1
    tp_rank, part = where_ref[0], where_ref[1]
    q_len = ranks * steps * sub
    scale = 64 ** (-0.5)
    low = lane_is_low(sub)
    for block, j, rank in pieces((ranks, steps)):
        slot = tp_rank ^ rank
        rows = slice(block * sub, (block + 1) * sub)
        tile = (proj_ref[slot, j, :, :HEAD_PAD].astype(F32) * scale).astype(BF)
        split_heads(tile, qs, rows, low)
        for p in range(parts):
            at = slice(p * q_len + block * sub, p * q_len + (block + 1) * sub)
            both = kv_ref[p, slot, j] if gathered else proj_ref[slot, j, :, HEAD_PAD:]
            ks[at, :] = both[:, :HEAD_PAD]
            vs[at, :] = both[:, HEAD_PAD:]

    def q_block(i, _):
        q_row = pl.multiple_of(i * BQ, BQ)
        q_first = part * q_len + q_row
        seg_q = seg_q_ref[pl.ds(q_row, BQ), :]

        def step(masked, kk, carry):
            k_row = pl.multiple_of(kk * BK, BK)
            keys = ks[pl.ds(k_row, BK), :]
            vals = vs[pl.ds(k_row, BK), :]
            if masked:
                ok = allowed_block(seg_q, seg_k_ref[:, pl.ds(k_row, BK)], 0, q_first, k_row, (BQ, BK))
            out = []
            for h in range(3):
                top, total, acc = carry[h]
                lanes = slice((h // 2) * LANES, (h // 2 + 1) * LANES)
                scores = dot_nt(qs[pl.ds(q_row, BQ), h * LANES : (h + 1) * LANES], keys[:, lanes])
                if masked:
                    scores = jnp.where(ok, scores, NEG)
                new_top = jnp.maximum(top, jnp.max(scores, axis=1, keepdims=True))
                probs = jnp.exp(scores - new_top)
                shrink = jnp.exp(top - new_top)
                total = total * shrink + jnp.sum(probs, axis=1, keepdims=True)
                acc = acc * shrink + dot_nn(probs.astype(BF), vals[:, lanes])
                out.append((new_top, total, acc))
            return tuple(out)

        start = tuple(
            (jnp.full((BQ, 1), NEG, F32), jnp.zeros((BQ, 1), F32), jnp.zeros((BQ, LANES), F32))
            for _ in range(3)
        )
        first, full = low_ref[i], full_ref[i]
        last = q_first // BK
        carry = lax.fori_loop(first, full, functools.partial(step, True), start)
        carry = lax.fori_loop(full, last, functools.partial(step, False), carry)
        carry = lax.fori_loop(last, last + BQ // BK, functools.partial(step, True), carry)
        heads = [acc / total for _, total, acc in carry]
        pair = jnp.where(lane_is_low(BQ), heads[0], heads[1]).astype(BF)
        third = heads[2].astype(BF)
        for n in range(BQ // sub):
            block = i * (BQ // sub) + n
            slot, j = tp_rank ^ lax.rem(block, ranks), block // ranks
            o_ref[slot, j, :, 0:128] = pair[n * sub : (n + 1) * sub]
            o_ref[slot, j, :, 128:256] = third[n * sub : (n + 1) * sub]
        for h in range(3):
            top, total, _ = carry[h]
            column = jnp.broadcast_to(top + jnp.log(total), (BQ, LANES))
            lse_ref[i, h] = column.T[0:8]
        return 0

    lax.fori_loop(0, q_len // BQ, q_block, 0)


def attend_back_kernel(
    gathered, q_range, k_range, k_done, more, where_ref, full_ref, high_ref, seg_q_ref, seg_k_ref, o_ref, do_ref, lse_ref, proj_ref, *refs
):
    refs = list(refs)
    kv_ref = refs.pop(0) if gathered else None
    sum_ref = refs.pop(0) if more else None
    dproj_ref = refs.pop(0)
    dkv_ref = refs.pop(0) if gathered else None
    rest_ref = refs.pop(0) if k_done > k_range[0] else None
    qs, ks, vs, kt, dos, dqs, delta = refs
    ranks, steps, sub, _ = proj_ref.shape
    parts = kv_ref.shape[0] if gathered else 1
    tp_rank, part = where_ref[0], where_ref[1]
    q_len = ranks * steps * sub
    scale = 64 ** (-0.5)
    low = lane_is_low(sub)
    q_first, q_end = q_range
    per_q = BQ // sub

    for block, j, rank in pieces((ranks, steps)):
        slot = tp_rank ^ rank
        rows = slice(block * sub, (block + 1) * sub)
        if q_first * per_q <= block < q_end * per_q:
            split_heads((proj_ref[slot, j, :, :HEAD_PAD].astype(F32) * scale).astype(BF), qs, rows, low)
            grad = do_ref[slot, j]
            split_heads(grad, dos, rows, low)
            product = grad.astype(F32) * o_ref[slot, j].astype(F32)
            pair, third = product[:, :LANES].T, product[:, LANES:].T
            lanes = slice(rows.start % BQ, rows.start % BQ + sub)
            for h, part_of in enumerate((pair[:64], pair[64:], third[:64])):
                delta[block // per_q, h : h + 1, lanes] = jnp.sum(part_of, axis=0, keepdims=True)
        for p in range(parts):
            if not k_range[0] * BK <= p * q_len + block * sub < k_range[1] * BK:
                continue
            at = slice(p * q_len + block * sub, p * q_len + (block + 1) * sub)
            both = kv_ref[p, slot, j] if gathered else proj_ref[slot, j, :, HEAD_PAD:]
            ks[at, :] = both[:, :HEAD_PAD]
            vs[at, :] = both[:, HEAD_PAD:]
            kt[at.start // BK, :, at.start % BK : at.start % BK + sub] = both[:, :HEAD_PAD].T
    dqs[...] = jnp.zeros_like(dqs)

    def k_block(kk, _):
        k_row = pl.multiple_of(kk * BK, BK)
        keys = ks[pl.ds(k_row, BK), :]
        vals = vs[pl.ds(k_row, BK), :]
        seg_k = seg_k_ref[pl.ds(k_row, BK), :]

        def step(masked, i, carry):
            q_row = pl.multiple_of(i * BQ, BQ)
            at = pl.ds(q_row, BQ)
            if masked:
                ok = allowed_block(seg_q_ref[i], seg_k, 1, part * q_len + q_row, k_row, (BK, BQ))
            dk, dv = list(carry[0]), list(carry[1])
            for h in range(3):
                t = h // 2
                lanes = slice(t * LANES, (t + 1) * LANES)
                mine = slice(h * LANES, (h + 1) * LANES)
                q_head, do_head = qs[at, mine], dos[at, mine]
                scores = dot_nt(keys[:, lanes], q_head)
                probs = jnp.exp(scores - lse_ref[i, h, 0:1, :])
                if masked:
                    probs = jnp.where(ok, probs, 0.0)
                grad_probs = dot_nt(vals[:, lanes], do_head)
                grad_scores = (probs * (grad_probs - delta[i, h : h + 1, :])).astype(BF)
                dv[t] = dv[t] + dot_nn(probs.astype(BF), do_head)
                dk[t] = dk[t] + dot_nn(grad_scores, q_head)
                rows = slice(h * 64, (h + 1) * 64)
                dqs[i, rows, :] += dot_nn(kt[kk, rows, :], grad_scores)
            return tuple(dk), tuple(dv)

        zero = jnp.zeros((BK, LANES), F32)
        carry = ((zero, zero), (zero, zero))
        if more:
            pieces_in = [sum_ref[pl.ds(k_row, BK), t * LANES : (t + 1) * LANES] for t in range(4)]
            carry = (tuple(pieces_in[:2]), tuple(pieces_in[2:]))
        ahead = kk - part * (q_len // BQ)
        inside = lambda value: jnp.clip(value, q_first, q_end)
        first = inside(ahead)
        diagonal = jnp.where(ahead >= 0, inside(ahead + 1), first)
        full = jnp.maximum(inside(full_ref[kk]), diagonal)
        high = jnp.maximum(inside(high_ref[kk]), full)
        carry = lax.fori_loop(first, diagonal, functools.partial(step, True), carry)
        carry = lax.fori_loop(diagonal, full, functools.partial(step, False), carry)
        carry = lax.fori_loop(full, high, functools.partial(step, True), carry)
        return carry[0] + carry[1]

    def finish(kk, _):
        sums = k_block(kk, 0)
        for n in range(BK // sub):
            block = lax.rem(kk, q_len // BK) * (BK // sub) + n
            slot, j = tp_rank ^ lax.rem(block, ranks), block // ranks
            for t in range(4):
                piece = sums[t][n * sub : (n + 1) * sub].astype(BF)
                lanes = slice(t * LANES, (t + 1) * LANES)
                if gathered:
                    dkv_ref[kk // (q_len // BK), slot, j, :, lanes] = piece
                else:
                    start = HEAD_PAD + t * LANES
                    dproj_ref[slot, j - k_done * BK // (ranks * sub), :, start : start + LANES] = piece
        return 0

    def keep(kk, _):
        sums = k_block(kk, 0)
        for t in range(4):
            rest_ref[pl.ds(pl.multiple_of(kk * BK, BK), BK), t * LANES : (t + 1) * LANES] = sums[t]
        return 0

    if rest_ref is not None:
        lax.fori_loop(k_range[0], k_done, keep, 0)
    lax.fori_loop(k_done, k_range[1], finish, 0)
    for block, j, rank in pieces((ranks, steps)):
        if q_first * per_q <= block < q_end * per_q:
            lanes = slice(block % per_q * sub, (block % per_q + 1) * sub)
            grad = (dqs[block // per_q, :, lanes] * scale).T.astype(BF)
            dproj_ref[tp_rank ^ rank, j - q_first * per_q // ranks, :, :HEAD_PAD] = grad


SMEM = pl.BlockSpec(memory_space=pltpu.SMEM)
VMEM = pl.BlockSpec(memory_space=pltpu.VMEM)
PARAMS = pltpu.CompilerParams(vmem_limit_bytes=VMEM_BYTES)


def attend(where, seg_q, seg_k, proj, keyvals):
    ranks, steps, sub, _ = proj.shape
    gathered = keyvals is not None
    q_len = ranks * steps * sub
    k_len = q_len * (keyvals.shape[0] if gathered else 1)
    q_first, q_last = seg_q[::BQ], seg_q[BQ - 1 :: BQ]
    k_first, k_last = seg_k[::BK], seg_k[BK - 1 :: BK]
    k_index = jnp.arange(k_len // BK)
    bound = where[1] * (q_len // BK) + jnp.arange(q_len // BQ) * (BQ // BK)
    before = k_index[None, :] < bound[:, None]
    first = jnp.sum(before & (k_last[None, :] < q_first[:, None]), axis=1).astype(jnp.int32)
    full = jnp.sum(before & (k_first[None, :] != q_last[:, None]), axis=1).astype(jnp.int32)
    inputs = (proj, keyvals) if gathered else (proj,)
    return pl.pallas_call(
        functools.partial(attend_kernel, gathered),
        out_shape=(
            jax.ShapeDtypeStruct((ranks, steps, sub, HEAD_PAD), BF),
            jax.ShapeDtypeStruct((q_len // BQ, 3, 8, BQ), F32),
        ),
        in_specs=[SMEM] * 3 + [VMEM] * (2 + len(inputs)),
        out_specs=(VMEM, VMEM),
        scratch_shapes=[
            pltpu.VMEM((q_len, 3 * LANES), BF),
            pltpu.VMEM((k_len, HEAD_PAD), BF),
            pltpu.VMEM((k_len, HEAD_PAD), BF),
        ],
        compiler_params=PARAMS,
        cost_estimate=pl.CostEstimate(
            flops=16 * q_len * k_len * 256, bytes_accessed=8 * q_len * 1024, transcendentals=3 * q_len * k_len // 2
        ),
        name="attend",
    )(where, first, jnp.maximum(full, first), seg_q[:, None], seg_k[None, :], *inputs)


def attend_back(where, seg_q, seg_k, proj, keyvals, attended, grad, lse, q_range, k_range, k_done, before=None):
    ranks, steps, sub, _ = proj.shape
    gathered = keyvals is not None
    q_len = ranks * steps * sub
    k_len = q_len * (keyvals.shape[0] if gathered else 1)
    q_first, q_last = seg_q[::BQ], seg_q[BQ - 1 :: BQ]
    k_first, k_last = seg_k[::BK], seg_k[BK - 1 :: BK]
    full = jnp.sum(q_last[None, :] <= k_first[:, None], axis=1).astype(jnp.int32)
    high = jnp.sum(q_first[None, :] <= k_last[:, None], axis=1).astype(jnp.int32)
    inputs = [attended, grad, lse, proj] + ([keyvals] if gathered else []) + ([before] if before is not None else [])
    part_steps = (q_range[1] - q_range[0]) * BQ // (ranks * sub)
    outs = [jax.ShapeDtypeStruct((ranks, part_steps, sub, proj.shape[3] if not gathered else HEAD_PAD), BF)]
    if gathered:
        outs.append(jax.ShapeDtypeStruct(keyvals.shape, BF))
    if k_done > k_range[0]:
        outs.append(jax.ShapeDtypeStruct((k_done * BK, 2 * HEAD_PAD), F32))
    return pl.pallas_call(
        functools.partial(attend_back_kernel, gathered, q_range, k_range, k_done, before is not None),
        out_shape=outs,
        in_specs=[SMEM] * 3 + [VMEM] * (2 + len(inputs)),
        out_specs=[VMEM] * len(outs),
        scratch_shapes=[
            pltpu.VMEM((q_len, 3 * LANES), BF),
            pltpu.VMEM((k_len, HEAD_PAD), BF),
            pltpu.VMEM((k_len, HEAD_PAD), BF),
            pltpu.VMEM((k_len // BK, HEAD_PAD, BK), BF),
            pltpu.VMEM((q_len, 3 * LANES), BF),
            pltpu.VMEM((q_len // BQ, HEAD_PAD, BQ), F32),
            pltpu.VMEM((q_len // BQ, 8, BQ), F32),
        ],
        compiler_params=PARAMS,
        cost_estimate=pl.CostEstimate(
            flops=12 * q_len * k_len * 256, bytes_accessed=16 * q_len * 1024, transcendentals=3 * q_len * k_len // 2
        ),
        name=f"attend_back_{q_range[0]}_{q_range[1]}",
    )(where, full, high, seg_q.reshape(-1, 1, BQ), seg_k[:, None], *inputs)


GELU_A, GELU_B = 0.7978845608028654, 0.044715
ORDER = (0, 2, 1, 3)


def row_mean(values):
    return jnp.mean(values, axis=-1, keepdims=True)


def middle_kernel(
    head_width, x_ref, m0, m1, m2, m3, cot_ref, vec_ref, up0, up1, up2, up3, down_even, down_odd,
    out_ref, gh_ref, do_ref, up_even_ref, up_odd_ref, down_even_ref, down_odd_ref, wout_even_ref, wout_odd_ref, small_ref,
    wu, wd, xhat, rstd, n2, act, gpre, mlp, dn2,
):
    at = pl.program_id(0)
    tokens, width = x_ref.shape
    units = wd.shape[0]
    chunk = 256
    merged = (m0, m1, m2, m3)
    ups = (up0, up1, up2, up3)
    downs = ((down_even, 0), (down_odd, 0), (down_even, 1), (down_odd, 1))
    bias_row = up0.shape[0] - 16

    @pl.when(at == 0)
    def _():
        gain, shift = vec_ref[0:1, :], vec_ref[1:2, :]
        for t in range(tokens // chunk):
            rows = slice(t * chunk, (t + 1) * chunk)
            hidden = x_ref[rows, :].astype(F32) + vec_ref[2:3, :]
            for s in range(4):
                hidden = hidden + dot_nn(merged[s][rows, :head_width], ups[s][units : units + head_width, :])
            center = hidden - row_mean(hidden)
            scale = lax.rsqrt(row_mean(center * center) + EPS)
            norm = center * scale
            xhat[rows, :] = norm
            rstd[rows, :] = jnp.broadcast_to(scale, (chunk, LANES))
            n2[rows, :] = (norm * gain + shift).astype(BF)
            mlp[rows, :] = hidden + vec_ref[3:4, :]
        dn2[...] = jnp.zeros_like(dn2)
        small_ref[...] = jnp.zeros_like(small_ref)

    for n, s in enumerate(ORDER):

        @pl.when(at == n)
        def _():
            wu[...] = ups[s][...]
            wd[...] = downs[s][0][downs[s][1]]

    slot = (at % 2) * 2 + at // 2
    bias = wu[bias_row : bias_row + 16, :][0:1].astype(F32)

    def tokens_step(t, total):
        rows = pl.ds(pl.multiple_of(t * chunk, chunk), chunk)
        pre = dot_nn(n2[rows, :], wu[:units, :]) + bias
        square = pre * pre
        tanh = jnp.tanh(GELU_A * pre * (1.0 + GELU_B * square))
        half = 0.5 * (1.0 + tanh)
        activ = (pre * half).astype(BF)
        act[rows, :] = activ
        mlp[rows, :] += dot_nn(activ, wd[...])
        slope = half + (0.5 * GELU_A) * pre * (1.0 - tanh * tanh) * (1.0 + (3.0 * GELU_B) * square)
        grad = (dot_nt(cot_ref[rows, :], wd[...]) * slope).astype(BF)
        gpre[rows, :] = grad
        dn2[rows, :] += dot_nt(grad, wu[:units, :])
        return total + jnp.sum(grad.astype(F32), axis=0, keepdims=True)

    total = lax.fori_loop(0, tokens // chunk, tokens_step, jnp.zeros((1, units), F32))
    for s in range(4):

        @pl.when(slot == s)
        def _():
            small_ref[4 + s : 5 + s, :] = total

    def weight_grads(up_out, down_out):
        for c in range(units // chunk):
            rows = slice(c * chunk, (c + 1) * chunk)
            down_out[0, rows, :] = dot_tn(act[:, rows], cot_ref[...]).astype(BF)
        for c in range(width // chunk):
            rows = slice(c * chunk, (c + 1) * chunk)
            up_out[0, rows, :] = dot_tn(n2[:, rows], gpre[...]).astype(BF)

    @pl.when(at < 2)
    def _():
        weight_grads(up_even_ref, down_even_ref)

    @pl.when(at >= 2)
    def _():
        weight_grads(up_odd_ref, down_odd_ref)

    @pl.when(at == 3)
    def _():
        gain = vec_ref[0:1, :]
        for t in range(tokens // chunk):
            rows = slice(t * chunk, (t + 1) * chunk)
            out_ref[rows, :] = mlp[rows, :].astype(BF)
            grad, norm, cot = dn2[rows, :], xhat[rows, :], cot_ref[rows, :].astype(F32)
            gg = grad * gain
            inner = gg - row_mean(gg) - norm * row_mean(gg * norm)
            hidden = cot + rstd[rows, 0:1] * inner
            gh_ref[rows, :] = hidden
            small_ref[0:1, :] += jnp.sum(grad * norm, axis=0, keepdims=True)
            small_ref[1:2, :] += jnp.sum(grad, axis=0, keepdims=True)
            small_ref[2:3, :] += jnp.sum(hidden, axis=0, keepdims=True)
            small_ref[3:4, :] += jnp.sum(cot, axis=0, keepdims=True)
            branch = hidden.astype(BF)
            gpre[rows, :width] = branch
            for s in range(4):
                back = dot_nt(branch, ups[s][units : units + head_width, :]).astype(BF)
                do_ref[s, rows, :head_width] = back
                do_ref[s, rows, head_width:] = jnp.zeros((chunk, HEAD_PAD - head_width), BF)
        for s in range(4):
            target = (wout_even_ref, wout_odd_ref)[s % 2]
            target[s // 2] = dot_tn(merged[s][...], gpre[:, :width])[:head_width].astype(BF)


def middle(head_width, x_rows, merged, cot_rows, vectors, ups, down_even, down_odd):
    tokens, width = x_rows.shape
    units = down_even.shape[1]
    whole = lambda shape: pl.BlockSpec(shape, lambda at: (0,) * len(shape))
    early = lambda at: (jnp.minimum(at, 1), 0, 0)
    late = lambda at: (jnp.maximum(at - 2, 0), 0, 0)
    once = lambda value: pl.BlockSpec(value.shape, lambda at: (0,) * value.ndim, pipeline_mode=pl.Buffered(1))
    struct = jax.ShapeDtypeStruct
    return pl.pallas_call(
        functools.partial(middle_kernel, head_width),
        grid=(4,),
        out_shape=(
            struct((tokens, width), BF),
            struct((tokens, width), F32),
            struct((4, tokens, HEAD_PAD), BF),
            struct((2, width, units), BF),
            struct((2, width, units), BF),
            struct((2, units, width), BF),
            struct((2, units, width), BF),
            struct((2, head_width, width), BF),
            struct((2, head_width, width), BF),
            struct((8, width), F32),
        ),
        in_specs=[whole((tokens, width))]
        + [whole((tokens, HEAD_PAD))] * 4
        + [whole((tokens, width)), whole(vectors.shape)]
        + [once(value) for value in (*ups, down_even, down_odd)],
        out_specs=(
            whole((tokens, width)),
            whole((tokens, width)),
            whole((4, tokens, HEAD_PAD)),
            pl.BlockSpec((1, width, units), early),
            pl.BlockSpec((1, width, units), late),
            pl.BlockSpec((1, units, width), early),
            pl.BlockSpec((1, units, width), late),
            whole((2, head_width, width)),
            whole((2, head_width, width)),
            whole((8, width)),
        ),
        scratch_shapes=[
            pltpu.VMEM(ups[0].shape, BF),
            pltpu.VMEM((units, width), BF),
            pltpu.VMEM((tokens, width), F32),
            pltpu.VMEM((tokens, LANES), F32),
            pltpu.VMEM((tokens, width), BF),
            pltpu.VMEM((tokens, units), BF),
            pltpu.VMEM((tokens, units), BF),
            pltpu.VMEM((tokens, width), F32),
            pltpu.VMEM((tokens, width), F32),
        ],
        compiler_params=PARAMS,
        cost_estimate=pl.CostEstimate(
            flops=60 * tokens * width * units, bytes_accessed=12 * units * width, transcendentals=4 * tokens * units
        ),
        name="middle",
    )(x_rows, *merged, cot_rows, vectors, *ups, down_even, down_odd)


def norm_parts(values):
    center = values - row_mean(values)
    rstd = lax.rsqrt(row_mean(center * center) + EPS)
    return center * rstd, rstd


def norm_back(xhat, rstd, gain, grad):
    gg = grad * gain
    return rstd * (gg - row_mean(gg) - xhat * row_mean(gg * xhat))


def pick(array, index, axis):
    return lax.dynamic_index_in_dim(array, index, axis, keepdims=False)


def on_device(
    block_in, segments, ln1_gain, ln1_shift, w_qkv, b_qv, w_out, b_out, ln2_gain, ln2_shift, w_up, b_up, w_down, b_down, cotangent
):
    seqs, sub, width = block_in.shape
    ranks, fsdp, ctx_size = lax.axis_size("tp"), lax.axis_size("fsdp"), lax.axis_size("ctx")
    parts = ctx_size // seqs
    tp_rank, ctx_rank, fsdp_rank = lax.axis_index("tp"), lax.axis_index("ctx"), lax.axis_index("fsdp")
    heads = b_qv.shape[0]
    head_width = heads * 64
    own = seqs * sub
    tokens = ranks * own
    shard = ln1_gain.shape[0]

    x_blocks = to_sequence(block_in)
    down_far = swap(w_down, "tp", 2)
    x_blocks, down_far = lax.optimization_barrier((x_blocks, down_far))
    x_own = x_blocks.reshape(own, width)

    vectors = [ln1_gain, ln1_shift, b_out, ln2_gain, ln2_shift, b_down, b_qv.reshape(-1), b_up.reshape(-1)]
    rows = jnp.stack([jnp.pad(v, (0, shard - v.shape[0])) for v in vectors])
    (small,) = gather_fsdp([rows[None]], 0)
    (qkv_mat,) = gather_fsdp([w_qkv], 1)
    gain_one, shift_one, out_bias, gain_two, shift_two, down_bias = (
        small[:, n].reshape(-1).astype(F32) for n in range(6)
    )
    qv_bias = small[:, 6, : b_qv.size].reshape((fsdp,) + b_qv.shape)
    qv_bias = qv_bias.transpose(1, 0, 2).reshape(heads, -1).astype(F32)
    up_bias = small[:, 7, : b_up.size].reshape((fsdp,) + b_up.shape).transpose(1, 0, 2).reshape(1, -1)
    extra = HEAD_PAD - head_width
    qkv_pad = jnp.pad(qkv_mat, ((0, 0), (0, extra), (0, 0))).reshape(3 * HEAD_PAD, width)
    bias_rows = jnp.stack(
        [qv_bias[:, :64].reshape(-1), jnp.zeros((head_width,), F32), qv_bias[:, 64:].reshape(-1)]
    )
    qkv_bias = jnp.pad(bias_rows, ((0, 0), (0, extra))).reshape(-1)

    up_rows, out_rows = gather_fsdp([w_up, w_out], 0)
    up_own = jnp.concatenate([up_rows, out_rows, jnp.pad(up_bias, ((0, 15), (0, 0)))], axis=0)
    down_pair = jnp.stack([w_down, down_far])

    x_float = x_own.astype(F32)
    xhat_one, rstd_one = norm_parts(x_float)
    normed_own = (xhat_one * gain_one + shift_one).astype(BF)
    normed_own, cotangent = lax.optimization_barrier((normed_own, cotangent))
    cot_rows = to_sequence(cotangent)
    normed_one = jnp.concatenate(gather_tp(normed_own), axis=0)
    normed_one, up_own, down_pair, cot_rows = lax.optimization_barrier(
        (normed_one, up_own, down_pair, cot_rows)
    )
    cot_rows = cot_rows.reshape(own, width)
    proj = (dot_nt(normed_one, qkv_pad) + qkv_bias).astype(BF).reshape(ranks, seqs, sub, 3 * HEAD_PAD)
    up_side = swap(up_own, "tp", 1)
    keyvals = None
    groups = [[g * parts + p for p in range(parts)] for g in range(ctx_size // parts)]
    if parts > 1:
        keyvals = lax.all_gather(
            proj[None, ..., HEAD_PAD:], "ctx", axis=0, tiled=True, axis_index_groups=groups
        )
    seq_rank, part = ctx_rank // parts, ctx_rank % parts
    where = jnp.stack([tp_rank, part]).astype(jnp.int32)
    seg_k = pick(segments, seq_rank, 0)
    seg_q = lax.dynamic_slice_in_dim(seg_k, part * tokens, tokens, 0)
    attended, lse = attend(where, seg_q, seg_k, proj, keyvals)

    up_far = swap(up_own, "tp", 2)
    (down_even,) = gather_fsdp([down_pair], 1)
    attended, up_far, up_side, down_even = lax.optimization_barrier(
        (attended, up_far, up_side, down_even)
    )
    ups = [up_own, up_side, up_far, swap(up_far, "tp", 1)]
    down_odd = swap(down_even, "tp", 1)

    slots = attended.reshape(ranks, own, HEAD_PAD)
    merged = [slots[0]] + [swap(slots[s], "tp", s) for s in range(1, ranks)]
    vecs = jnp.stack([gain_two, shift_two, out_bias, down_bias])
    vecs = jnp.pad(vecs, ((0, 4), (0, 0)))
    (
        block_out, grad_hidden, grad_slots, up_even, up_odd, down_even_g, down_odd_g, out_even, out_odd, sums,
    ) = middle(head_width, x_own, merged, cot_rows, vecs, ups, down_even, down_odd)
    grad_slots = [grad_slots[0]] + [swap(grad_slots[s], "tp", s) for s in range(1, ranks)]
    grad_attended = jnp.stack(grad_slots).reshape(ranks, seqs, sub, HEAD_PAD)

    up_near = add_low(up_even, swap(up_odd, "tp", 1))
    down_near = add_low(down_even_g, swap(down_odd_g, "tp", 1))
    grad_attended, up_near, down_near, block_out, out_even, out_odd = lax.optimization_barrier(
        (grad_attended, up_near, down_near, block_out, out_even, out_odd)
    )
    out_blocks = from_sequence(block_out.reshape(seqs, sub, width))

    up_mid = add_low(up_near[0], swap(up_near[1], "tp", 2))
    down_mid = scatter_fsdp(down_near.reshape(2, fsdp, -1, width).transpose(1, 0, 2, 3))

    q_blocks = tokens // BQ
    back = functools.partial(attend_back, where, seg_q, seg_k, proj, keyvals, attended)
    if parts > 1:
        dq, dkv = back(grad_attended, lse, (0, q_blocks), (0, parts * q_blocks), 0)
        dkv = lax.psum_scatter(
            dkv, "ctx", scatter_dimension=0, tiled=True, axis_index_groups=groups
        )
        halves = [jnp.concatenate([dq, dkv.reshape(ranks, seqs, sub, 2 * HEAD_PAD)], axis=-1)]
        edges = [0, seqs]
    else:
        mid = q_blocks // 2
        high, rest = back(grad_attended, lse, (mid, q_blocks), (0, q_blocks), mid)
        rest, high, up_mid, down_mid, out_even, out_odd, out_blocks = lax.optimization_barrier(
            (rest, high, up_mid, down_mid, out_even, out_odd, out_blocks)
        )
        (low,) = back(grad_attended, lse, (0, mid), (0, mid), 0, rest)
        halves = [low, high]
        edges = [0, mid * BQ // (ranks * sub), seqs]

    up_last = scatter_fsdp(up_mid.reshape(fsdp, -1, up_mid.shape[1]))
    down_last = add_low(down_mid[0], swap(down_mid[1], "tp", 2))
    out_near = add_low(out_even, swap(out_odd, "tp", 1))
    grad_rows = [None] * len(halves)

    def back_rows(half):
        rows = dot_nn(half.reshape(-1, 3 * HEAD_PAD), qkv_pad).astype(BF).reshape(ranks, -1, width)
        return near_sums([rows[s] for s in range(ranks)])

    if parts == 1:
        grad_rows[1] = back_rows(halves[1])
        halves[0], grad_rows[1], up_last, down_last, out_near = lax.optimization_barrier(
            (halves[0], grad_rows[1], up_last, down_last, out_near)
        )
    grad_rows[0] = back_rows(halves[0])
    out_mid = add_low(out_near[0], swap(out_near[1], "tp", 2))
    total = sum_ctx(jnp.concatenate([up_last, down_last], axis=0))
    sum_up, sum_down = total[: w_up.shape[0]], total[w_up.shape[0] :]

    normed_all = normed_one.reshape(ranks, seqs, sub, width)
    grad_qkv, grad_normed, bias_sum = 0.0, [], 0.0
    for n in reversed(range(len(halves))):
        rows = halves[n].reshape(-1, 3 * HEAD_PAD)
        grad_normed.insert(0, far_sum(*grad_rows[n]))
        seen = normed_all[:, edges[n] : edges[n + 1]].reshape(-1, width)
        grad_qkv = grad_qkv + dot_tn(rows, seen)
        bias_sum = bias_sum + jnp.sum(rows.astype(F32), axis=0)
    grad_normed_one = jnp.concatenate(grad_normed, axis=0)
    grad_x = grad_hidden + norm_back(xhat_one, rstd_one, gain_one, grad_normed_one)
    grad_blocks = from_sequence(grad_x.astype(BF).reshape(seqs, sub, width))

    grad_qkv = grad_qkv.reshape(3, HEAD_PAD, width)[:, :head_width].astype(BF)
    both = jnp.concatenate([grad_qkv, out_mid[None]]).reshape(4, fsdp, -1, width).transpose(1, 0, 2, 3)
    total = sum_ctx(scatter_fsdp(both).reshape(-1, width))
    sum_qkv, sum_out = total[: -w_out.shape[0]].reshape(w_qkv.shape), total[-w_out.shape[0] :]

    bias_sum = bias_sum.reshape(3, HEAD_PAD)[:, :head_width].reshape(3, heads, 64)
    bias_rows = jnp.concatenate([bias_sum[0], bias_sum[2]], axis=1)
    bias_all = lax.dynamic_update_slice(
        jnp.zeros((ranks * heads, 128), F32), bias_rows, (tp_rank * heads, 0)
    )
    up_bias_all = jnp.zeros((ranks, width), F32)
    for s in range(ranks):
        up_bias_all = lax.dynamic_update_slice(up_bias_all, sums[4 + s : 5 + s], (tp_rank ^ s, 0))
    ln1_sums = jnp.stack([jnp.sum(grad_normed_one * xhat_one, axis=0), jnp.sum(grad_normed_one, axis=0)])
    late = jnp.concatenate(
        [sums[:4].reshape(-1, LANES), up_bias_all.reshape(-1, LANES), ln1_sums.reshape(-1, LANES), bias_all]
    )
    for axis in ("tp", "ctx", "fsdp"):
        late = butterfly(late, axis)
    late_rows = late[: 10 * width // LANES].reshape(10, fsdp, shard)

    def mine_bias(rows, like):
        rows = lax.dynamic_slice_in_dim(rows, tp_rank * like.shape[0], like.shape[0], 0)
        return lax.dynamic_slice_in_dim(rows, fsdp_rank * like.shape[1], like.shape[1], 1)

    vector_sums = pick(late_rows, fsdp_rank, 1)
    sum_qv_bias = mine_bias(late[10 * width // LANES :], b_qv)
    up_bias_rows = late[4 * width // LANES : 8 * width // LANES]
    sum_up_bias = mine_bias(up_bias_rows.reshape(ranks * b_up.shape[0], -1), b_up)
    return (
        out_blocks, grad_blocks, vector_sums[8], vector_sums[9], sum_qkv, sum_qv_bias, sum_out, vector_sums[2],
        vector_sums[0], vector_sums[1], sum_up, sum_up_bias, sum_down, vector_sums[3],
    )


def solution(mesh):
    rows = P("fsdp", ("ctx", "tp"), None)
    vector = P("fsdp")
    out_rows = P(("tp", "fsdp"), None)
    qkv_rows = P(None, ("tp", "fsdp"), None)
    bias = P("tp", "fsdp")
    weights = (
        vector, vector, qkv_rows, bias, out_rows, vector, vector, vector, P("fsdp", "tp"), bias, out_rows, vector,
    )
    return jax.shard_map(
        on_device,
        mesh=mesh,
        in_specs=(rows, P("fsdp", None)) + weights + (rows,),
        out_specs=(rows, rows) + weights,
        check_vma=False,
    )
```

time: 567 us -> 357 us (0.63)
  starting transfers between devices: 144 us -> 52.7 us
  waiting for transfers between devices: 193 us -> 112 us
  matrix products: 68.3 us -> 11.7 us
  Pallas kernels: 44.8 us -> 96.2 us
  blocking collectives: 44.5 us -> 0 us
  other arithmetic: 26.9 us -> 36.6 us
    pallas_call x2 -> x4, Pallas kernels: 44.8 us -> 96.2 us  [the longest x2 37.8 us: attend_back(): pl.pallas_call(functools.partial(attend_back_kernel, gathered, q_range, k...]
    ppermute x61 -> x48, starting transfers between devices: 86.6 us -> 38.6 us  [swap(): return lax.ppermute(value, axis, [(i, i ^ bit) for i in range(size)])]
    psum x1 -> x0, blocking collectives: 44.5 us -> none  [on_device(): early = lax.psum(early, ('fsdp', 'ctx', 'tp')).reshape(-1)]
    ppermute x61 -> x48, waiting for transfers between devices: 152 us -> 111 us  [swap(): return lax.ppermute(value, axis, [(i, i ^ bit) for i in range(size)])]
    ppermute x12 -> x0, starting transfers between devices: 23 us -> none  [sum_ctx(): lax.ppermute(part(rank ^ s), 'ctx', [(i, i ^ s) for i in range(size)])]
    ppermute x12, waiting for transfers between devices: 21.7 us -> 0.17 us  [send(): return lax.ppermute(value, 'ctx', pairs)]
    dot_general x11 -> x1, matrix products: 23.9 us -> 2.86 us  [dot_nt(): lax.dot_general(left, right, (((1,), (1,)), ((), ())), preferred_element_...]
    ppermute x12, starting transfers between devices: 34.4 us -> 14.1 us  [send(): return lax.ppermute(value, 'ctx', pairs)]
  transfers between devices with their start and end apart: 85 -> 60, of which waited for: 32 -> 22; matrix products, arithmetic and copies ran while one was open for 21% -> 20% of each run, Pallas kernels for 8% -> 15%
where the time goes in v2:
time: 357 us; the launch traced here: 352 us
  waiting for transfers between devices  112 us (31%)
  Pallas kernels  96.2 us (27%)
  starting transfers between devices  52.7 us (15%)
  local copies, waits for them, and re-layouts  41 us (11%)
  other arithmetic  36.6 us (10%)
  matrix products  11.7 us (3%)
    ppermute x48, waiting for transfers between devices, swap(): return lax.ppermute(value, axis, [(i, i ^ bit) for i in range(size)])  111 us
    ppermute x48, starting transfers between devices, swap(): return lax.ppermute(value, axis, [(i, i ^ bit) for i in range(size)])  38.6 us
    pallas_call x2, Pallas kernels, attend_back(): pl.pallas_call(functools.partial(attend_back_kernel, gathered, q_range, k...  37.8 us
    pallas_call x1, Pallas kernels, middle(): pl.pallas_call(functools.partial(middle_kernel, head_width), grid=(4,), o...  31.3 us
    pallas_call x1, Pallas kernels, attend(): pl.pallas_call(functools.partial(attend_kernel, gathered), out_shape=(jax...  27.1 us
    ppermute x12, starting transfers between devices, send(): return lax.ppermute(value, 'ctx', pairs)  14.1 us
    convert_element_type x8, other arithmetic, add_low(): return (left.astype(F32) + right.astype(F32)).astype(BF)  9.87 us
  transfers between devices with their start and end apart: 60, of which 22 were waited for; matrix products, arithmetic and copies ran while one was open for 20% of the time, Pallas kernels for 15%

profile of v2, /device:TPU:0, one launch (start us, length us, event | category | flops | bytes accessed | tf_op | source)
XLA Modules:
  0.0 352.0 jit_solution(13029527347437616697)
XLA Ops:
  6.9 3.0 collective-permute-start.4
  10.0 2.1 constant_dynamic-slice_fusion.15
  12.0 1.6 collective-permute-start
  13.6 2.6 collective-permute-start.1
  16.2 1.3 collective-permute-start.2
  17.5 1.5 collective-permute-start.3
  25.2 1.3 stack_reshape.7
  26.5 1.3 stack_reshape.6
  29.2 1.3 reshape.385
  31.2 2.1 fusion.40
  34.6 1.5 collective-permute-start.8
  38.0 1.2 broadcast_select_fusion.3
  42.7 1.4 pad_maximum_fusion.3
  44.1 7.0 %collective-permute-done.8 = bf16[480,768]{1,0:T(8,128)(2,1)S(1)} collective-permute-done((bf16[480,768]{1,0:T(8,128)(2,1)S(1)}, bf16[480,768]{1,0:T(8,128)(2,1)S(1)}, u32[]{:S(2)}, u32[]{:S(2)}) %collective-permute-start.8) | collective-permute-done | bytes 737312 | tf_op jit(solution)/shard_map/ppermute | solution.py:35
  53.7 4.6 %collective-permute-done.6 = bf16[512,768]{1,0:T(8,128)(2,1)S(1)} collective-permute-done((bf16[512,768]{1,0:T(8,128)(2,1)S(1)}, bf16[512,768]{1,0:T(8,128)(2,1)S(1)}, u32[]{:S(2)}, u32[]{:S(2)}) %collective-permute-start.6) | collective-permute-done | bytes 786464 | tf_op jit(solution)/shard_map/ppermute | solution.py:35
  61.7 1.4 collective-permute-start.15
  63.1 2.9 add_convert_fusion
  66.0 27.1 %attend.1 = (bf16[4,4,128,256]{3,2,1,0:T(8,128)(2,1)S(1)}, f32[4,3,8,512]{3,2,1,0:T(8,128)S(1)}) custom-call(s32[2]{0:T(128)S(1)} %pad_add_fusion.where_ref, s32[4]{0:T(128)S(1)} %get-tuple-element.117.low_ref, s32[4]{0:T(128)S(1)} %max.3.full_ref, s32[2048,1]{1,0:T(8,128)S(1)} %copy.57.seg_q_ref.seg_k_ref, ...), custom_call_target="tpu_custom_call" | custom-call | flops 17179869184 | bytes 16777216 | tf_op jit(solution)/shard_map/attend/pallas_call | solution.py:391
  94.0 2.4 collective-permute-done.13.up2
  97.7 1.3 collective-permute-start.18
  99.0 4.5 %collective-permute-done.16.m1 = bf16[512,256]{1,0:T(8,128)(2,1)S(1)} collective-permute-done((bf16[512,256]{1,0:T(8,128)(2,1)S(1)}, bf16[512,256]{1,0:T(8,128)(2,1)S(1)}, u32[]{:S(2)}, u32[]{:S(2)}) %collective-permute-start.16) | collective-permute-done | bytes 262176 | tf_op jit(solution)/shard_map/ppermute | solution.py:35
  103.5 2.8 collective-permute-done.17.m2
  106.3 4.7 %collective-permute-done.18.m3 = bf16[512,256]{1,0:T(8,128)(2,1)S(1)} collective-permute-done((bf16[512,256]{1,0:T(8,128)(2,1)S(1)}, bf16[512,256]{1,0:T(8,128)(2,1)S(1)}, u32[]{:S(2)}, u32[]{:S(2)}) %collective-permute-start.18) | collective-permute-done | bytes 262176 | tf_op jit(solution)/shard_map/ppermute | solution.py:35
  112.9 31.3 %middle.1 = (bf16[512,768]{1,0:T(8,128)(2,1)S(1)}, f32[512,768]{1,0:T(8,128)}, bf16[4,512,256]{2,1,0:T(8,128)(2,1)S(1)}, bf16[2,768,768]{2,1,0:T(8,128)(2,1)}, b...) custom-call(bf16[512,768]{1,0:T(8,128)(2,1)S(1)} %bitcast.156, ...), custom_call_target="tpu_custom_call" | custom-call | flops 18119393280 | bytes 7077888 | tf_op jit(solution)/shard_map/middle/pallas_call | solution.py:572
  146.2 1.5 collective-permute-start.22
  149.3 5.0 %collective-permute-done.23 = bf16[512,256]{1,0:T(8,128)(2,1)} collective-permute-done((bf16[512,256]{1,0:T(8,128)(2,1)}, bf16[512,256]{1,0:T(8,128)(2,1)}, u32[]{:S(2)}, u32[]{:S(2)}) %collective-permute-start.23) | collective-permute-done | bytes 262176 | tf_op jit(solution)/shard_map/ppermute | solution.py:35
  154.3 6.0 %collective-permute-done.22 = bf16[512,256]{1,0:T(8,128)(2,1)} collective-permute-done((bf16[512,256]{1,0:T(8,128)(2,1)}, bf16[512,256]{1,0:T(8,128)(2,1)}, u32[]{:S(2)}, u32[]{:S(2)}) %collective-permute-start.22) | collective-permute-done | bytes 262176 | tf_op jit(solution)/shard_map/ppermute | solution.py:35
  160.3 1.2 pad_maximum_fusion.5.do_ref
  161.6 3.1 add_convert_fusion.2
  164.7 2.2 add_convert_fusion.1
  169.1 2.9 collective-permute-start.28
  172.0 1.8 collective-permute-start.29
  173.8 24.4 %attend_back_2_4.1 = (bf16[4,2,128,768]{3,2,1,0:T(8,128)(2,1)S(1)}, f32[1024,512]{1,0:T(8,128)}) custom-call(s32[2]{0:T(128)S(1)} %pad_add_fusion.where_ref, s32[4]{0:T(128)S(1)} %get-tuple-element.119.full_ref, s32[4]{0:T(128)S(1)} %get-tuple-element.118.high_ref, s32[4,1,512]{2,1,0:T(1,128)S(1)} %bitcast.164, s32[2048,1]{1,0:T(8,128)S(1)} %copy.57.seg_q_ref.seg_k_ref, ...), custom_call_target="tpu_custom_call" | custom-call | flops 12884901888 | bytes 33554432 | tf_op jit(solution)/shard_map/attend_back_2_4/pallas_call | solution.py:428
  199.5 13.4 %attend_back_0_2.1 = bf16[4,2,128,768]{3,2,1,0:T(8,128)(2,1)S(1)} custom-call(s32[2]{0:T(128)S(1)} %pad_add_fusion.where_ref, s32[4]{0:T(128)S(1)} %get-tuple-element.119.full_ref, s32[4]{0:T(128)S(1)} %get-tuple-element.118.high_ref, s32[4,1,512]{2,1,0:T(1,128)S(1)} %bitcast.165, s32[2048,1]{1,0:T(8,128)S(1)} %copy.57.seg_q_ref.seg_k_ref, ...), custom_call_target="tpu_custom_call" | custom-call | flops 12884901888 | bytes 33554432 | tf_op jit(solution)/shard_map/attend_back_0_2/pallas_call | solution.py:428
  212.9 1.4 convolution_convert_fusion.1
  215.0 1.6 collective-permute-start.33
  218.7 11.7 %collective-permute-done.33 = bf16[384,768]{1,0:T(8,128)(2,1)S(1)} collective-permute-done((bf16[384,768]{1,0:T(8,128)(2,1)S(1)}, bf16[384,768]{1,0:T(8,128)(2,1)S(1)}, u32[]{:S(2)}, u32[]{:S(2)}) %collective-permute-start.33) | collective-permute-done | bytes 589856 | tf_op jit(solution)/shard_map/ppermute | solution.py:35
  233.7 1.4 convolution_convert_fusion
  237.8 3.5 fusion.12
  241.3 2.5 fusion.2
  244.6 1.5 collective-permute-start.50
  246.4 1.6 slice.307
  249.1 4.8 %collective-permute-done.50 = bf16[192,768]{1,0:T(8,128)(2,1)} collective-permute-done((bf16[192,768]{1,0:T(8,128)(2,1)}, bf16[192,768]{1,0:T(8,128)(2,1)}, u32[]{:S(2)}, u32[]{:S(2)}) %collective-permute-start.50) | collective-permute-done | bytes 294944 | tf_op jit(solution)/shard_map/ppermute | solution.py:35
  258.7 1.6 collective-permute-start.38
  261.4 2.8 collective-permute-done.56
  264.2 1.2 fusion.16
  266.2 1.5 collective-permute-start.57
  271.3 1.6 collective-permute-start.44
  273.5 2.0 add_convert_fusion.3
  276.2 1.5 collective-permute-start.47
  277.8 2.0 collective-permute-start.46
  279.8 1.2 fusion.17
  281.3 2.6 collective-permute-done.47
  283.9 1.8 collective-permute-start.40
  286.3 9.0 %collective-permute-done.52 = bf16[2,96,768]{2,1,0:T(8,128)(2,1)S(1)} collective-permute-done((bf16[2,96,768]{2,1,0:T(8,128)(2,1)S(1)}, bf16[2,96,768]{2,1,0:T(8,128)(2,1)S(1)}, u32[]{:S(2)}, u32[]{:S(2)}) %collective-permute-start.52) | collective-permute-done | bytes 294944 | tf_op jit(solution)/shard_map/ppermute | solution.py:35
  296.4 2.7 collective-permute-start.53
  300.1 2.0 collective-permute-start.58
  304.1 11.6 %collective-permute-done.53 = bf16[96,768]{1,0:T(8,128)(2,1)S(1)} collective-permute-done((bf16[96,768]{1,0:T(8,128)(2,1)S(1)}, bf16[96,768]{1,0:T(8,128)(2,1)S(1)}, u32[]{:S(2)}, u32[]{:S(2)}) %collective-permute-start.53) | collective-permute-done | bytes 147488 | tf_op jit(solution)/shard_map/ppermute | solution.py:35
  315.8 9.4 %collective-permute-done.58 = bf16[192,768]{1,0:T(8,128)(2,1)S(1)} collective-permute-done((bf16[192,768]{1,0:T(8,128)(2,1)S(1)}, bf16[192,768]{1,0:T(8,128)(2,1)S(1)}, u32[]{:S(2)}, u32[]{:S(2)}) %collective-permute-start.58) | collective-permute-done | bytes 294944 | tf_op jit(solution)/shard_map/ppermute | solution.py:35
  325.2 3.0 collective-permute-done.54
  328.4 2.1 collective-permute-start.59
  330.6 7.6 %collective-permute-done.55 = bf16[2,96,768]{2,1,0:T(8,128)(2,1)S(1)} collective-permute-done((bf16[2,96,768]{2,1,0:T(8,128)(2,1)S(1)}, bf16[2,96,768]{2,1,0:T(8,128)(2,1)S(1)}, u32[]{:S(2)}, u32[]{:S(2)}) %collective-permute-start.55) | collective-permute-done | bytes 294944 | tf_op jit(solution)/shard_map/ppermute | solution.py:35
  340.2 9.8 %collective-permute-done.59 = bf16[2,192,768]{2,1,0:T(8,128)(2,1)S(1)} collective-permute-done((bf16[2,192,768]{2,1,0:T(8,128)(2,1)S(1)}, bf16[2,192,768]{2,1,0:T(8,128)(2,1)S(1)}, u32[]{:S(2)}, u32[]{:S(2)}) %collective-permute-start.59) | collective-permute-done | bytes 589856 | tf_op jit(solution)/shard_map/ppermute | solution.py:35
  350.2 1.6 fusion.56
  (328 shorter events, 68.0 us)
Async XLA Ops:
  0.7 18.8 %copy-start.12 = (bf16[384,768]{1,0:T(8,128)(2,1)S(1)}, bf16[384,768]{1,0:T(8,128)(2,1)}, u32[]{:S(2)}) copy-start(bf16[384,768]{1,0:T(8,128)(2,1)} %param.25) | copy-start | bytes 1769476
  6.9 13.7 %collective-permute-start.4 = (bf16[1,8,384]{2,1,0:T(8,128)(2,1)}, bf16[1,8,384]{2,1,0:T(8,128)(2,1)}, u32[]{:S(2)}, u32[]{:S(2)}) collective-permute-start(bf16[1,8,384]{2,1,0:T(8,128)(2,1)} %bitcast.7), channel_id=1, source_target_pairs={{0,16},{16,0},{1,17},{17,1},{2,18},{18,2},{3,19},{19,3},{4,20},{20... | collective-permute-start | bytes 18440 | tf_op jit(solution)/shard_map/ppermute | solution.py:35
  12.0 22.6 %collective-permute-start = (bf16[1,128,768]{2,1,0:T(8,128)(2,1)}, bf16[1,128,768]{2,1,0:T(8,128)(2,1)}, u32[]{:S(2)}, u32[]{:S(2)}) collective-permute-start(bf16[1,128,768]{2,1,0:T(8,128)(2,1)} %get-tuple-element.161), channel_id=1, source_target_pairs={{0,4},{4,8},{8,12},{12,0},{1,5},{5,9},{9,13},{13,1},{2,6},{6,10},{... | collective-permute-start | bytes 589832 | tf_op jit(solution)/shard_map/ppermute | solution.py:132
  13.6 23.4 %collective-permute-start.1 = (bf16[1,128,768]{2,1,0:T(8,128)(2,1)}, bf16[1,128,768]{2,1,0:T(8,128)(2,1)}, u32[]{:S(2)}, u32[]{:S(2)}) collective-permute-start(bf16[1,128,768]{2,1,0:T(8,128)(2,1)} %get-tuple-element.163), channel_id=1, source_target_pairs={{0,8},{4,12},{8,0},{12,4},{1,9},{5,13},{9,1},{13,5},{2,10},{6,14},... | collective-permute-start | bytes 589832 | tf_op jit(solution)/shard_map/ppermute | solution.py:132
  16.2 21.8 %collective-permute-start.2 = (bf16[1,128,768]{2,1,0:T(8,128)(2,1)}, bf16[1,128,768]{2,1,0:T(8,128)(2,1)S(1)}, u32[]{:S(2)}, u32[]{:S(2)}) collective-permute-start(bf16[1,128,768]{2,1,0:T(8,128)(2,1)} %get-tuple-element.160), channel_id=1, source_target_pairs={{0,12},{4,0},{8,4},{12,8},{1,13},{5,1},{9,5},{13,9},{2,14},{6,2},{... | collective-permute-start | bytes 589832 | tf_op jit(solution)/shard_map/ppermute | solution.py:132
  17.5 21.8 %collective-permute-start.3 = (bf16[384,768]{1,0:T(8,128)(2,1)}, bf16[384,768]{1,0:T(8,128)(2,1)}, u32[]{:S(2)}, u32[]{:S(2)}) collective-permute-start(bf16[384,768]{1,0:T(8,128)(2,1)} %param.27), channel_id=1, source_target_pairs={{0,2},{1,3},{2,0},{3,1},{4,6},{5,7},{6,4},{7,5},{8,10},{9,11},{10,... | collective-permute-start | bytes 1769480 | tf_op jit(solution)/shard_map/ppermute | solution.py:35
  20.6 17.4 %collective-permute-start.12 = (bf16[3,96,768]{2,1,0:T(8,128)(2,1)}, bf16[3,96,768]{2,1,0:T(8,128)(2,1)}, u32[]{:S(2)}, u32[]{:S(2)}) collective-permute-start(bf16[3,96,768]{2,1,0:T(8,128)(2,1)} %param.19), channel_id=1, source_target_pairs={{0,16},{16,0},{1,17},{17,1},{2,18},{18,2},{3,19},{19,3},{4,20},{20... | collective-permute-start | bytes 1327112 | tf_op jit(solution)/shard_map/ppermute | solution.py:35
  34.6 16.5 %collective-permute-start.8 = (bf16[480,768]{1,0:T(8,128)(2,1)S(1)}, bf16[480,768]{1,0:T(8,128)(2,1)S(1)}, u32[]{:S(2)}, u32[]{:S(2)}) collective-permute-start(bf16[480,768]{1,0:T(8,128)(2,1)S(1)} %pad_maximum_fusion.6), channel_id=1, source_target_pairs={{0,16},{16,0},{1,17},{17,1},{2,18},{18,2},{3,19},{19,3},{4,20},{20... | collective-permute-start | bytes 2211848 | tf_op jit(solution)/shard_map/ppermute | solution.py:35
  39.3 23.7 %copy-start.31 = (bf16[3,256,768]{2,1,0:T(8,128)(2,1)}, bf16[3,256,768]{2,1,0:T(8,128)(2,1)S(1)}, u32[]{:S(2)}) copy-start(bf16[3,256,768]{2,1,0:T(8,128)(2,1)S(1)} %fusion.15) | copy-start | bytes 3538948
  40.9 17.4 %collective-permute-start.6 = (bf16[512,768]{1,0:T(8,128)(2,1)S(1)}, bf16[512,768]{1,0:T(8,128)(2,1)S(1)}, u32[]{:S(2)}, u32[]{:S(2)}) collective-permute-start(bf16[512,768]{1,0:T(8,128)(2,1)S(1)} %add_convert_fusion.4), channel_id=1, source_target_pairs={{0,2},{1,3},{2,0},{3,1},{4,6},{5,7},{6,4},{7,5},{8,10},{9,11},{10,... | collective-permute-start | bytes 2359304 | tf_op jit(solution)/shard_map/ppermute | solution.py:35
  41.5 19.1 %collective-permute-start.5 = (bf16[512,768]{1,0:T(8,128)(2,1)S(1)}, bf16[512,768]{1,0:T(8,128)(2,1)S(1)}, u32[]{:S(2)}, u32[]{:S(2)}) collective-permute-start(bf16[512,768]{1,0:T(8,128)(2,1)S(1)} %add_convert_fusion.4), channel_id=1, source_target_pairs={{0,1},{1,0},{2,3},{3,2},{4,5},{5,4},{6,7},{7,6},{8,9},{9,8},{10,11... | collective-permute-start | bytes 2359304 | tf_op jit(solution)/shard_map/ppermute | solution.py:35
  41.7 18.7 %collective-permute-start.9 = (bf16[1,128,768]{2,1,0:T(8,128)(2,1)S(1)}, bf16[1,128,768]{2,1,0:T(8,128)(2,1)S(1)}, u32[]{:S(2)}, u32[]{:S(2)}) collective-permute-start(bf16[1,128,768]{2,1,0:T(8,128)(2,1)S(1)} %get-tuple-element.158), channel_id=1, source_target_pairs={{0,4},{4,8},{8,12},{12,0},{1,5},{5,9},{9,13},{13,1},{2,6},{6,10},{... | collective-permute-start | bytes 589832 | tf_op jit(solution)/shard_map/ppermute | solution.py:132
  42.4 18.0 %collective-permute-start.10 = (bf16[1,128,768]{2,1,0:T(8,128)(2,1)S(1)}, bf16[1,128,768]{2,1,0:T(8,128)(2,1)S(1)}, u32[]{:S(2)}, u32[]{:S(2)}) collective-permute-start(bf16[1,128,768]{2,1,0:T(8,128)(2,1)S(1)} %get-tuple-element.157), channel_id=1, source_target_pairs={{0,8},{4,12},{8,0},{12,4},{1,9},{5,13},{9,1},{13,5},{2,10},{6,14},... | collective-permute-start | bytes 589832 | tf_op jit(solution)/shard_map/ppermute | solution.py:132
  51.1 9.4 %collective-permute-start.11 = (bf16[1,128,768]{2,1,0:T(8,128)(2,1)S(1)}, bf16[1,128,768]{2,1,0:T(8,128)(2,1)S(1)}, u32[]{:S(2)}, u32[]{:S(2)}) collective-permute-start(bf16[1,128,768]{2,1,0:T(8,128)(2,1)S(1)} %get-tuple-element.156), channel_id=1, source_target_pairs={{0,12},{4,0},{8,4},{12,8},{1,13},{5,1},{9,5},{13,9},{2,14},{6,2},{... | collective-permute-start | bytes 589832 | tf_op jit(solution)/shard_map/ppermute | solution.py:132
  58.3 2.3 collective-permute-start.7
  61.0 35.4 %collective-permute-start.13 = (bf16[976,768]{1,0:T(8,128)(2,1)}, bf16[976,768]{1,0:T(8,128)(2,1)S(1)}, u32[]{:S(2)}, u32[]{:S(2)}) collective-permute-start(bf16[976,768]{1,0:T(8,128)(2,1)} %pad_dynamic-update-slice_fusion.up0), channel_id=1, source_target_pairs={{0,2},{1,3},{2,0},{3,1},{4,6},{5,7},{6,4},{7,5},{8,10},{9,11},{10,... | collective-permute-start | bytes 4497416 | tf_op jit(solution)/shard_map/ppermute | solution.py:35
  61.6 34.8 %collective-permute-start.14 = (bf16[976,768]{1,0:T(8,128)(2,1)}, bf16[976,768]{1,0:T(8,128)(2,1)S(1)}, u32[]{:S(2)}, u32[]{:S(2)}) collective-permute-start(bf16[976,768]{1,0:T(8,128)(2,1)} %pad_dynamic-update-slice_fusion.up0), channel_id=1, source_target_pairs={{0,1},{1,0},{2,3},{3,2},{4,5},{5,4},{6,7},{7,6},{8,9},{9,8},{10,11... | collective-permute-start | bytes 4497416 | tf_op jit(solution)/shard_map/ppermute | solution.py:35
  61.7 31.4 %collective-permute-start.15 = (bf16[2,384,768]{2,1,0:T(8,128)(2,1)S(1)}, bf16[2,384,768]{2,1,0:T(8,128)(2,1)S(1)}, u32[]{:S(2)}, u32[]{:S(2)}) collective-permute-start(bf16[2,384,768]{2,1,0:T(8,128)(2,1)S(1)} %pad_maximum_fusion.3), channel_id=1, source_target_pairs={{0,16},{16,0},{1,17},{17,1},{2,18},{18,2},{3,19},{19,3},{4,20},{20... | collective-permute-start | bytes 3538952 | tf_op jit(solution)/shard_map/ppermute | solution.py:35
  65.9 27.1 %copy-start.9 = (bf16[2048,768]{1,0:T(8,128)(2,1)}, bf16[2048,768]{1,0:T(8,128)(2,1)S(1)}, u32[]{:S(2)}) copy-start(bf16[2048,768]{1,0:T(8,128)(2,1)S(1)} %add_convert_fusion) | copy-start | bytes 9437188
  96.3 14.6 %collective-permute-start.20 = (bf16[2,768,768]{2,1,0:T(8,128)(2,1)S(1)}, bf16[2,768,768]{2,1,0:T(8,128)(2,1)S(1)}, u32[]{:S(2)}, u32[]{:S(2)}) collective-permute-start(bf16[2,768,768]{2,1,0:T(8,128)(2,1)S(1)} %pad_maximum_fusion.1.down_even), channel_id=1, source_target_pairs={{0,1},{1,0},{2,3},{3,2},{4,5},{5,4},{6,7},{7,6},{8,9},{9,8},{10,11... | collective-permute-start | bytes 7077896 | tf_op jit(solution)/shard_map/ppermute | solution.py:35
  96.4 14.6 %collective-permute-start.19 = (bf16[976,768]{1,0:T(8,128)(2,1)S(1)}, bf16[976,768]{1,0:T(8,128)(2,1)S(1)}, u32[]{:S(2)}, u32[]{:S(2)}) collective-permute-start(bf16[976,768]{1,0:T(8,128)(2,1)S(1)} %collective-permute-done.13.up2), channel_id=1, source_target_pairs={{0,1},{1,0},{2,3},{3,2},{4,5},{5,4},{6,7},{7,6},{8,9},{9,8},{10,11... | collective-permute-start | bytes 4497416 | tf_op jit(solution)/shard_map/ppermute | solution.py:35
  97.0 6.4 %collective-permute-start.16 = (bf16[512,256]{1,0:T(8,128)(2,1)S(1)}, bf16[512,256]{1,0:T(8,128)(2,1)S(1)}, u32[]{:S(2)}, u32[]{:S(2)}) collective-permute-start(bf16[512,256]{1,0:T(8,128)(2,1)S(1)} %bitcast.197), channel_id=1, source_target_pairs={{0,1},{1,0},{2,3},{3,2},{4,5},{5,4},{6,7},{7,6},{8,9},{9,8},{10,11... | collective-permute-start | bytes 786440 | tf_op jit(solution)/shard_map/ppermute | solution.py:35
  97.2 9.1 %collective-permute-start.17 = (bf16[512,256]{1,0:T(8,128)(2,1)S(1)}, bf16[512,256]{1,0:T(8,128)(2,1)S(1)}, u32[]{:S(2)}, u32[]{:S(2)}) collective-permute-start(bf16[512,256]{1,0:T(8,128)(2,1)S(1)} %bitcast.196), channel_id=1, source_target_pairs={{0,2},{1,3},{2,0},{3,1},{4,6},{5,7},{6,4},{7,5},{8,10},{9,11},{10,... | collective-permute-start | bytes 786440 | tf_op jit(solution)/shard_map/ppermute | solution.py:35
  97.7 13.3 %collective-permute-start.18 = (bf16[512,256]{1,0:T(8,128)(2,1)S(1)}, bf16[512,256]{1,0:T(8,128)(2,1)S(1)}, u32[]{:S(2)}, u32[]{:S(2)}) collective-permute-start(bf16[512,256]{1,0:T(8,128)(2,1)S(1)} %bitcast.195), channel_id=1, source_target_pairs={{0,3},{1,2},{2,1},{3,0},{4,7},{5,6},{6,5},{7,4},{8,11},{9,10},{10,... | collective-permute-start | bytes 786440 | tf_op jit(solution)/shard_map/ppermute | solution.py:35
  144.2 17.3 %collective-permute-start.24 = (bf16[2,768,768]{2,1,0:T(8,128)(2,1)}, bf16[2,768,768]{2,1,0:T(8,128)(2,1)}, u32[]{:S(2)}, u32[]{:S(2)}) collective-permute-start(bf16[2,768,768]{2,1,0:T(8,128)(2,1)} %get-tuple-element.74), channel_id=1, source_target_pairs={{0,1},{1,0},{2,3},{3,2},{4,5},{5,4},{6,7},{7,6},{8,9},{9,8},{10,11... | collective-permute-start | bytes 7077896 | tf_op jit(solution)/shard_map/ppermute | solution.py:35
  144.6 20.1 %collective-permute-start.25 = (bf16[2,768,768]{2,1,0:T(8,128)(2,1)}, bf16[2,768,768]{2,1,0:T(8,128)(2,1)}, u32[]{:S(2)}, u32[]{:S(2)}) collective-permute-start(bf16[2,768,768]{2,1,0:T(8,128)(2,1)} %get-tuple-element.76), channel_id=1, source_target_pairs={{0,1},{1,0},{2,3},{3,2},{4,5},{5,4},{6,7},{7,6},{8,9},{9,8},{10,11... | collective-permute-start | bytes 7077896 | tf_op jit(solution)/shard_map/ppermute | solution.py:35
  145.8 8.6 %collective-permute-start.23 = (bf16[512,256]{1,0:T(8,128)(2,1)}, bf16[512,256]{1,0:T(8,128)(2,1)}, u32[]{:S(2)}, u32[]{:S(2)}) collective-permute-start(bf16[512,256]{1,0:T(8,128)(2,1)} %get-tuple-element.137), channel_id=1, source_target_pairs={{0,3},{1,2},{2,1},{3,0},{4,7},{5,6},{6,5},{7,4},{8,11},{9,10},{10,... | collective-permute-start | bytes 786440 | tf_op jit(solution)/shard_map/ppermute | solution.py:35
  146.2 14.1 %collective-permute-start.22 = (bf16[512,256]{1,0:T(8,128)(2,1)}, bf16[512,256]{1,0:T(8,128)(2,1)}, u32[]{:S(2)}, u32[]{:S(2)}) collective-permute-start(bf16[512,256]{1,0:T(8,128)(2,1)} %get-tuple-element.138), channel_id=1, source_target_pairs={{0,2},{1,3},{2,0},{3,1},{4,6},{5,7},{6,4},{7,5},{8,10},{9,11},{10,... | collective-permute-start | bytes 786440 | tf_op jit(solution)/shard_map/ppermute | solution.py:35
  147.6 12.6 %collective-permute-start.21 = (bf16[512,256]{1,0:T(8,128)(2,1)}, bf16[512,256]{1,0:T(8,128)(2,1)}, u32[]{:S(2)}, u32[]{:S(2)}) collective-permute-start(bf16[512,256]{1,0:T(8,128)(2,1)} %get-tuple-element.139), channel_id=1, source_target_pairs={{0,1},{1,0},{2,3},{3,2},{4,5},{5,4},{6,7},{7,6},{8,9},{9,8},{10,11... | collective-permute-start | bytes 786440 | tf_op jit(solution)/shard_map/ppermute | solution.py:35
  167.0 31.3 %collective-permute-start.26 = (bf16[768,768]{1,0:T(8,128)(2,1)S(1)}, bf16[768,768]{1,0:T(8,128)(2,1)S(1)}, u32[]{:S(2)}, u32[]{:S(2)}) collective-permute-start(bf16[768,768]{1,0:T(8,128)(2,1)S(1)} %slice_bitcast_fusion), channel_id=1, source_target_pairs={{0,2},{1,3},{2,0},{3,1},{4,6},{5,7},{6,4},{7,5},{8,10},{9,11},{10,... | collective-permute-start | bytes 3538952 | tf_op jit(solution)/shard_map/ppermute | solution.py:35
  167.7 31.5 %collective-permute-start.27 = (bf16[2,384,768]{2,1,0:T(8,128)(2,1)S(1)}, bf16[2,384,768]{2,1,0:T(8,128)(2,1)S(1)}, u32[]{:S(2)}, u32[]{:S(2)}) collective-permute-start(bf16[2,384,768]{2,1,0:T(8,128)(2,1)S(1)} %dynamic-slice_bitcast_fusion), channel_id=1, source_target_pairs={{0,16},{16,0},{1,17},{17,1},{2,18},{18,2},{3,19},{19,3},{4,20},{20... | collective-permute-start | bytes 3538952 | tf_op jit(solution)/shard_map/ppermute | solution.py:35
  169.1 29.1 %collective-permute-start.28 = (bf16[1,128,768]{2,1,0:T(8,128)(2,1)}, bf16[1,128,768]{2,1,0:T(8,128)(2,1)S(1)}, u32[]{:S(2)}, u32[]{:S(2)}) collective-permute-start(bf16[1,128,768]{2,1,0:T(8,128)(2,1)} %get-tuple-element.154), channel_id=1, source_target_pairs={{4,0},{8,4},{12,8},{0,12},{5,1},{9,5},{13,9},{1,13},{6,2},{10,6},{... | collective-permute-start | bytes 589832 | tf_op jit(solution)/shard_map/ppermute | solution.py:132
  172.0 26.2 %collective-permute-start.29 = (bf16[1,128,768]{2,1,0:T(8,128)(2,1)}, bf16[1,128,768]{2,1,0:T(8,128)(2,1)S(1)}, u32[]{:S(2)}, u32[]{:S(2)}) collective-permute-start(bf16[1,128,768]{2,1,0:T(8,128)(2,1)} %get-tuple-element.153), channel_id=1, source_target_pairs={{8,0},{12,4},{0,8},{4,12},{9,1},{13,5},{1,9},{5,13},{10,2},{14,6},... | collective-permute-start | bytes 589832 | tf_op jit(solution)/shard_map/ppermute | solution.py:132
  173.8 24.5 %collective-permute-start.30 = (bf16[1,128,768]{2,1,0:T(8,128)(2,1)}, bf16[1,128,768]{2,1,0:T(8,128)(2,1)S(1)}, u32[]{:S(2)}, u32[]{:S(2)}) collective-permute-start(bf16[1,128,768]{2,1,0:T(8,128)(2,1)} %get-tuple-element.152), channel_id=1, source_target_pairs={{12,0},{0,4},{4,8},{8,12},{13,1},{1,5},{5,9},{9,13},{14,2},{2,6},{... | collective-permute-start | bytes 589832 | tf_op jit(solution)/shard_map/ppermute | solution.py:132
  212.9 20.8 %copy-start.2 = (bf16[4,2,128,768]{3,2,1,0:T(8,128)(2,1)}, bf16[4,2,128,768]{3,2,1,0:T(8,128)(2,1)S(1)}, u32[]{:S(2)}) copy-start(bf16[4,2,128,768]{3,2,1,0:T(8,128)(2,1)S(1)} %attend_back_0_2.1) | copy-start | bytes 4718596
  214.4 3.2 collective-permute-start.32
  214.4 3.2 collective-permute-start.31
  215.0 15.4 %collective-permute-start.33 = (bf16[384,768]{1,0:T(8,128)(2,1)S(1)}, bf16[384,768]{1,0:T(8,128)(2,1)S(1)}, u32[]{:S(2)}, u32[]{:S(2)}) collective-permute-start(bf16[384,768]{1,0:T(8,128)(2,1)S(1)} %dynamic-slice_bitcast_fusion.2), channel_id=1, source_target_pairs={{0,16},{16,0},{1,17},{17,1},{2,18},{18,2},{3,19},{19,3},{4,20},{20... | collective-permute-start | bytes 1769480 | tf_op jit(solution)/shard_map/ppermute | solution.py:35
  216.6 15.1 %collective-permute-start.34 = (bf16[384,768]{1,0:T(8,128)(2,1)S(1)}, bf16[384,768]{1,0:T(8,128)(2,1)S(1)}, u32[]{:S(2)}, u32[]{:S(2)}) collective-permute-start(bf16[384,768]{1,0:T(8,128)(2,1)S(1)} %slice_bitcast_fusion.1), channel_id=1, source_target_pairs={{0,2},{1,3},{2,0},{3,1},{4,6},{5,7},{6,4},{7,5},{8,10},{9,11},{10,... | collective-permute-start | bytes 1769480 | tf_op jit(solution)/shard_map/ppermute | solution.py:35
  217.5 15.2 %collective-permute-start.35 = (bf16[2,192,768]{2,1,0:T(8,128)(2,1)S(1)}, bf16[2,192,768]{2,1,0:T(8,128)(2,1)S(1)}, u32[]{:S(2)}, u32[]{:S(2)}) collective-permute-start(bf16[2,192,768]{2,1,0:T(8,128)(2,1)S(1)} %copy-done.8), channel_id=1, source_target_pairs={{0,1},{1,0},{2,3},{3,2},{4,5},{5,4},{6,7},{7,6},{8,9},{9,8},{10,11... | collective-permute-start | bytes 1769480 | tf_op jit(solution)/shard_map/ppermute | solution.py:35
  232.8 27.4 %collective-permute-start.39 = (bf16[256,768]{1,0:T(8,128)(2,1)}, bf16[256,768]{1,0:T(8,128)(2,1)}, u32[]{:S(2)}, u32[]{:S(2)}) collective-permute-start(bf16[256,768]{1,0:T(8,128)(2,1)} %get-tuple-element.99), channel_id=1, source_target_pairs={{0,2},{1,3},{2,0},{3,1},{4,6},{5,7},{6,4},{7,5},{8,10},{9,11},{10,... | collective-permute-start | bytes 1179656 | tf_op jit(solution)/shard_map/ppermute | solution.py:35
  237.3 20.4 %collective-permute-start.37 = (bf16[256,768]{1,0:T(8,128)(2,1)}, bf16[256,768]{1,0:T(8,128)(2,1)}, u32[]{:S(2)}, u32[]{:S(2)}) collective-permute-start(bf16[256,768]{1,0:T(8,128)(2,1)} %get-tuple-element.129), channel_id=1, source_target_pairs={{0,1},{1,0},{2,3},{3,2},{4,5},{5,4},{6,7},{7,6},{8,9},{9,8},{10,11... | collective-permute-start | bytes 1179656 | tf_op jit(solution)/shard_map/ppermute | solution.py:35
  237.3 30.4 %collective-permute-start.36 = (bf16[256,768]{1,0:T(8,128)(2,1)}, bf16[256,768]{1,0:T(8,128)(2,1)}, u32[]{:S(2)}, u32[]{:S(2)}) collective-permute-start(bf16[256,768]{1,0:T(8,128)(2,1)} %get-tuple-element.128), channel_id=1, source_target_pairs={{0,1},{1,0},{2,3},{3,2},{4,5},{5,4},{6,7},{7,6},{8,9},{9,8},{10,11... | collective-permute-start | bytes 1179656 | tf_op jit(solution)/shard_map/ppermute | solution.py:35
  244.6 9.2 %collective-permute-start.50 = (bf16[192,768]{1,0:T(8,128)(2,1)}, bf16[192,768]{1,0:T(8,128)(2,1)}, u32[]{:S(2)}, u32[]{:S(2)}) collective-permute-start(bf16[192,768]{1,0:T(8,128)(2,1)} %slice_bitcast_fusion.2), channel_id=1, source_target_pairs={{0,2},{1,3},{2,0},{3,1},{4,6},{5,7},{6,4},{7,5},{8,10},{9,11},{10,... | collective-permute-start | bytes 884744 | tf_op jit(solution)/shard_map/ppermute | solution.py:35
  248.9 15.3 %collective-permute-start.56 = (bf16[2,192,768]{2,1,0:T(8,128)(2,1)}, bf16[2,192,768]{2,1,0:T(8,128)(2,1)}, u32[]{:S(2)}, u32[]{:S(2)}) collective-permute-start(bf16[2,192,768]{2,1,0:T(8,128)(2,1)} %dynamic-slice_bitcast_fusion.1), channel_id=1, source_target_pairs={{0,4},{4,0},{8,12},{12,8},{1,5},{5,1},{9,13},{13,9},{2,6},{6,2},{1... | collective-permute-start | bytes 1769480 | tf_op jit(solution)/shard_map/ppermute | solution.py:35
  256.5 23.3 %collective-permute-start.51 = (bf16[4,96,768]{2,1,0:T(8,128)(2,1)}, bf16[4,96,768]{2,1,0:T(8,128)(2,1)}, u32[]{:S(2)}, u32[]{:S(2)}) collective-permute-start(bf16[4,96,768]{2,1,0:T(8,128)(2,1)} %fusion.21), channel_id=1, source_target_pairs={{0,16},{16,0},{1,17},{17,1},{2,18},{18,2},{3,19},{19,3},{4,20},{20... | collective-permute-start | bytes 1769480 | tf_op jit(solution)/shard_map/ppermute | solution.py:35
  258.7 10.0 %collective-permute-start.38 = (bf16[256,768]{1,0:T(8,128)(2,1)S(1)}, bf16[256,768]{1,0:T(8,128)(2,1)S(1)}, u32[]{:S(2)}, u32[]{:S(2)}) collective-permute-start(bf16[256,768]{1,0:T(8,128)(2,1)S(1)} %add_convert_fusion.6), channel_id=1, source_target_pairs={{0,2},{1,3},{2,0},{3,1},{4,6},{5,7},{6,4},{7,5},{8,10},{9,11},{10,... | collective-permute-start | bytes 1179656 | tf_op jit(solution)/shard_map/ppermute | solution.py:35
  266.2 30.2 %collective-permute-start.57 = (bf16[192,768]{1,0:T(8,128)(2,1)}, bf16[192,768]{1,0:T(8,128)(2,1)}, u32[]{:S(2)}, u32[]{:S(2)}) collective-permute-start(bf16[192,768]{1,0:T(8,128)(2,1)} %dynamic-slice_bitcast_fusion.3), channel_id=1, source_target_pairs={{0,8},{4,12},{8,0},{12,4},{1,9},{5,13},{9,1},{13,5},{2,10},{6,14},... | collective-permute-start | bytes 884744 | tf_op jit(solution)/shard_map/ppermute | solution.py:35
  271.3 4.2 %collective-permute-start.44 = (f32[72,128]{1,0:T(8,128)S(1)}, f32[72,128]{1,0:T(8,128)S(1)}, u32[]{:S(2)}, u32[]{:S(2)}) collective-permute-start(f32[72,128]{1,0:T(8,128)S(1)} %pad_maximum_fusion.9), channel_id=1, source_target_pairs={{0,2},{1,3},{2,0},{3,1},{4,6},{5,7},{6,4},{7,5},{8,10},{9,11},{10,... | collective-permute-start | bytes 110600 | tf_op jit(solution)/shard_map/ppermute | solution.py:35
  272.8 3.4 collective-permute-start.45
  272.8 3.4 collective-permute-start.43
  276.2 7.7 %collective-permute-start.47 = (f32[72,128]{1,0:T(8,128)S(1)}, f32[72,128]{1,0:T(8,128)S(1)}, u32[]{:S(2)}, u32[]{:S(2)}) collective-permute-start(f32[72,128]{1,0:T(8,128)S(1)} %add_add_fusion.1), channel_id=1, source_target_pairs={{0,8},{4,12},{8,0},{12,4},{1,9},{5,13},{9,1},{13,5},{2,10},{6,14},... | collective-permute-start | bytes 110600 | tf_op jit(solution)/shard_map/ppermute | solution.py:35
  277.8 7.9 %collective-permute-start.48 = (f32[72,128]{1,0:T(8,128)S(1)}, f32[72,128]{1,0:T(8,128)S(1)}, u32[]{:S(2)}, u32[]{:S(2)}) collective-permute-start(f32[72,128]{1,0:T(8,128)S(1)} %add_add_fusion.1), channel_id=1, source_target_pairs={{0,12},{4,8},{8,4},{12,0},{1,13},{5,9},{9,5},{13,1},{2,14},{6,10},... | collective-permute-start | bytes 110600 | tf_op jit(solution)/shard_map/ppermute | solution.py:35
  277.8 7.9 %collective-permute-start.46 = (f32[72,128]{1,0:T(8,128)S(1)}, f32[72,128]{1,0:T(8,128)S(1)}, u32[]{:S(2)}, u32[]{:S(2)}) collective-permute-start(f32[72,128]{1,0:T(8,128)S(1)} %add_add_fusion.1), channel_id=1, source_target_pairs={{0,4},{4,0},{8,12},{12,8},{1,5},{5,1},{9,13},{13,9},{2,6},{6,2},{1... | collective-permute-start | bytes 110600 | tf_op jit(solution)/shard_map/ppermute | solution.py:35
  281.0 14.2 %collective-permute-start.52 = (bf16[2,96,768]{2,1,0:T(8,128)(2,1)S(1)}, bf16[2,96,768]{2,1,0:T(8,128)(2,1)S(1)}, u32[]{:S(2)}, u32[]{:S(2)}) collective-permute-start(bf16[2,96,768]{2,1,0:T(8,128)(2,1)S(1)} %dynamic-slice_bitcast_fusion.4), channel_id=1, source_target_pairs={{0,4},{4,0},{8,12},{12,8},{1,5},{5,1},{9,13},{13,9},{2,6},{6,2},{1... | collective-permute-start | bytes 884744 | tf_op jit(solution)/shard_map/ppermute | solution.py:35
  283.9 20.2 %collective-permute-start.40 = (bf16[1,128,768]{2,1,0:T(8,128)(2,1)S(1)}, bf16[1,128,768]{2,1,0:T(8,128)(2,1)S(1)}, u32[]{:S(2)}, u32[]{:S(2)}) collective-permute-start(bf16[1,128,768]{2,1,0:T(8,128)(2,1)S(1)} %get-tuple-element.150), channel_id=1, source_target_pairs={{4,0},{8,4},{12,8},{0,12},{5,1},{9,5},{13,9},{1,13},{6,2},{10,6},{... | collective-permute-start | bytes 589832 | tf_op jit(solution)/shard_map/ppermute | solution.py:132
  285.7 44.9 %collective-permute-start.41 = (bf16[1,128,768]{2,1,0:T(8,128)(2,1)S(1)}, bf16[1,128,768]{2,1,0:T(8,128)(2,1)S(1)}, u32[]{:S(2)}, u32[]{:S(2)}) collective-permute-start(bf16[1,128,768]{2,1,0:T(8,128)(2,1)S(1)} %get-tuple-element.149), channel_id=1, source_target_pairs={{8,0},{12,4},{0,8},{4,12},{9,1},{13,5},{1,9},{5,13},{10,2},{14,6},... | collective-permute-start | bytes 589832 | tf_op jit(solution)/shard_map/ppermute | solution.py:132
  285.7 44.9 %collective-permute-start.42 = (bf16[1,128,768]{2,1,0:T(8,128)(2,1)S(1)}, bf16[1,128,768]{2,1,0:T(8,128)(2,1)S(1)}, u32[]{:S(2)}, u32[]{:S(2)}) collective-permute-start(bf16[1,128,768]{2,1,0:T(8,128)(2,1)S(1)} %get-tuple-element.148), channel_id=1, source_target_pairs={{12,0},{0,4},{4,8},{8,12},{13,1},{1,5},{5,9},{9,13},{14,2},{2,6},{... | collective-permute-start | bytes 589832 | tf_op jit(solution)/shard_map/ppermute | solution.py:132
  295.3 4.8 %collective-permute-start.49 = (f32[72,128]{1,0:T(8,128)S(1)}, f32[72,128]{1,0:T(8,128)S(1)}, u32[]{:S(2)}, u32[]{:S(2)}) collective-permute-start(f32[72,128]{1,0:T(8,128)S(1)} %add_add_fusion), channel_id=1, source_target_pairs={{0,16},{16,0},{1,17},{17,1},{2,18},{18,2},{3,19},{19,3},{4,20},{20... | collective-permute-start | bytes 110600 | tf_op jit(solution)/shard_map/ppermute | solution.py:35
  296.4 19.3 %collective-permute-start.53 = (bf16[96,768]{1,0:T(8,128)(2,1)S(1)}, bf16[96,768]{1,0:T(8,128)(2,1)S(1)}, u32[]{:S(2)}, u32[]{:S(2)}) collective-permute-start(bf16[96,768]{1,0:T(8,128)(2,1)S(1)} %dynamic-slice_bitcast_fusion.5), channel_id=1, source_target_pairs={{0,8},{4,12},{8,0},{12,4},{1,9},{5,13},{9,1},{13,5},{2,10},{6,14},... | collective-permute-start | bytes 442376 | tf_op jit(solution)/shard_map/ppermute | solution.py:35
  300.1 25.1 %collective-permute-start.58 = (bf16[192,768]{1,0:T(8,128)(2,1)S(1)}, bf16[192,768]{1,0:T(8,128)(2,1)S(1)}, u32[]{:S(2)}, u32[]{:S(2)}) collective-permute-start(bf16[192,768]{1,0:T(8,128)(2,1)S(1)} %fusion.24), channel_id=1, source_target_pairs={{0,8},{4,12},{8,0},{12,4},{1,9},{5,13},{9,1},{13,5},{2,10},{6,14},... | collective-permute-start | bytes 884744 | tf_op jit(solution)/shard_map/ppermute | solution.py:35
  315.7 12.5 %collective-permute-start.54 = (bf16[96,768]{1,0:T(8,128)(2,1)S(1)}, bf16[96,768]{1,0:T(8,128)(2,1)S(1)}, u32[]{:S(2)}, u32[]{:S(2)}) collective-permute-start(bf16[96,768]{1,0:T(8,128)(2,1)S(1)} %fusion.27), channel_id=1, source_target_pairs={{0,8},{4,12},{8,0},{12,4},{1,9},{5,13},{9,1},{13,5},{2,10},{6,14},... | collective-permute-start | bytes 442376 | tf_op jit(solution)/shard_map/ppermute | solution.py:35
  328.3 9.9 %collective-permute-start.55 = (bf16[2,96,768]{2,1,0:T(8,128)(2,1)S(1)}, bf16[2,96,768]{2,1,0:T(8,128)(2,1)S(1)}, u32[]{:S(2)}, u32[]{:S(2)}) collective-permute-start(bf16[2,96,768]{2,1,0:T(8,128)(2,1)S(1)} %pad_maximum_fusion.8), channel_id=1, source_target_pairs={{0,4},{4,0},{8,12},{12,8},{1,5},{5,1},{9,13},{13,9},{2,6},{6,2},{1... | collective-permute-start | bytes 884744 | tf_op jit(solution)/shard_map/ppermute | solution.py:35
  328.4 21.5 %collective-permute-start.59 = (bf16[2,192,768]{2,1,0:T(8,128)(2,1)S(1)}, bf16[2,192,768]{2,1,0:T(8,128)(2,1)S(1)}, u32[]{:S(2)}, u32[]{:S(2)}) collective-permute-start(bf16[2,192,768]{2,1,0:T(8,128)(2,1)S(1)} %pad_maximum_fusion.7), channel_id=1, source_target_pairs={{0,4},{4,0},{8,12},{12,8},{1,5},{5,1},{9,13},{13,9},{2,6},{6,2},{1... | collective-permute-start | bytes 1769480 | tf_op jit(solution)/shard_map/ppermute | solution.py:35
  (46 other events, 301.4 us)

commit v3 on v2

--- a/solution.py
+++ b/solution.py
@@ -74,19 +74,43 @@
     return (mine.astype(F32) + swap(theirs, "fsdp", 1).astype(F32)).astype(value.dtype)
 
 
-def sum_ctx(value):
+def scatter_pair(value, split):
+    size = lax.axis_size("fsdp")
+    pieces = [part.reshape((size, -1) + part.shape[1:]) for part in (value[:split], value[split:])]
+    if size != 2:
+        return jnp.concatenate([scatter_fsdp(piece) for piece in pieces], axis=0)
+    rank = lax.axis_index("fsdp")
+
+    def cut(index):
+        both = [lax.dynamic_index_in_dim(piece, index, 0, keepdims=False) for piece in pieces]
+        return jnp.concatenate(both, axis=0)
+
+    return (cut(rank).astype(F32) + swap(cut(1 - rank), "fsdp", 1).astype(F32)).astype(value.dtype)
+
+
+def ctx_plan(rows):
     size = lax.axis_size("ctx")
-    rows = value.shape[0]
-    if size != 4 or rows % (8 * size):
-        return lax.psum(value, "ctx").astype(F32)
+    return size == 4 and rows % (8 * size) == 0
+
+
+def ctx_reduce(value):
+    if not ctx_plan(value.shape[0]):
+        return lax.psum(value, "ctx")
     rank = lax.axis_index("ctx")
-    near, far = rank % 2, rank // 2
-    parts = value.reshape((2, 2, rows // size) + value.shape[1:])
 
     def halve(array, axis, bit, side):
         mine = lax.dynamic_index_in_dim(array, side, axis, keepdims=False)
         theirs = lax.dynamic_index_in_dim(array, 1 - side, axis, keepdims=False)
         return (mine.astype(F32) + swap(theirs, "ctx", bit).astype(F32)).astype(value.dtype)
+
+    parts = value.reshape((2, 2, value.shape[0] // 4) + value.shape[1:])
+    return halve(halve(parts, 1, 1, rank % 2), 0, 2, rank // 2)
+
+
+def ctx_spread(total, rows):
+    if not ctx_plan(rows):
+        return total.astype(F32)
+    rank = lax.axis_index("ctx")
 
     def double(array, axis, bit, side):
         other = swap(array, "ctx", bit)
@@ -95,9 +119,8 @@
             [jnp.where(first, array, other), jnp.where(first, other, array)], axis=axis
         )
 
-    total = halve(halve(parts, 1, 1, near), 0, 2, far)
-    total = double(double(total, 0, 2, far), 1, 1, near)
-    return total.reshape(value.shape).astype(F32)
+    total = double(double(total, 0, 2, rank // 2), 1, 1, rank % 2)
+    return total.reshape((rows,) + total.shape[3:]).astype(F32)
 
 
 def gather_tp(value):
@@ -463,7 +486,7 @@
     at = pl.program_id(0)
     tokens, width = x_ref.shape
     units = wd.shape[0]
-    chunk = 256
+    chunk, wide = tokens, 256
     merged = (m0, m1, m2, m3)
     ups = (up0, up1, up2, up3)
     downs = ((down_even, 0), (down_odd, 0), (down_even, 1), (down_odd, 1))
@@ -520,11 +543,11 @@
             small_ref[4 + s : 5 + s, :] = total
 
     def weight_grads(up_out, down_out):
-        for c in range(units // chunk):
-            rows = slice(c * chunk, (c + 1) * chunk)
+        for c in range(units // wide):
+            rows = slice(c * wide, (c + 1) * wide)
             down_out[0, rows, :] = dot_tn(act[:, rows], cot_ref[...]).astype(BF)
-        for c in range(width // chunk):
-            rows = slice(c * chunk, (c + 1) * chunk)
+        for c in range(width // wide):
+            rows = slice(c * wide, (c + 1) * wide)
             up_out[0, rows, :] = dot_tn(n2[:, rows], gpre[...]).astype(BF)
 
     @pl.when(at < 2)
@@ -712,18 +735,25 @@
     (
         block_out, grad_hidden, grad_slots, up_even, up_odd, down_even_g, down_odd_g, out_even, out_odd, sums,
     ) = middle(head_width, x_own, merged, cot_rows, vecs, ups, down_even, down_odd)
+
+    up_near = jnp.concatenate(
+        [add_low(up_even, swap(up_odd, "tp", 1)), add_low(out_even, swap(out_odd, "tp", 1))], axis=1
+    )
+    down_near = add_low(down_even_g, swap(down_odd_g, "tp", 1))
+    grad_slots = [grad_slots[s] for s in range(ranks)]
+    grad_slots[1], up_near, down_near = lax.optimization_barrier((grad_slots[1], up_near, down_near))
     grad_slots = [grad_slots[0]] + [swap(grad_slots[s], "tp", s) for s in range(1, ranks)]
     grad_attended = jnp.stack(grad_slots).reshape(ranks, seqs, sub, HEAD_PAD)
-
-    up_near = add_low(up_even, swap(up_odd, "tp", 1))
-    down_near = add_low(down_even_g, swap(down_odd_g, "tp", 1))
-    grad_attended, up_near, down_near, block_out, out_even, out_odd = lax.optimization_barrier(
-        (grad_attended, up_near, down_near, block_out, out_even, out_odd)
+    grad_attended, up_near, down_near, block_out = lax.optimization_barrier(
+        (grad_attended, up_near, down_near, block_out)
     )
     out_blocks = from_sequence(block_out.reshape(seqs, sub, width))
 
     up_mid = add_low(up_near[0], swap(up_near[1], "tp", 2))
     down_mid = scatter_fsdp(down_near.reshape(2, fsdp, -1, width).transpose(1, 0, 2, 3))
+
+    def project_back(half):
+        return dot_nn(half.reshape(-1, 3 * HEAD_PAD), qkv_pad).astype(BF).reshape(ranks, -1, width)
 
     q_blocks = tokens // BQ
     back = functools.partial(attend_back, where, seg_q, seg_k, proj, keyvals, attended)
@@ -737,31 +767,28 @@
     else:
         mid = q_blocks // 2
         high, rest = back(grad_attended, lse, (mid, q_blocks), (0, q_blocks), mid)
-        rest, high, up_mid, down_mid, out_even, out_odd, out_blocks = lax.optimization_barrier(
-            (rest, high, up_mid, down_mid, out_even, out_odd, out_blocks)
+        rest, high, up_mid, down_mid, out_blocks = lax.optimization_barrier(
+            (rest, high, up_mid, down_mid, out_blocks)
         )
+        high_rows = project_back(high)
+        rest, high_rows = lax.optimization_barrier((rest, high_rows))
         (low,) = back(grad_attended, lse, (0, mid), (0, mid), 0, rest)
         halves = [low, high]
         edges = [0, mid * BQ // (ranks * sub), seqs]
 
-    up_last = scatter_fsdp(up_mid.reshape(fsdp, -1, up_mid.shape[1]))
+    up_last = scatter_pair(up_mid, width)
     down_last = add_low(down_mid[0], swap(down_mid[1], "tp", 2))
-    out_near = add_low(out_even, swap(out_odd, "tp", 1))
-    grad_rows = [None] * len(halves)
-
-    def back_rows(half):
-        rows = dot_nn(half.reshape(-1, 3 * HEAD_PAD), qkv_pad).astype(BF).reshape(ranks, -1, width)
-        return near_sums([rows[s] for s in range(ranks)])
-
     if parts == 1:
-        grad_rows[1] = back_rows(halves[1])
-        halves[0], grad_rows[1], up_last, down_last, out_near = lax.optimization_barrier(
-            (halves[0], grad_rows[1], up_last, down_last, out_near)
+        halves[0], high_rows, up_last, down_last = lax.optimization_barrier(
+            (halves[0], high_rows, up_last, down_last)
         )
-    grad_rows[0] = back_rows(halves[0])
-    out_mid = add_low(out_near[0], swap(out_near[1], "tp", 2))
-    total = sum_ctx(jnp.concatenate([up_last, down_last], axis=0))
-    sum_up, sum_down = total[: w_up.shape[0]], total[w_up.shape[0] :]
+        slots = [project_back(halves[0]), high_rows]
+    else:
+        slots = [project_back(halves[0])]
+    grad_rows = [near_sums([rows[s] for s in range(ranks)]) for rows in reversed(slots)][::-1]
+    quarter = ctx_reduce(jnp.concatenate([up_last, down_last], axis=0))
+    cuts = [0, w_up.shape[0], w_up.shape[0] + w_out.shape[0], w_up.shape[0] + w_out.shape[0] + w_down.shape[0]]
+    halves, grad_rows = lax.optimization_barrier((halves, grad_rows))
 
     normed_all = normed_one.reshape(ranks, seqs, sub, width)
     grad_qkv, grad_normed, bias_sum = 0.0, [], 0.0
@@ -773,12 +800,17 @@
         bias_sum = bias_sum + jnp.sum(rows.astype(F32), axis=0)
     grad_normed_one = jnp.concatenate(grad_normed, axis=0)
     grad_x = grad_hidden + norm_back(xhat_one, rstd_one, gain_one, grad_normed_one)
-    grad_blocks = from_sequence(grad_x.astype(BF).reshape(seqs, sub, width))
+    grad_x = grad_x.astype(BF)
+    ln1_sums = jnp.stack([jnp.sum(grad_normed_one * xhat_one, axis=0), jnp.sum(grad_normed_one, axis=0)])
+    grad_x, ln1_sums, quarter = lax.optimization_barrier((grad_x, ln1_sums, quarter))
+    grad_blocks = from_sequence(grad_x.reshape(seqs, sub, width))
+    total = ctx_spread(quarter, cuts[3])
+    sum_up, sum_out, sum_down = (total[cuts[n] : cuts[n + 1]] for n in range(3))
 
     grad_qkv = grad_qkv.reshape(3, HEAD_PAD, width)[:, :head_width].astype(BF)
-    both = jnp.concatenate([grad_qkv, out_mid[None]]).reshape(4, fsdp, -1, width).transpose(1, 0, 2, 3)
-    total = sum_ctx(scatter_fsdp(both).reshape(-1, width))
-    sum_qkv, sum_out = total[: -w_out.shape[0]].reshape(w_qkv.shape), total[-w_out.shape[0] :]
+    qkv_shard = scatter_fsdp(grad_qkv.reshape(3, fsdp, -1, width).transpose(1, 0, 2, 3))
+    qkv_rows = qkv_shard.reshape(-1, width)
+    sum_qkv = ctx_spread(ctx_reduce(qkv_rows), qkv_rows.shape[0]).reshape(w_qkv.shape)
 
     bias_sum = bias_sum.reshape(3, HEAD_PAD)[:, :head_width].reshape(3, heads, 64)
     bias_rows = jnp.concatenate([bias_sum[0], bias_sum[2]], axis=1)
@@ -788,10 +820,10 @@
     up_bias_all = jnp.zeros((ranks, width), F32)
     for s in range(ranks):
         up_bias_all = lax.dynamic_update_slice(up_bias_all, sums[4 + s : 5 + s], (tp_rank ^ s, 0))
-    ln1_sums = jnp.stack([jnp.sum(grad_normed_one * xhat_one, axis=0), jnp.sum(grad_normed_one, axis=0)])
     late = jnp.concatenate(
         [sums[:4].reshape(-1, LANES), up_bias_all.reshape(-1, LANES), ln1_sums.reshape(-1, LANES), bias_all]
     )
+    late, grad_blocks = lax.optimization_barrier((late, grad_blocks))
     for axis in ("tp", "ctx", "fsdp"):
         late = butterfly(late, axis)
     late_rows = late[: 10 * width // LANES].reshape(10, fsdp, shard)

time: 357 us -> 333 us (0.933)
  waiting for transfers between devices: 112 us -> 86.8 us
  starting transfers between devices: 52.7 us -> 63.8 us
  other arithmetic: 36.6 us -> 30 us
    ppermute x48 -> x47, waiting for transfers between devices: 111 us -> 67.2 us  [swap(): return lax.ppermute(value, axis, [(i, i ^ bit) for i in range(size)])]
    ppermute x12, waiting for transfers between devices: 0.17 us -> 19.6 us  [send(): return lax.ppermute(value, 'ctx', pairs)]
    ppermute x48 -> x47, starting transfers between devices: 38.6 us -> 47.7 us  [swap(): return lax.ppermute(value, axis, [(i, i ^ bit) for i in range(size)])]
    convert_element_type x8 -> x7, other arithmetic: 9.87 us -> 5.37 us  [add_low(): return (left.astype(F32) + right.astype(F32)).astype(BF)]
    unnamed x101 -> x71, local copies, waits for them, and re-layouts: 6.2 us -> 7.27 us
  transfers between devices with their start and end apart: 60 -> 59, of which waited for: 22 -> 21; matrix products, arithmetic and copies ran while one was open for 20% -> 18% of each run, Pallas kernels for 15% -> 19%
where the time goes in v3:
time: 333 us; the launch traced here: 329 us
  Pallas kernels  94.3 us (28%)
  waiting for transfers between devices  86.8 us (26%)
  starting transfers between devices  63.8 us (19%)
  local copies, waits for them, and re-layouts  41.5 us (12%)
  other arithmetic  30 us (9%)
  matrix products  10.2 us (3%)
    ppermute x47, waiting for transfers between devices, swap(): return lax.ppermute(value, axis, [(i, i ^ bit) for i in range(size)])  67.2 us
    ppermute x47, starting transfers between devices, swap(): return lax.ppermute(value, axis, [(i, i ^ bit) for i in range(size)])  47.7 us
    pallas_call x2, Pallas kernels, attend_back(): pl.pallas_call(functools.partial(attend_back_kernel, gathered, q_range, k...  36.7 us
    pallas_call x1, Pallas kernels, middle(): pl.pallas_call(functools.partial(middle_kernel, head_width), grid=(4,), o...  30.5 us
    pallas_call x1, Pallas kernels, attend(): pl.pallas_call(functools.partial(attend_kernel, gathered), out_shape=(jax...  27.1 us
    ppermute x12, waiting for transfers between devices, send(): return lax.ppermute(value, 'ctx', pairs)  19.6 us
    ppermute x12, starting transfers between devices, send(): return lax.ppermute(value, 'ctx', pairs)  16 us
    unnamed x71, local copies, waits for them, and re-layouts  7.27 us
  transfers between devices with their start and end apart: 59, of which 21 were waited for; matrix products, arithmetic and copies ran while one was open for 18% of the time, Pallas kernels for 19%

profile of v3, /device:TPU:0, one launch (start us, length us, event | category | flops | bytes accessed | tf_op | source)
XLA Modules:
  0.0 328.8 jit_solution(3578068615229272595)
XLA Ops:
  6.9 3.0 collective-permute-start.4
  10.0 2.1 constant_dynamic-slice_fusion.14
  12.0 1.6 collective-permute-start
  13.6 2.6 collective-permute-start.1
  16.2 1.3 collective-permute-start.2
  17.5 1.5 collective-permute-start.3
  25.9 1.3 stack_reshape.6
  27.3 1.3 pad_maximum_fusion.13
  30.5 1.2 fusion.36
  33.1 1.6 collective-permute-start.8
  36.6 1.2 broadcast_select_fusion.3
  40.7 1.4 pad_maximum_fusion.5
  42.1 7.6 %collective-permute-done.8 = bf16[480,768]{1,0:T(8,128)(2,1)S(1)} collective-permute-done((bf16[480,768]{1,0:T(8,128)(2,1)S(1)}, bf16[480,768]{1,0:T(8,128)(2,1)S(1)}, u32[]{:S(2)}, u32[]{:S(2)}) %collective-permute-start.8) | collective-permute-done | bytes 737312 | tf_op jit(solution)/shard_map/ppermute | solution.py:35
  52.4 4.0 %collective-permute-done.6 = bf16[512,768]{1,0:T(8,128)(2,1)S(1)} collective-permute-done((bf16[512,768]{1,0:T(8,128)(2,1)S(1)}, bf16[512,768]{1,0:T(8,128)(2,1)S(1)}, u32[]{:S(2)}, u32[]{:S(2)}) %collective-permute-start.6) | collective-permute-done | bytes 786464 | tf_op jit(solution)/shard_map/ppermute | solution.py:35
  60.2 1.2 collective-permute-start.15
  61.4 2.9 add_convert_fusion
  64.2 27.1 %attend.1 = (bf16[4,4,128,256]{3,2,1,0:T(8,128)(2,1)S(1)}, f32[4,3,8,512]{3,2,1,0:T(8,128)S(1)}) custom-call(s32[2]{0:T(128)S(1)} %pad_add_fusion.where_ref, s32[4]{0:T(128)S(1)} %get-tuple-element.137.low_ref, s32[4]{0:T(128)S(1)} %max.3.full_ref, s32[2048,1]{1,0:T(8,128)S(1)} %copy.54.seg_q_ref.seg_k_ref, ...), custom_call_target="tpu_custom_call" | custom-call | flops 17179869184 | bytes 16777216 | tf_op jit(solution)/shard_map/attend/pallas_call | solution.py:414
  92.3 2.1 collective-permute-done.13.up2
  95.6 1.3 collective-permute-start.18
  96.9 4.5 %collective-permute-done.16.m1 = bf16[512,256]{1,0:T(8,128)(2,1)S(1)} collective-permute-done((bf16[512,256]{1,0:T(8,128)(2,1)S(1)}, bf16[512,256]{1,0:T(8,128)(2,1)S(1)}, u32[]{:S(2)}, u32[]{:S(2)}) %collective-permute-start.16) | collective-permute-done | bytes 262176 | tf_op jit(solution)/shard_map/ppermute | solution.py:35
  101.4 2.8 collective-permute-done.17.m2
  104.2 4.7 %collective-permute-done.18.m3 = bf16[512,256]{1,0:T(8,128)(2,1)S(1)} collective-permute-done((bf16[512,256]{1,0:T(8,128)(2,1)S(1)}, bf16[512,256]{1,0:T(8,128)(2,1)S(1)}, u32[]{:S(2)}, u32[]{:S(2)}) %collective-permute-start.18) | collective-permute-done | bytes 262176 | tf_op jit(solution)/shard_map/ppermute | solution.py:35
  110.8 30.5 %middle.1 = (bf16[512,768]{1,0:T(8,128)(2,1)S(1)}, f32[512,768]{1,0:T(8,128)}, bf16[4,512,256]{2,1,0:T(8,128)(2,1)S(1)}, bf16[2,768,768]{2,1,0:T(8,128)(2,1)}, b...) custom-call(bf16[512,768]{1,0:T(8,128)(2,1)S(1)} %bitcast.159, ...), custom_call_target="tpu_custom_call" | custom-call | flops 18119393280 | bytes 7077888 | tf_op jit(solution)/shard_map/middle/pallas_call | solution.py:595
  143.4 1.5 collective-permute-start.25
  144.9 2.7 collective-permute-done.22
  148.3 1.8 pad_maximum_fusion.1
  151.1 2.0 add_convert_fusion.1
  154.1 3.4 %collective-permute-done.25 = bf16[512,256]{1,0:T(8,128)(2,1)} collective-permute-done((bf16[512,256]{1,0:T(8,128)(2,1)}, bf16[512,256]{1,0:T(8,128)(2,1)}, u32[]{:S(2)}, u32[]{:S(2)}) %collective-permute-start.25) | collective-permute-done | bytes 262176 | tf_op jit(solution)/shard_map/ppermute | solution.py:35
  157.6 1.2 pad_maximum_fusion.6.do_ref
  158.7 1.6 slice_bitcast_fusion
  163.3 2.9 collective-permute-start.29
  166.2 1.8 collective-permute-start.30
  168.0 24.1 %attend_back_2_4.1 = (bf16[4,2,128,768]{3,2,1,0:T(8,128)(2,1)S(1)}, f32[1024,512]{1,0:T(8,128)}) custom-call(s32[2]{0:T(128)S(1)} %pad_add_fusion.where_ref, s32[4]{0:T(128)S(1)} %get-tuple-element.139.full_ref, s32[4]{0:T(128)S(1)} %get-tuple-element.138.high_ref, s32[4,1,512]{2,1,0:T(1,128)S(1)} %bitcast.167, s32[2048,1]{1,0:T(8,128)S(1)} %copy.54.seg_q_ref.seg_k_ref, ...), custom_call_target="tpu_custom_call" | custom-call | flops 12884901888 | bytes 33554432 | tf_op jit(solution)/shard_map/attend_back_2_4/pallas_call | solution.py:451
  194.4 1.5 copy-done.9
  196.5 1.1 copy-done.24
  197.6 1.4 convolution_convert_fusion.1
  199.9 12.6 %attend_back_0_2.1 = bf16[4,2,128,768]{3,2,1,0:T(8,128)(2,1)S(1)} custom-call(s32[2]{0:T(128)S(1)} %pad_add_fusion.where_ref, s32[4]{0:T(128)S(1)} %get-tuple-element.139.full_ref, s32[4]{0:T(128)S(1)} %get-tuple-element.138.high_ref, s32[4,1,512]{2,1,0:T(1,128)S(1)} %bitcast.168, s32[2048,1]{1,0:T(8,128)S(1)} %copy.54.seg_q_ref.seg_k_ref, ...), custom_call_target="tpu_custom_call" | custom-call | flops 12884901888 | bytes 33554432 | tf_op jit(solution)/shard_map/attend_back_0_2/pallas_call | solution.py:451
  213.4 2.9 collective-permute-done.32
  216.5 1.4 convolution_convert_fusion
  220.2 1.2 collective-permute-start.40
  224.3 1.2 collective-permute-start.39
  226.3 3.0 fusion.13
  229.4 1.5 fusion.3
  231.8 1.7 collective-permute-start.52
  233.7 3.7 %collective-permute-done.40 = bf16[2,216,768]{2,1,0:T(8,128)(2,1)} collective-permute-done((bf16[2,216,768]{2,1,0:T(8,128)(2,1)}, bf16[2,216,768]{2,1,0:T(8,128)(2,1)}, u32[]{:S(2)}, u32[]{:S(2)}) %collective-permute-start.40) | collective-permute-done | bytes 663584 | tf_op jit(solution)/shard_map/ppermute | solution.py:35
  237.4 1.2 fusion.15
  238.7 2.6 collective-permute-start.41
  242.5 1.3 collective-permute-done.38
  247.2 1.1 fusion.18
  249.3 6.8 %collective-permute-done.41 = bf16[216,768]{1,0:T(8,128)(2,1)S(1)} collective-permute-done((bf16[216,768]{1,0:T(8,128)(2,1)S(1)}, bf16[216,768]{1,0:T(8,128)(2,1)S(1)}, u32[]{:S(2)}, u32[]{:S(2)}) %collective-permute-start.41) | collective-permute-done | bytes 331808 | tf_op jit(solution)/shard_map/ppermute | solution.py:35
  256.3 3.6 %collective-permute-start.42 = (bf16[1,128,768]{2,1,0:T(8,128)(2,1)S(1)}, bf16[1,128,768]{2,1,0:T(8,128)(2,1)S(1)}, u32[]{:S(2)}, u32[]{:S(2)}) collective-permute-start(bf16[1,128,768]{2,1,0:T(8,128)(2,1)S(1)} %get-tuple-element.170), channel_id=1, source_target_pairs={{4,0},{8,4},{12,8},{0,12},{5,1},{9,5},{13,9},{1,13},{6,2},{10,6},{... | collective-permute-start | bytes 589832 | tf_op jit(solution)/shard_map/ppermute | solution.py:155
  260.5 2.3 collective-permute-start.57
  262.9 4.3 %collective-permute-start.54 = (bf16[72,768]{1,0:T(8,128)(2,1)S(1)}, bf16[72,768]{1,0:T(8,128)(2,1)S(1)}, u32[]{:S(2)}, u32[]{:S(2)}) collective-permute-start(bf16[72,768]{1,0:T(8,128)(2,1)S(1)} %dynamic-slice_bitcast_fusion.9), channel_id=1, source_target_pairs={{0,8},{4,12},{8,0},{12,4},{1,9},{5,13},{9,1},{13,5},{2,10},{6,14},... | collective-permute-start | bytes 331784 | tf_op jit(solution)/shard_map/ppermute | solution.py:35
  267.3 19.1 %collective-permute-done.43 = bf16[1,128,768]{2,1,0:T(8,128)(2,1)S(1)} collective-permute-done((bf16[1,128,768]{2,1,0:T(8,128)(2,1)S(1)}, bf16[1,128,768]{2,1,0:T(8,128)(2,1)S(1)}, u32[]{:S(2)}, u32[]{:S(2)}) %collective-permute-start.43) | collective-permute-done | bytes 196640 | tf_op jit(solution)/shard_map/ppermute | solution.py:155
  287.2 1.4 collective-permute-start.45
  288.7 6.2 %collective-permute-done.54 = bf16[72,768]{1,0:T(8,128)(2,1)S(1)} collective-permute-done((bf16[72,768]{1,0:T(8,128)(2,1)S(1)}, bf16[72,768]{1,0:T(8,128)(2,1)S(1)}, u32[]{:S(2)}, u32[]{:S(2)}) %collective-permute-start.54) | collective-permute-done | bytes 110624 | tf_op jit(solution)/shard_map/ppermute | solution.py:35
  295.0 3.0 collective-permute-start.49
  298.0 7.2 %collective-permute-start.50 = (f32[72,128]{1,0:T(8,128)S(1)}, f32[72,128]{1,0:T(8,128)S(1)}, u32[]{:S(2)}, u32[]{:S(2)}) collective-permute-start(f32[72,128]{1,0:T(8,128)S(1)} %add_add_fusion.1), channel_id=1, source_target_pairs={{0,12},{4,8},{8,4},{12,0},{1,13},{5,9},{9,5},{13,1},{2,14},{6,10},... | collective-permute-start | bytes 110600 | tf_op jit(solution)/shard_map/ppermute | solution.py:35
  305.4 2.1 collective-permute-start.58
  308.4 1.2 collective-permute-done.48
  310.0 3.7 %collective-permute-done.51 = f32[72,128]{1,0:T(8,128)S(1)} collective-permute-done((f32[72,128]{1,0:T(8,128)S(1)}, f32[72,128]{1,0:T(8,128)S(1)}, u32[]{:S(2)}, u32[]{:S(2)}) %collective-permute-start.51) | collective-permute-done | bytes 36896 | tf_op jit(solution)/shard_map/ppermute | solution.py:35
  315.6 7.9 %collective-permute-done.56 = bf16[2,72,768]{2,1,0:T(8,128)(2,1)S(1)} collective-permute-done((bf16[2,72,768]{2,1,0:T(8,128)(2,1)S(1)}, bf16[2,72,768]{2,1,0:T(8,128)(2,1)S(1)}, u32[]{:S(2)}, u32[]{:S(2)}) %collective-permute-start.56) | collective-permute-done | bytes 221216 | tf_op jit(solution)/shard_map/ppermute | solution.py:35
  324.6 1.2 select_bitcast_fusion.1
  327.0 1.6 fusion.52
  (298 shorter events, 63.9 us)
Async XLA Ops:
  0.7 18.8 %copy-start.13 = (bf16[384,768]{1,0:T(8,128)(2,1)S(1)}, bf16[384,768]{1,0:T(8,128)(2,1)}, u32[]{:S(2)}) copy-start(bf16[384,768]{1,0:T(8,128)(2,1)} %param.25) | copy-start | bytes 1769476
  0.7 18.8 %copy-start.22 = (bf16[96,768]{1,0:T(8,128)(2,1)S(1)}, bf16[96,768]{1,0:T(8,128)(2,1)}, u32[]{:S(2)}) copy-start(bf16[96,768]{1,0:T(8,128)(2,1)} %param.21) | copy-start | bytes 442372
  6.9 13.7 %collective-permute-start.4 = (bf16[1,8,384]{2,1,0:T(8,128)(2,1)}, bf16[1,8,384]{2,1,0:T(8,128)(2,1)}, u32[]{:S(2)}, u32[]{:S(2)}) collective-permute-start(bf16[1,8,384]{2,1,0:T(8,128)(2,1)} %bitcast.7), channel_id=1, source_target_pairs={{0,16},{16,0},{1,17},{17,1},{2,18},{18,2},{3,19},{19,3},{4,20},{20... | collective-permute-start | bytes 18440 | tf_op jit(solution)/shard_map/ppermute | solution.py:35
  12.0 21.1 %collective-permute-start = (bf16[1,128,768]{2,1,0:T(8,128)(2,1)}, bf16[1,128,768]{2,1,0:T(8,128)(2,1)}, u32[]{:S(2)}, u32[]{:S(2)}) collective-permute-start(bf16[1,128,768]{2,1,0:T(8,128)(2,1)} %get-tuple-element.185), channel_id=1, source_target_pairs={{0,4},{4,8},{8,12},{12,0},{1,5},{5,9},{9,13},{13,1},{2,6},{6,10},{... | collective-permute-start | bytes 589832 | tf_op jit(solution)/shard_map/ppermute | solution.py:155
  13.6 22.0 %collective-permute-start.1 = (bf16[1,128,768]{2,1,0:T(8,128)(2,1)}, bf16[1,128,768]{2,1,0:T(8,128)(2,1)}, u32[]{:S(2)}, u32[]{:S(2)}) collective-permute-start(bf16[1,128,768]{2,1,0:T(8,128)(2,1)} %get-tuple-element.187), channel_id=1, source_target_pairs={{0,8},{4,12},{8,0},{12,4},{1,9},{5,13},{9,1},{13,5},{2,10},{6,14},... | collective-permute-start | bytes 589832 | tf_op jit(solution)/shard_map/ppermute | solution.py:155
  16.2 20.4 %collective-permute-start.2 = (bf16[1,128,768]{2,1,0:T(8,128)(2,1)}, bf16[1,128,768]{2,1,0:T(8,128)(2,1)S(1)}, u32[]{:S(2)}, u32[]{:S(2)}) collective-permute-start(bf16[1,128,768]{2,1,0:T(8,128)(2,1)} %get-tuple-element.184), channel_id=1, source_target_pairs={{0,12},{4,0},{8,4},{12,8},{1,13},{5,1},{9,5},{13,9},{2,14},{6,2},{... | collective-permute-start | bytes 589832 | tf_op jit(solution)/shard_map/ppermute | solution.py:155
  17.5 20.4 %collective-permute-start.3 = (bf16[384,768]{1,0:T(8,128)(2,1)}, bf16[384,768]{1,0:T(8,128)(2,1)}, u32[]{:S(2)}, u32[]{:S(2)}) collective-permute-start(bf16[384,768]{1,0:T(8,128)(2,1)} %param.27), channel_id=1, source_target_pairs={{0,2},{1,3},{2,0},{3,1},{4,6},{5,7},{6,4},{7,5},{8,10},{9,11},{10,... | collective-permute-start | bytes 1769480 | tf_op jit(solution)/shard_map/ppermute | solution.py:35
  20.6 16.0 %collective-permute-start.12 = (bf16[3,96,768]{2,1,0:T(8,128)(2,1)}, bf16[3,96,768]{2,1,0:T(8,128)(2,1)}, u32[]{:S(2)}, u32[]{:S(2)}) collective-permute-start(bf16[3,96,768]{2,1,0:T(8,128)(2,1)} %param.19), channel_id=1, source_target_pairs={{0,16},{16,0},{1,17},{17,1},{2,18},{18,2},{3,19},{19,3},{4,20},{20... | collective-permute-start | bytes 1327112 | tf_op jit(solution)/shard_map/ppermute | solution.py:35
  33.1 16.6 %collective-permute-start.8 = (bf16[480,768]{1,0:T(8,128)(2,1)S(1)}, bf16[480,768]{1,0:T(8,128)(2,1)S(1)}, u32[]{:S(2)}, u32[]{:S(2)}) collective-permute-start(bf16[480,768]{1,0:T(8,128)(2,1)S(1)} %pad_maximum_fusion.7), channel_id=1, source_target_pairs={{0,16},{16,0},{1,17},{17,1},{2,18},{18,2},{3,19},{19,3},{4,20},{20... | collective-permute-start | bytes 2211848 | tf_op jit(solution)/shard_map/ppermute | solution.py:35
  37.9 23.4 %copy-start.23 = (bf16[3,256,768]{2,1,0:T(8,128)(2,1)}, bf16[3,256,768]{2,1,0:T(8,128)(2,1)S(1)}, u32[]{:S(2)}) copy-start(bf16[3,256,768]{2,1,0:T(8,128)(2,1)S(1)} %fusion.16) | copy-start | bytes 3538948
  38.9 17.4 %collective-permute-start.6 = (bf16[512,768]{1,0:T(8,128)(2,1)S(1)}, bf16[512,768]{1,0:T(8,128)(2,1)S(1)}, u32[]{:S(2)}, u32[]{:S(2)}) collective-permute-start(bf16[512,768]{1,0:T(8,128)(2,1)S(1)} %add_convert_fusion.4), channel_id=1, source_target_pairs={{0,2},{1,3},{2,0},{3,1},{4,6},{5,7},{6,4},{7,5},{8,10},{9,11},{10,... | collective-permute-start | bytes 2359304 | tf_op jit(solution)/shard_map/ppermute | solution.py:35
  39.5 19.3 %collective-permute-start.5 = (bf16[512,768]{1,0:T(8,128)(2,1)S(1)}, bf16[512,768]{1,0:T(8,128)(2,1)S(1)}, u32[]{:S(2)}, u32[]{:S(2)}) collective-permute-start(bf16[512,768]{1,0:T(8,128)(2,1)S(1)} %add_convert_fusion.4), channel_id=1, source_target_pairs={{0,1},{1,0},{2,3},{3,2},{4,5},{5,4},{6,7},{7,6},{8,9},{9,8},{10,11... | collective-permute-start | bytes 2359304 | tf_op jit(solution)/shard_map/ppermute | solution.py:35
  39.7 18.6 %collective-permute-start.9 = (bf16[1,128,768]{2,1,0:T(8,128)(2,1)S(1)}, bf16[1,128,768]{2,1,0:T(8,128)(2,1)S(1)}, u32[]{:S(2)}, u32[]{:S(2)}) collective-permute-start(bf16[1,128,768]{2,1,0:T(8,128)(2,1)S(1)} %get-tuple-element.182), channel_id=1, source_target_pairs={{0,4},{4,8},{8,12},{12,0},{1,5},{5,9},{9,13},{13,1},{2,6},{6,10},{... | collective-permute-start | bytes 589832 | tf_op jit(solution)/shard_map/ppermute | solution.py:155
  40.4 17.9 %collective-permute-start.10 = (bf16[1,128,768]{2,1,0:T(8,128)(2,1)S(1)}, bf16[1,128,768]{2,1,0:T(8,128)(2,1)S(1)}, u32[]{:S(2)}, u32[]{:S(2)}) collective-permute-start(bf16[1,128,768]{2,1,0:T(8,128)(2,1)S(1)} %get-tuple-element.181), channel_id=1, source_target_pairs={{0,8},{4,12},{8,0},{12,4},{1,9},{5,13},{9,1},{13,5},{2,10},{6,14},... | collective-permute-start | bytes 589832 | tf_op jit(solution)/shard_map/ppermute | solution.py:155
  49.7 9.1 %collective-permute-start.11 = (bf16[1,128,768]{2,1,0:T(8,128)(2,1)S(1)}, bf16[1,128,768]{2,1,0:T(8,128)(2,1)S(1)}, u32[]{:S(2)}, u32[]{:S(2)}) collective-permute-start(bf16[1,128,768]{2,1,0:T(8,128)(2,1)S(1)} %get-tuple-element.180), channel_id=1, source_target_pairs={{0,12},{4,0},{8,4},{12,8},{1,13},{5,1},{9,5},{13,9},{2,14},{6,2},{... | collective-permute-start | bytes 589832 | tf_op jit(solution)/shard_map/ppermute | solution.py:155
  56.3 2.6 collective-permute-start.7
  59.3 35.1 %collective-permute-start.13 = (bf16[976,768]{1,0:T(8,128)(2,1)}, bf16[976,768]{1,0:T(8,128)(2,1)S(1)}, u32[]{:S(2)}, u32[]{:S(2)}) collective-permute-start(bf16[976,768]{1,0:T(8,128)(2,1)} %pad_dynamic-update-slice_fusion.up0), channel_id=1, source_target_pairs={{0,2},{1,3},{2,0},{3,1},{4,6},{5,7},{6,4},{7,5},{8,10},{9,11},{10,... | collective-permute-start | bytes 4497416 | tf_op jit(solution)/shard_map/ppermute | solution.py:35
  60.2 34.2 %collective-permute-start.14 = (bf16[976,768]{1,0:T(8,128)(2,1)}, bf16[976,768]{1,0:T(8,128)(2,1)}, u32[]{:S(2)}, u32[]{:S(2)}) collective-permute-start(bf16[976,768]{1,0:T(8,128)(2,1)} %pad_dynamic-update-slice_fusion.up0), channel_id=1, source_target_pairs={{0,1},{1,0},{2,3},{3,2},{4,5},{5,4},{6,7},{7,6},{8,9},{9,8},{10,11... | collective-permute-start | bytes 4497416 | tf_op jit(solution)/shard_map/ppermute | solution.py:35
  60.2 31.2 %collective-permute-start.15 = (bf16[2,384,768]{2,1,0:T(8,128)(2,1)S(1)}, bf16[2,384,768]{2,1,0:T(8,128)(2,1)S(1)}, u32[]{:S(2)}, u32[]{:S(2)}) collective-permute-start(bf16[2,384,768]{2,1,0:T(8,128)(2,1)S(1)} %pad_maximum_fusion.5), channel_id=1, source_target_pairs={{0,16},{16,0},{1,17},{17,1},{2,18},{18,2},{3,19},{19,3},{4,20},{20... | collective-permute-start | bytes 3538952 | tf_op jit(solution)/shard_map/ppermute | solution.py:35
  64.2 27.1 %copy-start.6 = (bf16[2048,768]{1,0:T(8,128)(2,1)}, bf16[2048,768]{1,0:T(8,128)(2,1)S(1)}, u32[]{:S(2)}) copy-start(bf16[2048,768]{1,0:T(8,128)(2,1)S(1)} %add_convert_fusion) | copy-start | bytes 9437188
  94.3 14.6 %collective-permute-start.20 = (bf16[2,768,768]{2,1,0:T(8,128)(2,1)S(1)}, bf16[2,768,768]{2,1,0:T(8,128)(2,1)S(1)}, u32[]{:S(2)}, u32[]{:S(2)}) collective-permute-start(bf16[2,768,768]{2,1,0:T(8,128)(2,1)S(1)} %pad_maximum_fusion.2.down_even), channel_id=1, source_target_pairs={{0,1},{1,0},{2,3},{3,2},{4,5},{5,4},{6,7},{7,6},{8,9},{9,8},{10,11... | collective-permute-start | bytes 7077896 | tf_op jit(solution)/shard_map/ppermute | solution.py:35
  94.3 14.6 %collective-permute-start.19 = (bf16[976,768]{1,0:T(8,128)(2,1)S(1)}, bf16[976,768]{1,0:T(8,128)(2,1)S(1)}, u32[]{:S(2)}, u32[]{:S(2)}) collective-permute-start(bf16[976,768]{1,0:T(8,128)(2,1)S(1)} %collective-permute-done.13.up2), channel_id=1, source_target_pairs={{0,1},{1,0},{2,3},{3,2},{4,5},{5,4},{6,7},{7,6},{8,9},{9,8},{10,11... | collective-permute-start | bytes 4497416 | tf_op jit(solution)/shard_map/ppermute | solution.py:35
  94.9 6.4 %collective-permute-start.16 = (bf16[512,256]{1,0:T(8,128)(2,1)S(1)}, bf16[512,256]{1,0:T(8,128)(2,1)S(1)}, u32[]{:S(2)}, u32[]{:S(2)}) collective-permute-start(bf16[512,256]{1,0:T(8,128)(2,1)S(1)} %bitcast.199), channel_id=1, source_target_pairs={{0,1},{1,0},{2,3},{3,2},{4,5},{5,4},{6,7},{7,6},{8,9},{9,8},{10,11... | collective-permute-start | bytes 786440 | tf_op jit(solution)/shard_map/ppermute | solution.py:35
  95.1 9.1 %collective-permute-start.17 = (bf16[512,256]{1,0:T(8,128)(2,1)S(1)}, bf16[512,256]{1,0:T(8,128)(2,1)S(1)}, u32[]{:S(2)}, u32[]{:S(2)}) collective-permute-start(bf16[512,256]{1,0:T(8,128)(2,1)S(1)} %bitcast.198), channel_id=1, source_target_pairs={{0,2},{1,3},{2,0},{3,1},{4,6},{5,7},{6,4},{7,5},{8,10},{9,11},{10,... | collective-permute-start | bytes 786440 | tf_op jit(solution)/shard_map/ppermute | solution.py:35
  95.6 13.3 %collective-permute-start.18 = (bf16[512,256]{1,0:T(8,128)(2,1)S(1)}, bf16[512,256]{1,0:T(8,128)(2,1)S(1)}, u32[]{:S(2)}, u32[]{:S(2)}) collective-permute-start(bf16[512,256]{1,0:T(8,128)(2,1)S(1)} %bitcast.197), channel_id=1, source_target_pairs={{0,3},{1,2},{2,1},{3,0},{4,7},{5,6},{6,5},{7,4},{8,11},{9,10},{10,... | collective-permute-start | bytes 786440 | tf_op jit(solution)/shard_map/ppermute | solution.py:35
  141.3 6.4 %collective-permute-start.21 = (bf16[2,768,768]{2,1,0:T(8,128)(2,1)}, bf16[2,768,768]{2,1,0:T(8,128)(2,1)S(1)}, u32[]{:S(2)}, u32[]{:S(2)}) collective-permute-start(bf16[2,768,768]{2,1,0:T(8,128)(2,1)} %get-tuple-element.84), channel_id=1, source_target_pairs={{0,1},{1,0},{2,3},{3,2},{4,5},{5,4},{6,7},{7,6},{8,9},{9,8},{10,11... | collective-permute-start | bytes 7077896 | tf_op jit(solution)/shard_map/ppermute | solution.py:35
  141.6 8.7 %collective-permute-start.23 = (bf16[2,768,768]{2,1,0:T(8,128)(2,1)}, bf16[2,768,768]{2,1,0:T(8,128)(2,1)S(1)}, u32[]{:S(2)}, u32[]{:S(2)}) collective-permute-start(bf16[2,768,768]{2,1,0:T(8,128)(2,1)} %get-tuple-element.88), channel_id=1, source_target_pairs={{0,1},{1,0},{2,3},{3,2},{4,5},{5,4},{6,7},{7,6},{8,9},{9,8},{10,11... | collective-permute-start | bytes 7077896 | tf_op jit(solution)/shard_map/ppermute | solution.py:35
  141.9 5.7 %collective-permute-start.22 = (bf16[2,192,768]{2,1,0:T(8,128)(2,1)S(1)}, bf16[2,192,768]{2,1,0:T(8,128)(2,1)S(1)}, u32[]{:S(2)}, u32[]{:S(2)}) collective-permute-start(bf16[2,192,768]{2,1,0:T(8,128)(2,1)S(1)} %get-tuple-element.86), channel_id=1, source_target_pairs={{0,1},{1,0},{2,3},{3,2},{4,5},{5,4},{6,7},{7,6},{8,9},{9,8},{10,11... | collective-permute-start | bytes 1769480 | tf_op jit(solution)/shard_map/ppermute | solution.py:35
  143.0 11.1 %collective-permute-start.26 = (bf16[512,256]{1,0:T(8,128)(2,1)}, bf16[512,256]{1,0:T(8,128)(2,1)S(1)}, u32[]{:S(2)}, u32[]{:S(2)}) collective-permute-start(bf16[512,256]{1,0:T(8,128)(2,1)} %get-tuple-element.159), channel_id=1, source_target_pairs={{0,3},{1,2},{2,1},{3,0},{4,7},{5,6},{6,5},{7,4},{8,11},{9,10},{10,... | collective-permute-start | bytes 786440 | tf_op jit(solution)/shard_map/ppermute | solution.py:35
  143.4 14.2 %collective-permute-start.25 = (bf16[512,256]{1,0:T(8,128)(2,1)}, bf16[512,256]{1,0:T(8,128)(2,1)}, u32[]{:S(2)}, u32[]{:S(2)}) collective-permute-start(bf16[512,256]{1,0:T(8,128)(2,1)} %get-tuple-element.160), channel_id=1, source_target_pairs={{0,2},{1,3},{2,0},{3,1},{4,6},{5,7},{6,4},{7,5},{8,10},{9,11},{10,... | collective-permute-start | bytes 786440 | tf_op jit(solution)/shard_map/ppermute | solution.py:35
  153.1 4.5 %collective-permute-start.24 = (bf16[512,256]{1,0:T(8,128)(2,1)S(1)}, bf16[512,256]{1,0:T(8,128)(2,1)}, u32[]{:S(2)}, u32[]{:S(2)}) collective-permute-start(bf16[512,256]{1,0:T(8,128)(2,1)S(1)} %get-tuple-element.89), channel_id=1, source_target_pairs={{0,1},{1,0},{2,3},{3,2},{4,5},{5,4},{6,7},{7,6},{8,9},{9,8},{10,11... | collective-permute-start | bytes 786440 | tf_op jit(solution)/shard_map/ppermute | solution.py:35
  160.4 34.1 %collective-permute-start.27 = (bf16[960,768]{1,0:T(8,128)(2,1)S(1)}, bf16[960,768]{1,0:T(8,128)(2,1)S(1)}, u32[]{:S(2)}, u32[]{:S(2)}) collective-permute-start(bf16[960,768]{1,0:T(8,128)(2,1)S(1)} %slice_bitcast_fusion), channel_id=1, source_target_pairs={{0,2},{1,3},{2,0},{3,1},{4,6},{5,7},{6,4},{7,5},{8,10},{9,11},{10,... | collective-permute-start | bytes 4423688 | tf_op jit(solution)/shard_map/ppermute | solution.py:35
  161.1 33.1 %collective-permute-start.28 = (bf16[2,384,768]{2,1,0:T(8,128)(2,1)S(1)}, bf16[2,384,768]{2,1,0:T(8,128)(2,1)S(1)}, u32[]{:S(2)}, u32[]{:S(2)}) collective-permute-start(bf16[2,384,768]{2,1,0:T(8,128)(2,1)S(1)} %dynamic-slice_bitcast_fusion), channel_id=1, source_target_pairs={{0,16},{16,0},{1,17},{17,1},{2,18},{18,2},{3,19},{19,3},{4,20},{20... | collective-permute-start | bytes 3538952 | tf_op jit(solution)/shard_map/ppermute | solution.py:35
  163.3 28.7 %collective-permute-start.29 = (bf16[1,128,768]{2,1,0:T(8,128)(2,1)S(1)}, bf16[1,128,768]{2,1,0:T(8,128)(2,1)S(1)}, u32[]{:S(2)}, u32[]{:S(2)}) collective-permute-start(bf16[1,128,768]{2,1,0:T(8,128)(2,1)S(1)} %get-tuple-element.178), channel_id=1, source_target_pairs={{4,0},{8,4},{12,8},{0,12},{5,1},{9,5},{13,9},{1,13},{6,2},{10,6},{... | collective-permute-start | bytes 589832 | tf_op jit(solution)/shard_map/ppermute | solution.py:155
  166.2 26.6 %collective-permute-start.30 = (bf16[1,128,768]{2,1,0:T(8,128)(2,1)S(1)}, bf16[1,128,768]{2,1,0:T(8,128)(2,1)S(1)}, u32[]{:S(2)}, u32[]{:S(2)}) collective-permute-start(bf16[1,128,768]{2,1,0:T(8,128)(2,1)S(1)} %get-tuple-element.177), channel_id=1, source_target_pairs={{8,0},{12,4},{0,8},{4,12},{9,1},{13,5},{1,9},{5,13},{10,2},{14,6},... | collective-permute-start | bytes 589832 | tf_op jit(solution)/shard_map/ppermute | solution.py:155
  168.0 25.5 %collective-permute-start.31 = (bf16[1,128,768]{2,1,0:T(8,128)(2,1)S(1)}, bf16[1,128,768]{2,1,0:T(8,128)(2,1)S(1)}, u32[]{:S(2)}, u32[]{:S(2)}) collective-permute-start(bf16[1,128,768]{2,1,0:T(8,128)(2,1)S(1)} %get-tuple-element.176), channel_id=1, source_target_pairs={{12,0},{0,4},{4,8},{8,12},{13,1},{1,5},{5,9},{9,13},{14,2},{2,6},{... | collective-permute-start | bytes 589832 | tf_op jit(solution)/shard_map/ppermute | solution.py:155
  199.2 17.1 %collective-permute-start.32 = (bf16[480,768]{1,0:T(8,128)(2,1)S(1)}, bf16[480,768]{1,0:T(8,128)(2,1)S(1)}, u32[]{:S(2)}, u32[]{:S(2)}) collective-permute-start(bf16[480,768]{1,0:T(8,128)(2,1)S(1)} %pad_maximum_fusion.8), channel_id=1, source_target_pairs={{0,16},{16,0},{1,17},{17,1},{2,18},{18,2},{3,19},{19,3},{4,20},{20... | collective-permute-start | bytes 2211848 | tf_op jit(solution)/shard_map/ppermute | solution.py:35
  199.3 14.0 %collective-permute-start.33 = (bf16[384,768]{1,0:T(8,128)(2,1)S(1)}, bf16[384,768]{1,0:T(8,128)(2,1)S(1)}, u32[]{:S(2)}, u32[]{:S(2)}) collective-permute-start(bf16[384,768]{1,0:T(8,128)(2,1)S(1)} %slice_bitcast_fusion.1), channel_id=1, source_target_pairs={{0,2},{1,3},{2,0},{3,1},{4,6},{5,7},{6,4},{7,5},{8,10},{9,11},{10,... | collective-permute-start | bytes 1769480 | tf_op jit(solution)/shard_map/ppermute | solution.py:35
  218.0 3.4 %collective-permute-start.35 = (bf16[256,768]{1,0:T(8,128)(2,1)S(1)}, bf16[256,768]{1,0:T(8,128)(2,1)S(1)}, u32[]{:S(2)}, u32[]{:S(2)}) collective-permute-start(bf16[256,768]{1,0:T(8,128)(2,1)S(1)} %get-tuple-element.152), channel_id=1, source_target_pairs={{0,1},{1,0},{2,3},{3,2},{4,5},{5,4},{6,7},{7,6},{8,9},{9,8},{10,11... | collective-permute-start | bytes 1179656 | tf_op jit(solution)/shard_map/ppermute | solution.py:35
  218.0 3.4 %collective-permute-start.34 = (bf16[256,768]{1,0:T(8,128)(2,1)S(1)}, bf16[256,768]{1,0:T(8,128)(2,1)S(1)}, u32[]{:S(2)}, u32[]{:S(2)}) collective-permute-start(bf16[256,768]{1,0:T(8,128)(2,1)S(1)} %get-tuple-element.153), channel_id=1, source_target_pairs={{0,1},{1,0},{2,3},{3,2},{4,5},{5,4},{6,7},{7,6},{8,9},{9,8},{10,11... | collective-permute-start | bytes 1179656 | tf_op jit(solution)/shard_map/ppermute | solution.py:35
  218.6 3.9 %collective-permute-start.37 = (bf16[256,768]{1,0:T(8,128)(2,1)S(1)}, bf16[256,768]{1,0:T(8,128)(2,1)S(1)}, u32[]{:S(2)}, u32[]{:S(2)}) collective-permute-start(bf16[256,768]{1,0:T(8,128)(2,1)S(1)} %get-tuple-element.148), channel_id=1, source_target_pairs={{0,1},{1,0},{2,3},{3,2},{4,5},{5,4},{6,7},{7,6},{8,9},{9,8},{10,11... | collective-permute-start | bytes 1179656 | tf_op jit(solution)/shard_map/ppermute | solution.py:35
  218.7 3.7 %collective-permute-start.36 = (bf16[256,768]{1,0:T(8,128)(2,1)S(1)}, bf16[256,768]{1,0:T(8,128)(2,1)S(1)}, u32[]{:S(2)}, u32[]{:S(2)}) collective-permute-start(bf16[256,768]{1,0:T(8,128)(2,1)S(1)} %get-tuple-element.149), channel_id=1, source_target_pairs={{0,1},{1,0},{2,3},{3,2},{4,5},{5,4},{6,7},{7,6},{8,9},{9,8},{10,11... | collective-permute-start | bytes 1179656 | tf_op jit(solution)/shard_map/ppermute | solution.py:35
  220.2 17.2 %collective-permute-start.40 = (bf16[2,216,768]{2,1,0:T(8,128)(2,1)}, bf16[2,216,768]{2,1,0:T(8,128)(2,1)}, u32[]{:S(2)}, u32[]{:S(2)}) collective-permute-start(bf16[2,216,768]{2,1,0:T(8,128)(2,1)} %dynamic-slice_bitcast_fusion.1), channel_id=1, source_target_pairs={{0,4},{4,0},{8,12},{12,8},{1,5},{5,1},{9,13},{13,9},{2,6},{6,2},{1... | collective-permute-start | bytes 1990664 | tf_op jit(solution)/shard_map/ppermute | solution.py:35
  224.3 17.1 %collective-permute-start.39 = (bf16[256,768]{1,0:T(8,128)(2,1)}, bf16[256,768]{1,0:T(8,128)(2,1)}, u32[]{:S(2)}, u32[]{:S(2)}) collective-permute-start(bf16[256,768]{1,0:T(8,128)(2,1)} %get-tuple-element.114), channel_id=1, source_target_pairs={{0,2},{1,3},{2,0},{3,1},{4,6},{5,7},{6,4},{7,5},{8,10},{9,11},{10,... | collective-permute-start | bytes 1179656 | tf_op jit(solution)/shard_map/ppermute | solution.py:35
  225.5 18.4 %collective-permute-start.38 = (bf16[256,768]{1,0:T(8,128)(2,1)}, bf16[256,768]{1,0:T(8,128)(2,1)}, u32[]{:S(2)}, u32[]{:S(2)}) collective-permute-start(bf16[256,768]{1,0:T(8,128)(2,1)} %get-tuple-element.112), channel_id=1, source_target_pairs={{0,2},{1,3},{2,0},{3,1},{4,6},{5,7},{6,4},{7,5},{8,10},{9,11},{10,... | collective-permute-start | bytes 1179656 | tf_op jit(solution)/shard_map/ppermute | solution.py:35
  231.8 15.4 %collective-permute-start.52 = (bf16[3,96,768]{2,1,0:T(8,128)(2,1)}, bf16[3,96,768]{2,1,0:T(8,128)(2,1)}, u32[]{:S(2)}, u32[]{:S(2)}) collective-permute-start(bf16[3,96,768]{2,1,0:T(8,128)(2,1)} %dynamic-slice_bitcast_fusion.4), channel_id=1, source_target_pairs={{0,16},{16,0},{1,17},{17,1},{2,18},{18,2},{3,19},{19,3},{4,20},{20... | collective-permute-start | bytes 1327112 | tf_op jit(solution)/shard_map/ppermute | solution.py:35
  238.7 17.4 %collective-permute-start.41 = (bf16[216,768]{1,0:T(8,128)(2,1)S(1)}, bf16[216,768]{1,0:T(8,128)(2,1)S(1)}, u32[]{:S(2)}, u32[]{:S(2)}) collective-permute-start(bf16[216,768]{1,0:T(8,128)(2,1)S(1)} %dynamic-slice_bitcast_fusion.5), channel_id=1, source_target_pairs={{0,8},{4,12},{8,0},{12,4},{1,9},{5,13},{9,1},{13,5},{2,10},{6,14},... | collective-permute-start | bytes 995336 | tf_op jit(solution)/shard_map/ppermute | solution.py:35
  248.4 14.5 %collective-permute-start.53 = (bf16[2,72,768]{2,1,0:T(8,128)(2,1)S(1)}, bf16[2,72,768]{2,1,0:T(8,128)(2,1)S(1)}, u32[]{:S(2)}, u32[]{:S(2)}) collective-permute-start(bf16[2,72,768]{2,1,0:T(8,128)(2,1)S(1)} %dynamic-slice_bitcast_fusion.6), channel_id=1, source_target_pairs={{0,4},{4,0},{8,12},{12,8},{1,5},{5,1},{9,13},{13,9},{2,6},{6,2},{1... | collective-permute-start | bytes 663560 | tf_op jit(solution)/shard_map/ppermute | solution.py:35
  256.3 10.9 %collective-permute-start.42 = (bf16[1,128,768]{2,1,0:T(8,128)(2,1)S(1)}, bf16[1,128,768]{2,1,0:T(8,128)(2,1)S(1)}, u32[]{:S(2)}, u32[]{:S(2)}) collective-permute-start(bf16[1,128,768]{2,1,0:T(8,128)(2,1)S(1)} %get-tuple-element.170), channel_id=1, source_target_pairs={{4,0},{8,4},{12,8},{0,12},{5,1},{9,5},{13,9},{1,13},{6,2},{10,6},{... | collective-permute-start | bytes 589832 | tf_op jit(solution)/shard_map/ppermute | solution.py:155
  259.9 26.5 %collective-permute-start.43 = (bf16[1,128,768]{2,1,0:T(8,128)(2,1)S(1)}, bf16[1,128,768]{2,1,0:T(8,128)(2,1)S(1)}, u32[]{:S(2)}, u32[]{:S(2)}) collective-permute-start(bf16[1,128,768]{2,1,0:T(8,128)(2,1)S(1)} %get-tuple-element.169), channel_id=1, source_target_pairs={{8,0},{12,4},{0,8},{4,12},{9,1},{13,5},{1,9},{5,13},{10,2},{14,6},... | collective-permute-start | bytes 589832 | tf_op jit(solution)/shard_map/ppermute | solution.py:155
  259.9 26.5 %collective-permute-start.44 = (bf16[1,128,768]{2,1,0:T(8,128)(2,1)S(1)}, bf16[1,128,768]{2,1,0:T(8,128)(2,1)S(1)}, u32[]{:S(2)}, u32[]{:S(2)}) collective-permute-start(bf16[1,128,768]{2,1,0:T(8,128)(2,1)S(1)} %get-tuple-element.168), channel_id=1, source_target_pairs={{12,0},{0,4},{4,8},{8,12},{13,1},{1,5},{5,9},{9,13},{14,2},{2,6},{... | collective-permute-start | bytes 589832 | tf_op jit(solution)/shard_map/ppermute | solution.py:155
  260.5 44.7 %collective-permute-start.57 = (bf16[216,768]{1,0:T(8,128)(2,1)S(1)}, bf16[216,768]{1,0:T(8,128)(2,1)S(1)}, u32[]{:S(2)}, u32[]{:S(2)}) collective-permute-start(bf16[216,768]{1,0:T(8,128)(2,1)S(1)} %fusion.21), channel_id=1, source_target_pairs={{0,8},{4,12},{8,0},{12,4},{1,9},{5,13},{9,1},{13,5},{2,10},{6,14},... | collective-permute-start | bytes 995336 | tf_op jit(solution)/shard_map/ppermute | solution.py:35
  262.9 31.9 %collective-permute-start.54 = (bf16[72,768]{1,0:T(8,128)(2,1)S(1)}, bf16[72,768]{1,0:T(8,128)(2,1)S(1)}, u32[]{:S(2)}, u32[]{:S(2)}) collective-permute-start(bf16[72,768]{1,0:T(8,128)(2,1)S(1)} %dynamic-slice_bitcast_fusion.9), channel_id=1, source_target_pairs={{0,8},{4,12},{8,0},{12,4},{1,9},{5,13},{9,1},{13,5},{2,10},{6,14},... | collective-permute-start | bytes 331784 | tf_op jit(solution)/shard_map/ppermute | solution.py:35
  286.5 18.9 %copy-start.26 = (bf16[4,128,768]{2,1,0:T(8,128)(2,1)}, bf16[4,128,768]{2,1,0:T(8,128)(2,1)S(1)}, u32[]{:S(2)}) copy-start(bf16[4,128,768]{2,1,0:T(8,128)(2,1)S(1)} %constant_dynamic-update-slice_fusion) | copy-start | bytes 2359300
  286.5 8.5 %collective-permute-start.46 = (f32[72,128]{1,0:T(8,128)S(1)}, f32[72,128]{1,0:T(8,128)S(1)}, u32[]{:S(2)}, u32[]{:S(2)}) collective-permute-start(f32[72,128]{1,0:T(8,128)S(1)} %pad_maximum_fusion.11), channel_id=1, source_target_pairs={{0,2},{1,3},{2,0},{3,1},{4,6},{5,7},{6,4},{7,5},{8,10},{9,11},{10,... | collective-permute-start | bytes 110600 | tf_op jit(solution)/shard_map/ppermute | solution.py:35
  287.2 7.7 %collective-permute-start.47 = (f32[72,128]{1,0:T(8,128)S(1)}, f32[72,128]{1,0:T(8,128)S(1)}, u32[]{:S(2)}, u32[]{:S(2)}) collective-permute-start(f32[72,128]{1,0:T(8,128)S(1)} %pad_maximum_fusion.11), channel_id=1, source_target_pairs={{0,3},{1,2},{2,1},{3,0},{4,7},{5,6},{6,5},{7,4},{8,11},{9,10},{10,... | collective-permute-start | bytes 110600 | tf_op jit(solution)/shard_map/ppermute | solution.py:35
  287.2 7.7 %collective-permute-start.45 = (f32[72,128]{1,0:T(8,128)S(1)}, f32[72,128]{1,0:T(8,128)S(1)}, u32[]{:S(2)}, u32[]{:S(2)}) collective-permute-start(f32[72,128]{1,0:T(8,128)S(1)} %pad_maximum_fusion.11), channel_id=1, source_target_pairs={{0,1},{1,0},{2,3},{3,2},{4,5},{5,4},{6,7},{7,6},{8,9},{9,8},{10,11... | collective-permute-start | bytes 110600 | tf_op jit(solution)/shard_map/ppermute | solution.py:35
  294.9 10.3 %collective-permute-start.55 = (bf16[72,768]{1,0:T(8,128)(2,1)S(1)}, bf16[72,768]{1,0:T(8,128)(2,1)S(1)}, u32[]{:S(2)}, u32[]{:S(2)}) collective-permute-start(bf16[72,768]{1,0:T(8,128)(2,1)S(1)} %fusion.23), channel_id=1, source_target_pairs={{0,8},{4,12},{8,0},{12,4},{1,9},{5,13},{9,1},{13,5},{2,10},{6,14},... | collective-permute-start | bytes 331784 | tf_op jit(solution)/shard_map/ppermute | solution.py:35
  295.0 12.6 %collective-permute-start.49 = (f32[72,128]{1,0:T(8,128)S(1)}, f32[72,128]{1,0:T(8,128)S(1)}, u32[]{:S(2)}, u32[]{:S(2)}) collective-permute-start(f32[72,128]{1,0:T(8,128)S(1)} %add_add_fusion.1), channel_id=1, source_target_pairs={{0,8},{4,12},{8,0},{12,4},{1,9},{5,13},{9,1},{13,5},{2,10},{6,14},... | collective-permute-start | bytes 110600 | tf_op jit(solution)/shard_map/ppermute | solution.py:35
  298.0 10.4 %collective-permute-start.50 = (f32[72,128]{1,0:T(8,128)S(1)}, f32[72,128]{1,0:T(8,128)S(1)}, u32[]{:S(2)}, u32[]{:S(2)}) collective-permute-start(f32[72,128]{1,0:T(8,128)S(1)} %add_add_fusion.1), channel_id=1, source_target_pairs={{0,12},{4,8},{8,4},{12,0},{1,13},{5,9},{9,5},{13,1},{2,14},{6,10},... | collective-permute-start | bytes 110600 | tf_op jit(solution)/shard_map/ppermute | solution.py:35
  305.2 4.4 %collective-permute-start.48 = (f32[72,128]{1,0:T(8,128)S(1)}, f32[72,128]{1,0:T(8,128)S(1)}, u32[]{:S(2)}, u32[]{:S(2)}) collective-permute-start(f32[72,128]{1,0:T(8,128)S(1)} %add_add_fusion.1), channel_id=1, source_target_pairs={{0,4},{4,0},{8,12},{12,8},{1,5},{5,1},{9,13},{13,9},{2,6},{6,2},{1... | collective-permute-start | bytes 110600 | tf_op jit(solution)/shard_map/ppermute | solution.py:35
  305.4 19.2 %collective-permute-start.58 = (bf16[2,216,768]{2,1,0:T(8,128)(2,1)S(1)}, bf16[2,216,768]{2,1,0:T(8,128)(2,1)}, u32[]{:S(2)}, u32[]{:S(2)}) collective-permute-start(bf16[2,216,768]{2,1,0:T(8,128)(2,1)S(1)} %pad_maximum_fusion.9), channel_id=1, source_target_pairs={{0,4},{4,0},{8,12},{12,8},{1,5},{5,1},{9,13},{13,9},{2,6},{6,2},{1... | collective-permute-start | bytes 1990664 | tf_op jit(solution)/shard_map/ppermute | solution.py:35
  307.5 16.0 %collective-permute-start.56 = (bf16[2,72,768]{2,1,0:T(8,128)(2,1)S(1)}, bf16[2,72,768]{2,1,0:T(8,128)(2,1)S(1)}, u32[]{:S(2)}, u32[]{:S(2)}) collective-permute-start(bf16[2,72,768]{2,1,0:T(8,128)(2,1)S(1)} %pad_maximum_fusion.10), channel_id=1, source_target_pairs={{0,4},{4,0},{8,12},{12,8},{1,5},{5,1},{9,13},{13,9},{2,6},{6,2},{1... | collective-permute-start | bytes 663560 | tf_op jit(solution)/shard_map/ppermute | solution.py:35
  309.6 4.0 %collective-permute-start.51 = (f32[72,128]{1,0:T(8,128)S(1)}, f32[72,128]{1,0:T(8,128)S(1)}, u32[]{:S(2)}, u32[]{:S(2)}) collective-permute-start(f32[72,128]{1,0:T(8,128)S(1)} %add_add_fusion), channel_id=1, source_target_pairs={{0,16},{16,0},{1,17},{17,1},{2,18},{18,2},{3,19},{19,3},{4,20},{20... | collective-permute-start | bytes 110600 | tf_op jit(solution)/shard_map/ppermute | solution.py:35
  (30 other events, 156.2 us)

commit v4 on v3

--- a/solution.py
+++ b/solution.py
@@ -107,19 +107,22 @@
     return halve(halve(parts, 1, 1, rank % 2), 0, 2, rank // 2)
 
 
+def ctx_double(array, axis, bit, side):
+    other = swap(array, "ctx", bit)
+    first = side == 0
+    return jnp.stack([jnp.where(first, array, other), jnp.where(first, other, array)], axis=axis)
+
+
+def ctx_spread_far(total, rows):
+    if not ctx_plan(rows):
+        return total
+    return ctx_double(total, 0, 2, lax.axis_index("ctx") // 2)
+
+
 def ctx_spread(total, rows):
     if not ctx_plan(rows):
         return total.astype(F32)
-    rank = lax.axis_index("ctx")
-
-    def double(array, axis, bit, side):
-        other = swap(array, "ctx", bit)
-        first = side == 0
-        return jnp.stack(
-            [jnp.where(first, array, other), jnp.where(first, other, array)], axis=axis
-        )
-
-    total = double(double(total, 0, 2, rank // 2), 1, 1, rank % 2)
+    total = ctx_double(total, 1, 1, lax.axis_index("ctx") % 2)
     return total.reshape((rows,) + total.shape[3:]).astype(F32)
 
 
@@ -736,9 +739,11 @@
         block_out, grad_hidden, grad_slots, up_even, up_odd, down_even_g, down_odd_g, out_even, out_odd, sums,
     ) = middle(head_width, x_own, merged, cot_rows, vecs, ups, down_even, down_odd)
 
-    up_near = jnp.concatenate(
-        [add_low(up_even, swap(up_odd, "tp", 1)), add_low(out_even, swap(out_odd, "tp", 1))], axis=1
-    )
+    up_got, out_got = swap(up_odd, "tp", 1), swap(out_odd, "tp", 1)
+    up_near = [
+        jnp.concatenate([add_low(up_even[n], up_got[n]), add_low(out_even[n], out_got[n])])
+        for n in range(2)
+    ]
     down_near = add_low(down_even_g, swap(down_odd_g, "tp", 1))
     grad_slots = [grad_slots[s] for s in range(ranks)]
     grad_slots[1], up_near, down_near = lax.optimization_barrier((grad_slots[1], up_near, down_near))
@@ -802,15 +807,16 @@
     grad_x = grad_hidden + norm_back(xhat_one, rstd_one, gain_one, grad_normed_one)
     grad_x = grad_x.astype(BF)
     ln1_sums = jnp.stack([jnp.sum(grad_normed_one * xhat_one, axis=0), jnp.sum(grad_normed_one, axis=0)])
-    grad_x, ln1_sums, quarter = lax.optimization_barrier((grad_x, ln1_sums, quarter))
+    grad_qkv = grad_qkv.reshape(3, HEAD_PAD, width)[:, :head_width].astype(BF)
+    qkv_shard = scatter_fsdp(grad_qkv.reshape(3, fsdp, -1, width).transpose(1, 0, 2, 3))
+    qkv_rows, quarter = lax.optimization_barrier((qkv_shard.reshape(-1, width), quarter))
+    quarter = ctx_spread_far(quarter, cuts[3])
+    grad_x, quarter = lax.optimization_barrier((grad_x, quarter))
     grad_blocks = from_sequence(grad_x.reshape(seqs, sub, width))
     total = ctx_spread(quarter, cuts[3])
     sum_up, sum_out, sum_down = (total[cuts[n] : cuts[n + 1]] for n in range(3))
-
-    grad_qkv = grad_qkv.reshape(3, HEAD_PAD, width)[:, :head_width].astype(BF)
-    qkv_shard = scatter_fsdp(grad_qkv.reshape(3, fsdp, -1, width).transpose(1, 0, 2, 3))
-    qkv_rows = qkv_shard.reshape(-1, width)
-    sum_qkv = ctx_spread(ctx_reduce(qkv_rows), qkv_rows.shape[0]).reshape(w_qkv.shape)
+    sum_qkv = ctx_spread_far(ctx_reduce(qkv_rows), qkv_rows.shape[0])
+    sum_qkv = ctx_spread(sum_qkv, qkv_rows.shape[0]).reshape(w_qkv.shape)
 
     bias_sum = bias_sum.reshape(3, HEAD_PAD)[:, :head_width].reshape(3, heads, 64)
     bias_rows = jnp.concatenate([bias_sum[0], bias_sum[2]], axis=1)
@@ -823,9 +829,9 @@
     late = jnp.concatenate(
         [sums[:4].reshape(-1, LANES), up_bias_all.reshape(-1, LANES), ln1_sums.reshape(-1, LANES), bias_all]
     )
+    late = butterfly(butterfly(late, "tp"), "fsdp")
     late, grad_blocks = lax.optimization_barrier((late, grad_blocks))
-    for axis in ("tp", "ctx", "fsdp"):
-        late = butterfly(late, axis)
+    late = butterfly(late, "ctx")
     late_rows = late[: 10 * width // LANES].reshape(10, fsdp, shard)
 
     def mine_bias(rows, like):

time: 333 us -> 331 us (level)
  waiting for transfers between devices: 86.8 us -> 102 us
  Pallas kernels: 94.3 us -> 83.2 us
  starting transfers between devices: 63.8 us -> 58.4 us
    ppermute x47, waiting for transfers between devices: 67.2 us -> 85.6 us  [swap(): return lax.ppermute(value, axis, [(i, i ^ bit) for i in range(size)])]
    pallas_call x2, Pallas kernels: 36.7 us -> 30.2 us  [attend_back(): pl.pallas_call(functools.partial(attend_back_kernel, gathered, q_range, k...]
    ppermute x47, starting transfers between devices: 47.7 us -> 41.6 us  [swap(): return lax.ppermute(value, axis, [(i, i ^ bit) for i in range(size)])]
    pallas_call x1, Pallas kernels: 27.1 us -> 22.1 us  [attend(): pl.pallas_call(functools.partial(attend_kernel, gathered), out_shape=(jax...]
    unnamed x71 -> x79, local copies, waits for them, and re-layouts: 7.27 us -> 4.68 us
  transfers between devices with their start and end apart: 59 -> 59, of which waited for: 21 -> 29; matrix products, arithmetic and copies ran while one was open for 18% -> 19% of each run, Pallas kernels for 19% -> 16%
where the time goes in v4:
time: 331 us; the launch traced here: 327 us
  waiting for transfers between devices  102 us (31%)
  Pallas kernels  83.2 us (25%)
  starting transfers between devices  58.4 us (18%)
  local copies, waits for them, and re-layouts  39.9 us (12%)
  other arithmetic  30.5 us (9%)
  matrix products  10.1 us (3%)
    ppermute x47, waiting for transfers between devices, swap(): return lax.ppermute(value, axis, [(i, i ^ bit) for i in range(size)])  85.6 us
    ppermute x47, starting transfers between devices, swap(): return lax.ppermute(value, axis, [(i, i ^ bit) for i in range(size)])  41.6 us
    pallas_call x1, Pallas kernels, middle(): pl.pallas_call(functools.partial(middle_kernel, head_width), grid=(4,), o...  30.8 us
    pallas_call x2, Pallas kernels, attend_back(): pl.pallas_call(functools.partial(attend_back_kernel, gathered, q_range, k...  30.2 us
    pallas_call x1, Pallas kernels, attend(): pl.pallas_call(functools.partial(attend_kernel, gathered), out_shape=(jax...  22.1 us
    ppermute x12, starting transfers between devices, send(): return lax.ppermute(value, 'ctx', pairs)  16.8 us
    ppermute x12, waiting for transfers between devices, send(): return lax.ppermute(value, 'ctx', pairs)  16.7 us
  transfers between devices with their start and end apart: 59, of which 29 were waited for; matrix products, arithmetic and copies ran while one was open for 19% of the time, Pallas kernels for 16%

profile of v4, /device:TPU:0, one launch (start us, length us, event | category | flops | bytes accessed | tf_op | source)
XLA Modules:
  0.0 326.6 jit_solution(14213217063610854157)
XLA Ops:
  6.9 3.0 collective-permute-start.4
  10.0 2.1 constant_dynamic-slice_fusion.14
  12.0 1.6 collective-permute-start
  13.6 2.6 collective-permute-start.1
  16.2 1.3 collective-permute-start.2
  17.5 1.5 collective-permute-start.3
  25.2 1.3 stack_reshape.7
  26.5 1.3 stack_reshape.6
  29.2 1.3 reshape.403
  31.2 2.1 fusion.39
  34.0 1.6 collective-permute-start.8
  37.5 1.2 broadcast_select_fusion.3
  41.6 1.4 pad_maximum_fusion.6
  43.0 7.6 %collective-permute-done.8 = bf16[480,768]{1,0:T(8,128)(2,1)S(1)} collective-permute-done((bf16[480,768]{1,0:T(8,128)(2,1)S(1)}, bf16[480,768]{1,0:T(8,128)(2,1)S(1)}, u32[]{:S(2)}, u32[]{:S(2)}) %collective-permute-start.8) | collective-permute-done | bytes 737312 | tf_op jit(solution)/shard_map/ppermute | solution.py:35
  53.1 4.1 %collective-permute-done.6 = bf16[512,768]{1,0:T(8,128)(2,1)S(1)} collective-permute-done((bf16[512,768]{1,0:T(8,128)(2,1)S(1)}, bf16[512,768]{1,0:T(8,128)(2,1)S(1)}, u32[]{:S(2)}, u32[]{:S(2)}) %collective-permute-start.6) | collective-permute-done | bytes 786464 | tf_op jit(solution)/shard_map/ppermute | solution.py:35
  62.2 2.9 add_convert_fusion
  65.1 22.1 %attend.1 = (bf16[4,4,128,256]{3,2,1,0:T(8,128)(2,1)S(1)}, f32[4,3,8,512]{3,2,1,0:T(8,128)S(1)}) custom-call(s32[2]{0:T(128)S(1)} %pad_add_fusion.where_ref, s32[4]{0:T(128)S(1)} %get-tuple-element.143.low_ref, s32[4]{0:T(128)S(1)} %max.3.full_ref, s32[2048,1]{1,0:T(8,128)S(1)} %copy.56.seg_q_ref.seg_k_ref, ...), custom_call_target="tpu_custom_call" | custom-call | flops 17179869184 | bytes 16777216 | tf_op jit(solution)/shard_map/attend/pallas_call | solution.py:417
  87.3 2.1 collective-permute-done.15
  89.8 5.4 %collective-permute-done.13.up2 = bf16[976,768]{1,0:T(8,128)(2,1)S(1)} collective-permute-done((bf16[976,768]{1,0:T(8,128)(2,1)}, bf16[976,768]{1,0:T(8,128)(2,1)S(1)}, u32[]{:S(2)}, u32[]{:S(2)}) %collective-permute-start.13) | collective-permute-done | bytes 1499168 | tf_op jit(solution)/shard_map/ppermute | solution.py:35
  96.5 1.3 collective-permute-start.18
  97.8 4.5 %collective-permute-done.16.m1 = bf16[512,256]{1,0:T(8,128)(2,1)S(1)} collective-permute-done((bf16[512,256]{1,0:T(8,128)(2,1)S(1)}, bf16[512,256]{1,0:T(8,128)(2,1)S(1)}, u32[]{:S(2)}, u32[]{:S(2)}) %collective-permute-start.16) | collective-permute-done | bytes 262176 | tf_op jit(solution)/shard_map/ppermute | solution.py:35
  102.2 2.8 collective-permute-done.17.m2
  105.0 4.7 %collective-permute-done.18.m3 = bf16[512,256]{1,0:T(8,128)(2,1)S(1)} collective-permute-done((bf16[512,256]{1,0:T(8,128)(2,1)S(1)}, bf16[512,256]{1,0:T(8,128)(2,1)S(1)}, u32[]{:S(2)}, u32[]{:S(2)}) %collective-permute-start.18) | collective-permute-done | bytes 262176 | tf_op jit(solution)/shard_map/ppermute | solution.py:35
  111.7 30.8 %middle.1 = (bf16[512,768]{1,0:T(8,128)(2,1)S(1)}, f32[512,768]{1,0:T(8,128)}, bf16[4,512,256]{2,1,0:T(8,128)(2,1)S(1)}, bf16[2,768,768]{2,1,0:T(8,128)(2,1)}, b...) custom-call(bf16[512,768]{1,0:T(8,128)(2,1)S(1)} %bitcast.165, ...), custom_call_target="tpu_custom_call" | custom-call | flops 18119393280 | bytes 7077888 | tf_op jit(solution)/shard_map/middle/pallas_call | solution.py:598
  144.6 1.5 collective-permute-start.25
  146.1 2.7 collective-permute-done.22
  149.6 1.8 pad_maximum_fusion.3
  152.3 2.1 add_convert_fusion.1
  155.5 3.3 %collective-permute-done.25 = bf16[512,256]{1,0:T(8,128)(2,1)} collective-permute-done((bf16[512,256]{1,0:T(8,128)(2,1)}, bf16[512,256]{1,0:T(8,128)(2,1)}, u32[]{:S(2)}, u32[]{:S(2)}) %collective-permute-start.25) | collective-permute-done | bytes 262176 | tf_op jit(solution)/shard_map/ppermute | solution.py:35
  160.5 1.3 dynamic-slice_bitcast_fusion
  164.1 2.9 collective-permute-start.29
  167.0 1.8 collective-permute-start.30
  168.8 17.1 %attend_back_2_4.1 = (bf16[4,2,128,768]{3,2,1,0:T(8,128)(2,1)S(1)}, f32[1024,512]{1,0:T(8,128)}) custom-call(s32[2]{0:T(128)S(1)} %pad_add_fusion.where_ref, s32[4]{0:T(128)S(1)} %get-tuple-element.145.full_ref, s32[4]{0:T(128)S(1)} %get-tuple-element.144.high_ref, s32[4,1,512]{2,1,0:T(1,128)S(1)} %bitcast.173, s32[2048,1]{1,0:T(8,128)S(1)} %copy.56.seg_q_ref.seg_k_ref, ...), custom_call_target="tpu_custom_call" | custom-call | flops 12884901888 | bytes 33554432 | tf_op jit(solution)/shard_map/attend_back_2_4/pallas_call | solution.py:454
  188.0 1.3 collective-permute-done.28
  189.6 4.3 %collective-permute-done.27 = bf16[960,768]{1,0:T(8,128)(2,1)S(1)} collective-permute-done((bf16[960,768]{1,0:T(8,128)(2,1)S(1)}, bf16[960,768]{1,0:T(8,128)(2,1)S(1)}, u32[]{:S(2)}, u32[]{:S(2)}) %collective-permute-start.27) | collective-permute-done | bytes 1474592 | tf_op jit(solution)/shard_map/ppermute | solution.py:35
  195.6 1.4 convolution_convert_fusion.1
  197.2 4.3 %collective-permute-start.32 = (bf16[480,768]{1,0:T(8,128)(2,1)S(1)}, bf16[480,768]{1,0:T(8,128)(2,1)S(1)}, u32[]{:S(2)}, u32[]{:S(2)}) collective-permute-start(bf16[480,768]{1,0:T(8,128)(2,1)S(1)} %pad_maximum_fusion.9), channel_id=1, source_target_pairs={{0,16},{16,0},{1,17},{17,1},{2,18},{18,2},{3,19},{19,3},{4,20},{20... | collective-permute-start | bytes 2211848 | tf_op jit(solution)/shard_map/ppermute | solution.py:35
  202.2 13.1 %attend_back_0_2.1 = bf16[4,2,128,768]{3,2,1,0:T(8,128)(2,1)S(1)} custom-call(s32[2]{0:T(128)S(1)} %pad_add_fusion.where_ref, s32[4]{0:T(128)S(1)} %get-tuple-element.145.full_ref, s32[4]{0:T(128)S(1)} %get-tuple-element.144.high_ref, s32[4,1,512]{2,1,0:T(1,128)S(1)} %bitcast.174, s32[2048,1]{1,0:T(8,128)S(1)} %copy.56.seg_q_ref.seg_k_ref, ...), custom_call_target="tpu_custom_call" | custom-call | flops 12884901888 | bytes 33554432 | tf_op jit(solution)/shard_map/attend_back_0_2/pallas_call | solution.py:454
  215.4 1.4 collective-permute-done.32
  217.0 1.4 convolution_convert_fusion
  223.8 1.4 collective-permute-start.38
  225.9 3.0 fusion.12
  228.9 1.4 fusion.2
  231.2 1.8 collective-permute-start.44
  233.2 4.8 %collective-permute-done.45 = bf16[2,216,768]{2,1,0:T(8,128)(2,1)} collective-permute-done((bf16[2,216,768]{2,1,0:T(8,128)(2,1)}, bf16[2,216,768]{2,1,0:T(8,128)(2,1)}, u32[]{:S(2)}, u32[]{:S(2)}) %collective-permute-start.45) | collective-permute-done | bytes 663584 | tf_op jit(solution)/shard_map/ppermute | solution.py:35
  237.9 1.2 fusion.14
  240.0 2.6 collective-permute-start.46
  248.1 1.8 collective-permute-done.41
  250.7 1.4 collective-permute-start.43
  253.2 4.3 %collective-permute-done.46 = bf16[216,768]{1,0:T(8,128)(2,1)} collective-permute-done((bf16[216,768]{1,0:T(8,128)(2,1)}, bf16[216,768]{1,0:T(8,128)(2,1)}, u32[]{:S(2)}, u32[]{:S(2)}) %collective-permute-start.46) | collective-permute-done | bytes 331808 | tf_op jit(solution)/shard_map/ppermute | solution.py:35
  260.0 3.4 %collective-permute-start.47 = (bf16[216,768]{1,0:T(8,128)(2,1)S(1)}, bf16[216,768]{1,0:T(8,128)(2,1)S(1)}, u32[]{:S(2)}, u32[]{:S(2)}) collective-permute-start(bf16[216,768]{1,0:T(8,128)(2,1)S(1)} %fusion.22), channel_id=1, source_target_pairs={{0,8},{4,12},{8,0},{12,4},{1,9},{5,13},{9,1},{13,5},{2,10},{6,14},... | collective-permute-start | bytes 995336 | tf_op jit(solution)/shard_map/ppermute | solution.py:35
  263.5 5.5 %collective-permute-done.54 = bf16[2,72,768]{2,1,0:T(8,128)(2,1)S(1)} collective-permute-done((bf16[2,72,768]{2,1,0:T(8,128)(2,1)S(1)}, bf16[2,72,768]{2,1,0:T(8,128)(2,1)S(1)}, u32[]{:S(2)}, u32[]{:S(2)}) %collective-permute-start.54) | collective-permute-done | bytes 221216 | tf_op jit(solution)/shard_map/ppermute | solution.py:35
  269.9 11.7 %collective-permute-done.47 = bf16[216,768]{1,0:T(8,128)(2,1)S(1)} collective-permute-done((bf16[216,768]{1,0:T(8,128)(2,1)S(1)}, bf16[216,768]{1,0:T(8,128)(2,1)S(1)}, u32[]{:S(2)}, u32[]{:S(2)}) %collective-permute-start.47) | collective-permute-done | bytes 331808 | tf_op jit(solution)/shard_map/ppermute | solution.py:35
  281.8 1.3 collective-permute-done.55
  283.3 2.4 collective-permute-start.48
  285.7 2.0 collective-permute-start.49
  289.2 1.7 collective-permute-done.56
  290.9 2.9 collective-permute-done.48
  293.8 13.4 %collective-permute-done.49 = bf16[1,128,768]{2,1,0:T(8,128)(2,1)S(1)} collective-permute-done((bf16[1,128,768]{2,1,0:T(8,128)(2,1)S(1)}, bf16[1,128,768]{2,1,0:T(8,128)(2,1)S(1)}, u32[]{:S(2)}, u32[]{:S(2)}) %collective-permute-start.49) | collective-permute-done | bytes 196640 | tf_op jit(solution)/shard_map/ppermute | solution.py:158
  308.3 2.5 collective-permute-start.51
  310.9 3.6 %collective-permute-done.52 = f32[72,128]{1,0:T(8,128)S(1)} collective-permute-done((f32[72,128]{1,0:T(8,128)S(1)}, f32[72,128]{1,0:T(8,128)S(1)}, u32[]{:S(2)}, u32[]{:S(2)}) %collective-permute-start.52) | collective-permute-done | bytes 36896 | tf_op jit(solution)/shard_map/ppermute | solution.py:35
  314.5 3.3 %collective-permute-done.53 = f32[72,128]{1,0:T(8,128)S(1)} collective-permute-done((f32[72,128]{1,0:T(8,128)S(1)}, f32[72,128]{1,0:T(8,128)S(1)}, u32[]{:S(2)}, u32[]{:S(2)}) %collective-permute-start.53) | collective-permute-done | bytes 36896 | tf_op jit(solution)/shard_map/ppermute | solution.py:35
  320.8 1.5 collective-permute-done.57
  324.7 1.6 fusion.55
  (306 shorter events, 71.9 us)
Async XLA Ops:
  0.7 18.8 %copy-start.13 = (bf16[384,768]{1,0:T(8,128)(2,1)S(1)}, bf16[384,768]{1,0:T(8,128)(2,1)}, u32[]{:S(2)}) copy-start(bf16[384,768]{1,0:T(8,128)(2,1)} %param.25) | copy-start | bytes 1769476
  6.9 13.7 %collective-permute-start.4 = (bf16[1,8,384]{2,1,0:T(8,128)(2,1)}, bf16[1,8,384]{2,1,0:T(8,128)(2,1)}, u32[]{:S(2)}, u32[]{:S(2)}) collective-permute-start(bf16[1,8,384]{2,1,0:T(8,128)(2,1)} %bitcast.7), channel_id=1, source_target_pairs={{0,16},{16,0},{1,17},{17,1},{2,18},{18,2},{3,19},{19,3},{4,20},{20... | collective-permute-start | bytes 18440 | tf_op jit(solution)/shard_map/ppermute | solution.py:35
  12.0 22.0 %collective-permute-start = (bf16[1,128,768]{2,1,0:T(8,128)(2,1)}, bf16[1,128,768]{2,1,0:T(8,128)(2,1)}, u32[]{:S(2)}, u32[]{:S(2)}) collective-permute-start(bf16[1,128,768]{2,1,0:T(8,128)(2,1)} %get-tuple-element.195), channel_id=1, source_target_pairs={{0,4},{4,8},{8,12},{12,0},{1,5},{5,9},{9,13},{13,1},{2,6},{6,10},{... | collective-permute-start | bytes 589832 | tf_op jit(solution)/shard_map/ppermute | solution.py:158
  13.6 22.9 %collective-permute-start.1 = (bf16[1,128,768]{2,1,0:T(8,128)(2,1)}, bf16[1,128,768]{2,1,0:T(8,128)(2,1)}, u32[]{:S(2)}, u32[]{:S(2)}) collective-permute-start(bf16[1,128,768]{2,1,0:T(8,128)(2,1)} %get-tuple-element.197), channel_id=1, source_target_pairs={{0,8},{4,12},{8,0},{12,4},{1,9},{5,13},{9,1},{13,5},{2,10},{6,14},... | collective-permute-start | bytes 589832 | tf_op jit(solution)/shard_map/ppermute | solution.py:158
  16.2 21.3 %collective-permute-start.2 = (bf16[1,128,768]{2,1,0:T(8,128)(2,1)}, bf16[1,128,768]{2,1,0:T(8,128)(2,1)S(1)}, u32[]{:S(2)}, u32[]{:S(2)}) collective-permute-start(bf16[1,128,768]{2,1,0:T(8,128)(2,1)} %get-tuple-element.194), channel_id=1, source_target_pairs={{0,12},{4,0},{8,4},{12,8},{1,13},{5,1},{9,5},{13,9},{2,14},{6,2},{... | collective-permute-start | bytes 589832 | tf_op jit(solution)/shard_map/ppermute | solution.py:158
  17.5 21.3 %collective-permute-start.3 = (bf16[384,768]{1,0:T(8,128)(2,1)}, bf16[384,768]{1,0:T(8,128)(2,1)}, u32[]{:S(2)}, u32[]{:S(2)}) collective-permute-start(bf16[384,768]{1,0:T(8,128)(2,1)} %param.27), channel_id=1, source_target_pairs={{0,2},{1,3},{2,0},{3,1},{4,6},{5,7},{6,4},{7,5},{8,10},{9,11},{10,... | collective-permute-start | bytes 1769480 | tf_op jit(solution)/shard_map/ppermute | solution.py:35
  20.6 16.9 %collective-permute-start.12 = (bf16[3,96,768]{2,1,0:T(8,128)(2,1)}, bf16[3,96,768]{2,1,0:T(8,128)(2,1)}, u32[]{:S(2)}, u32[]{:S(2)}) collective-permute-start(bf16[3,96,768]{2,1,0:T(8,128)(2,1)} %param.19), channel_id=1, source_target_pairs={{0,16},{16,0},{1,17},{17,1},{2,18},{18,2},{3,19},{19,3},{4,20},{20... | collective-permute-start | bytes 1327112 | tf_op jit(solution)/shard_map/ppermute | solution.py:35
  34.0 16.6 %collective-permute-start.8 = (bf16[480,768]{1,0:T(8,128)(2,1)S(1)}, bf16[480,768]{1,0:T(8,128)(2,1)S(1)}, u32[]{:S(2)}, u32[]{:S(2)}) collective-permute-start(bf16[480,768]{1,0:T(8,128)(2,1)S(1)} %pad_maximum_fusion.8), channel_id=1, source_target_pairs={{0,16},{16,0},{1,17},{17,1},{2,18},{18,2},{3,19},{19,3},{4,20},{20... | collective-permute-start | bytes 2211848 | tf_op jit(solution)/shard_map/ppermute | solution.py:35
  38.8 23.4 %copy-start.26 = (bf16[3,256,768]{2,1,0:T(8,128)(2,1)}, bf16[3,256,768]{2,1,0:T(8,128)(2,1)S(1)}, u32[]{:S(2)}) copy-start(bf16[3,256,768]{2,1,0:T(8,128)(2,1)S(1)} %fusion.17) | copy-start | bytes 3538948
  39.8 17.4 %collective-permute-start.6 = (bf16[512,768]{1,0:T(8,128)(2,1)S(1)}, bf16[512,768]{1,0:T(8,128)(2,1)S(1)}, u32[]{:S(2)}, u32[]{:S(2)}) collective-permute-start(bf16[512,768]{1,0:T(8,128)(2,1)S(1)} %add_convert_fusion.6), channel_id=1, source_target_pairs={{0,2},{1,3},{2,0},{3,1},{4,6},{5,7},{6,4},{7,5},{8,10},{9,11},{10,... | collective-permute-start | bytes 2359304 | tf_op jit(solution)/shard_map/ppermute | solution.py:35
  40.4 19.3 %collective-permute-start.5 = (bf16[512,768]{1,0:T(8,128)(2,1)S(1)}, bf16[512,768]{1,0:T(8,128)(2,1)S(1)}, u32[]{:S(2)}, u32[]{:S(2)}) collective-permute-start(bf16[512,768]{1,0:T(8,128)(2,1)S(1)} %add_convert_fusion.6), channel_id=1, source_target_pairs={{0,1},{1,0},{2,3},{3,2},{4,5},{5,4},{6,7},{7,6},{8,9},{9,8},{10,11... | collective-permute-start | bytes 2359304 | tf_op jit(solution)/shard_map/ppermute | solution.py:35
  40.5 18.6 %collective-permute-start.9 = (bf16[1,128,768]{2,1,0:T(8,128)(2,1)S(1)}, bf16[1,128,768]{2,1,0:T(8,128)(2,1)S(1)}, u32[]{:S(2)}, u32[]{:S(2)}) collective-permute-start(bf16[1,128,768]{2,1,0:T(8,128)(2,1)S(1)} %get-tuple-element.192), channel_id=1, source_target_pairs={{0,4},{4,8},{8,12},{12,0},{1,5},{5,9},{9,13},{13,1},{2,6},{6,10},{... | collective-permute-start | bytes 589832 | tf_op jit(solution)/shard_map/ppermute | solution.py:158
  41.3 17.9 %collective-permute-start.10 = (bf16[1,128,768]{2,1,0:T(8,128)(2,1)S(1)}, bf16[1,128,768]{2,1,0:T(8,128)(2,1)S(1)}, u32[]{:S(2)}, u32[]{:S(2)}) collective-permute-start(bf16[1,128,768]{2,1,0:T(8,128)(2,1)S(1)} %get-tuple-element.191), channel_id=1, source_target_pairs={{0,8},{4,12},{8,0},{12,4},{1,9},{5,13},{9,1},{13,5},{2,10},{6,14},... | collective-permute-start | bytes 589832 | tf_op jit(solution)/shard_map/ppermute | solution.py:158
  50.6 9.1 %collective-permute-start.11 = (bf16[1,128,768]{2,1,0:T(8,128)(2,1)S(1)}, bf16[1,128,768]{2,1,0:T(8,128)(2,1)S(1)}, u32[]{:S(2)}, u32[]{:S(2)}) collective-permute-start(bf16[1,128,768]{2,1,0:T(8,128)(2,1)S(1)} %get-tuple-element.190), channel_id=1, source_target_pairs={{0,12},{4,0},{8,4},{12,8},{1,13},{5,1},{9,5},{13,9},{2,14},{6,2},{... | collective-permute-start | bytes 589832 | tf_op jit(solution)/shard_map/ppermute | solution.py:158
  57.2 2.6 collective-permute-start.7
  60.1 35.0 %collective-permute-start.13 = (bf16[976,768]{1,0:T(8,128)(2,1)}, bf16[976,768]{1,0:T(8,128)(2,1)S(1)}, u32[]{:S(2)}, u32[]{:S(2)}) collective-permute-start(bf16[976,768]{1,0:T(8,128)(2,1)} %pad_dynamic-update-slice_fusion.up0), channel_id=1, source_target_pairs={{0,2},{1,3},{2,0},{3,1},{4,6},{5,7},{6,4},{7,5},{8,10},{9,11},{10,... | collective-permute-start | bytes 4497416 | tf_op jit(solution)/shard_map/ppermute | solution.py:35
  61.0 34.1 %collective-permute-start.14 = (bf16[976,768]{1,0:T(8,128)(2,1)}, bf16[976,768]{1,0:T(8,128)(2,1)}, u32[]{:S(2)}, u32[]{:S(2)}) collective-permute-start(bf16[976,768]{1,0:T(8,128)(2,1)} %pad_dynamic-update-slice_fusion.up0), channel_id=1, source_target_pairs={{0,1},{1,0},{2,3},{3,2},{4,5},{5,4},{6,7},{7,6},{8,9},{9,8},{10,11... | collective-permute-start | bytes 4497416 | tf_op jit(solution)/shard_map/ppermute | solution.py:35
  61.0 28.4 %collective-permute-start.15 = (bf16[2,384,768]{2,1,0:T(8,128)(2,1)S(1)}, bf16[2,384,768]{2,1,0:T(8,128)(2,1)S(1)}, u32[]{:S(2)}, u32[]{:S(2)}) collective-permute-start(bf16[2,384,768]{2,1,0:T(8,128)(2,1)S(1)} %pad_maximum_fusion.6), channel_id=1, source_target_pairs={{0,16},{16,0},{1,17},{17,1},{2,18},{18,2},{3,19},{19,3},{4,20},{20... | collective-permute-start | bytes 3538952 | tf_op jit(solution)/shard_map/ppermute | solution.py:35
  65.1 22.2 %copy-start.6 = (bf16[2048,768]{1,0:T(8,128)(2,1)}, bf16[2048,768]{1,0:T(8,128)(2,1)S(1)}, u32[]{:S(2)}) copy-start(bf16[2048,768]{1,0:T(8,128)(2,1)S(1)} %add_convert_fusion) | copy-start | bytes 9437188
  89.7 20.0 %copy-start.20 = (bf16[2,768,768]{2,1,0:T(8,128)(2,1)}, bf16[2,768,768]{2,1,0:T(8,128)(2,1)S(1)}, u32[]{:S(2)}) copy-start(bf16[2,768,768]{2,1,0:T(8,128)(2,1)S(1)} %pad_maximum_fusion.1.down_even) | copy-start | bytes 7077892
  95.2 14.6 %collective-permute-start.20 = (bf16[2,768,768]{2,1,0:T(8,128)(2,1)S(1)}, bf16[2,768,768]{2,1,0:T(8,128)(2,1)S(1)}, u32[]{:S(2)}, u32[]{:S(2)}) collective-permute-start(bf16[2,768,768]{2,1,0:T(8,128)(2,1)S(1)} %pad_maximum_fusion.1.down_even), channel_id=1, source_target_pairs={{0,1},{1,0},{2,3},{3,2},{4,5},{5,4},{6,7},{7,6},{8,9},{9,8},{10,11... | collective-permute-start | bytes 7077896 | tf_op jit(solution)/shard_map/ppermute | solution.py:35
  95.2 14.6 %collective-permute-start.19 = (bf16[976,768]{1,0:T(8,128)(2,1)S(1)}, bf16[976,768]{1,0:T(8,128)(2,1)S(1)}, u32[]{:S(2)}, u32[]{:S(2)}) collective-permute-start(bf16[976,768]{1,0:T(8,128)(2,1)S(1)} %collective-permute-done.13.up2), channel_id=1, source_target_pairs={{0,1},{1,0},{2,3},{3,2},{4,5},{5,4},{6,7},{7,6},{8,9},{9,8},{10,11... | collective-permute-start | bytes 4497416 | tf_op jit(solution)/shard_map/ppermute | solution.py:35
  95.8 6.4 %collective-permute-start.16 = (bf16[512,256]{1,0:T(8,128)(2,1)S(1)}, bf16[512,256]{1,0:T(8,128)(2,1)S(1)}, u32[]{:S(2)}, u32[]{:S(2)}) collective-permute-start(bf16[512,256]{1,0:T(8,128)(2,1)S(1)} %bitcast.205), channel_id=1, source_target_pairs={{0,1},{1,0},{2,3},{3,2},{4,5},{5,4},{6,7},{7,6},{8,9},{9,8},{10,11... | collective-permute-start | bytes 786440 | tf_op jit(solution)/shard_map/ppermute | solution.py:35
  95.9 9.1 %collective-permute-start.17 = (bf16[512,256]{1,0:T(8,128)(2,1)S(1)}, bf16[512,256]{1,0:T(8,128)(2,1)S(1)}, u32[]{:S(2)}, u32[]{:S(2)}) collective-permute-start(bf16[512,256]{1,0:T(8,128)(2,1)S(1)} %bitcast.204), channel_id=1, source_target_pairs={{0,2},{1,3},{2,0},{3,1},{4,6},{5,7},{6,4},{7,5},{8,10},{9,11},{10,... | collective-permute-start | bytes 786440 | tf_op jit(solution)/shard_map/ppermute | solution.py:35
  96.5 13.3 %collective-permute-start.18 = (bf16[512,256]{1,0:T(8,128)(2,1)S(1)}, bf16[512,256]{1,0:T(8,128)(2,1)S(1)}, u32[]{:S(2)}, u32[]{:S(2)}) collective-permute-start(bf16[512,256]{1,0:T(8,128)(2,1)S(1)} %bitcast.203), channel_id=1, source_target_pairs={{0,3},{1,2},{2,1},{3,0},{4,7},{5,6},{6,5},{7,4},{8,11},{9,10},{10,... | collective-permute-start | bytes 786440 | tf_op jit(solution)/shard_map/ppermute | solution.py:35
  142.5 6.4 %collective-permute-start.21 = (bf16[2,768,768]{2,1,0:T(8,128)(2,1)}, bf16[2,768,768]{2,1,0:T(8,128)(2,1)S(1)}, u32[]{:S(2)}, u32[]{:S(2)}) collective-permute-start(bf16[2,768,768]{2,1,0:T(8,128)(2,1)} %get-tuple-element.87), channel_id=1, source_target_pairs={{0,1},{1,0},{2,3},{3,2},{4,5},{5,4},{6,7},{7,6},{8,9},{9,8},{10,11... | collective-permute-start | bytes 7077896 | tf_op jit(solution)/shard_map/ppermute | solution.py:35
  142.8 8.7 %collective-permute-start.23 = (bf16[2,768,768]{2,1,0:T(8,128)(2,1)}, bf16[2,768,768]{2,1,0:T(8,128)(2,1)S(1)}, u32[]{:S(2)}, u32[]{:S(2)}) collective-permute-start(bf16[2,768,768]{2,1,0:T(8,128)(2,1)} %get-tuple-element.91), channel_id=1, source_target_pairs={{0,1},{1,0},{2,3},{3,2},{4,5},{5,4},{6,7},{7,6},{8,9},{9,8},{10,11... | collective-permute-start | bytes 7077896 | tf_op jit(solution)/shard_map/ppermute | solution.py:35
  143.1 5.7 %collective-permute-start.22 = (bf16[2,192,768]{2,1,0:T(8,128)(2,1)S(1)}, bf16[2,192,768]{2,1,0:T(8,128)(2,1)S(1)}, u32[]{:S(2)}, u32[]{:S(2)}) collective-permute-start(bf16[2,192,768]{2,1,0:T(8,128)(2,1)S(1)} %get-tuple-element.89), channel_id=1, source_target_pairs={{0,1},{1,0},{2,3},{3,2},{4,5},{5,4},{6,7},{7,6},{8,9},{9,8},{10,11... | collective-permute-start | bytes 1769480 | tf_op jit(solution)/shard_map/ppermute | solution.py:35
  144.2 11.3 %collective-permute-start.26 = (bf16[512,256]{1,0:T(8,128)(2,1)}, bf16[512,256]{1,0:T(8,128)(2,1)S(1)}, u32[]{:S(2)}, u32[]{:S(2)}) collective-permute-start(bf16[512,256]{1,0:T(8,128)(2,1)} %get-tuple-element.169), channel_id=1, source_target_pairs={{0,3},{1,2},{2,1},{3,0},{4,7},{5,6},{6,5},{7,4},{8,11},{9,10},{10,... | collective-permute-start | bytes 786440 | tf_op jit(solution)/shard_map/ppermute | solution.py:35
  144.6 14.2 %collective-permute-start.25 = (bf16[512,256]{1,0:T(8,128)(2,1)}, bf16[512,256]{1,0:T(8,128)(2,1)}, u32[]{:S(2)}, u32[]{:S(2)}) collective-permute-start(bf16[512,256]{1,0:T(8,128)(2,1)} %get-tuple-element.170), channel_id=1, source_target_pairs={{0,2},{1,3},{2,0},{3,1},{4,6},{5,7},{6,4},{7,5},{8,10},{9,11},{10,... | collective-permute-start | bytes 786440 | tf_op jit(solution)/shard_map/ppermute | solution.py:35
  154.4 4.3 %collective-permute-start.24 = (bf16[512,256]{1,0:T(8,128)(2,1)S(1)}, bf16[512,256]{1,0:T(8,128)(2,1)}, u32[]{:S(2)}, u32[]{:S(2)}) collective-permute-start(bf16[512,256]{1,0:T(8,128)(2,1)S(1)} %get-tuple-element.92), channel_id=1, source_target_pairs={{0,1},{1,0},{2,3},{3,2},{4,5},{5,4},{6,7},{7,6},{8,9},{9,8},{10,11... | collective-permute-start | bytes 786440 | tf_op jit(solution)/shard_map/ppermute | solution.py:35
  159.9 34.0 %collective-permute-start.27 = (bf16[960,768]{1,0:T(8,128)(2,1)S(1)}, bf16[960,768]{1,0:T(8,128)(2,1)S(1)}, u32[]{:S(2)}, u32[]{:S(2)}) collective-permute-start(bf16[960,768]{1,0:T(8,128)(2,1)S(1)} %copy-done.24), channel_id=1, source_target_pairs={{0,2},{1,3},{2,0},{3,1},{4,6},{5,7},{6,4},{7,5},{8,10},{9,11},{10,... | collective-permute-start | bytes 4423688 | tf_op jit(solution)/shard_map/ppermute | solution.py:35
  161.9 27.4 %collective-permute-start.28 = (bf16[2,384,768]{2,1,0:T(8,128)(2,1)S(1)}, bf16[2,384,768]{2,1,0:T(8,128)(2,1)S(1)}, u32[]{:S(2)}, u32[]{:S(2)}) collective-permute-start(bf16[2,384,768]{2,1,0:T(8,128)(2,1)S(1)} %dynamic-slice_bitcast_fusion), channel_id=1, source_target_pairs={{0,16},{16,0},{1,17},{17,1},{2,18},{18,2},{3,19},{19,3},{4,20},{20... | collective-permute-start | bytes 3538952 | tf_op jit(solution)/shard_map/ppermute | solution.py:35
  164.1 21.8 %collective-permute-start.29 = (bf16[1,128,768]{2,1,0:T(8,128)(2,1)S(1)}, bf16[1,128,768]{2,1,0:T(8,128)(2,1)S(1)}, u32[]{:S(2)}, u32[]{:S(2)}) collective-permute-start(bf16[1,128,768]{2,1,0:T(8,128)(2,1)S(1)} %get-tuple-element.188), channel_id=1, source_target_pairs={{4,0},{8,4},{12,8},{0,12},{5,1},{9,5},{13,9},{1,13},{6,2},{10,6},{... | collective-permute-start | bytes 589832 | tf_op jit(solution)/shard_map/ppermute | solution.py:158
  167.0 19.6 %collective-permute-start.30 = (bf16[1,128,768]{2,1,0:T(8,128)(2,1)S(1)}, bf16[1,128,768]{2,1,0:T(8,128)(2,1)S(1)}, u32[]{:S(2)}, u32[]{:S(2)}) collective-permute-start(bf16[1,128,768]{2,1,0:T(8,128)(2,1)S(1)} %get-tuple-element.187), channel_id=1, source_target_pairs={{8,0},{12,4},{0,8},{4,12},{9,1},{13,5},{1,9},{5,13},{10,2},{14,6},... | collective-permute-start | bytes 589832 | tf_op jit(solution)/shard_map/ppermute | solution.py:158
  168.8 18.6 %collective-permute-start.31 = (bf16[1,128,768]{2,1,0:T(8,128)(2,1)S(1)}, bf16[1,128,768]{2,1,0:T(8,128)(2,1)S(1)}, u32[]{:S(2)}, u32[]{:S(2)}) collective-permute-start(bf16[1,128,768]{2,1,0:T(8,128)(2,1)S(1)} %get-tuple-element.186), channel_id=1, source_target_pairs={{12,0},{0,4},{4,8},{8,12},{13,1},{1,5},{5,9},{9,13},{14,2},{2,6},{... | collective-permute-start | bytes 589832 | tf_op jit(solution)/shard_map/ppermute | solution.py:158
  168.8 20.5 %copy-start.9 = (bf16[2,768,768]{2,1,0:T(8,128)(2,1)S(1)}, bf16[2,768,768]{2,1,0:T(8,128)(2,1)}, u32[]{:S(2)}) copy-start(bf16[2,768,768]{2,1,0:T(8,128)(2,1)} %add_convert_fusion.1) | copy-start | bytes 7077892
  197.2 19.6 %collective-permute-start.32 = (bf16[480,768]{1,0:T(8,128)(2,1)S(1)}, bf16[480,768]{1,0:T(8,128)(2,1)S(1)}, u32[]{:S(2)}, u32[]{:S(2)}) collective-permute-start(bf16[480,768]{1,0:T(8,128)(2,1)S(1)} %pad_maximum_fusion.9), channel_id=1, source_target_pairs={{0,16},{16,0},{1,17},{17,1},{2,18},{18,2},{3,19},{19,3},{4,20},{20... | collective-permute-start | bytes 2211848 | tf_op jit(solution)/shard_map/ppermute | solution.py:35
  201.6 13.7 %collective-permute-start.33 = (bf16[384,768]{1,0:T(8,128)(2,1)S(1)}, bf16[384,768]{1,0:T(8,128)(2,1)S(1)}, u32[]{:S(2)}, u32[]{:S(2)}) collective-permute-start(bf16[384,768]{1,0:T(8,128)(2,1)S(1)} %slice_bitcast_fusion), channel_id=1, source_target_pairs={{0,2},{1,3},{2,0},{3,1},{4,6},{5,7},{6,4},{7,5},{8,10},{9,11},{10,... | collective-permute-start | bytes 1769480 | tf_op jit(solution)/shard_map/ppermute | solution.py:35
  218.5 2.3 collective-permute-start.35
  218.6 2.3 collective-permute-start.34
  219.1 2.9 collective-permute-start.37
  219.2 2.7 collective-permute-start.36
  220.7 17.2 %collective-permute-start.45 = (bf16[2,216,768]{2,1,0:T(8,128)(2,1)}, bf16[2,216,768]{2,1,0:T(8,128)(2,1)}, u32[]{:S(2)}, u32[]{:S(2)}) collective-permute-start(bf16[2,216,768]{2,1,0:T(8,128)(2,1)} %dynamic-slice_bitcast_fusion.1), channel_id=1, source_target_pairs={{0,4},{4,0},{8,12},{12,8},{1,5},{5,1},{9,13},{13,9},{2,6},{6,2},{1... | collective-permute-start | bytes 1990664 | tf_op jit(solution)/shard_map/ppermute | solution.py:35
  223.8 18.8 %collective-permute-start.38 = (bf16[256,768]{1,0:T(8,128)(2,1)}, bf16[256,768]{1,0:T(8,128)(2,1)}, u32[]{:S(2)}, u32[]{:S(2)}) collective-permute-start(bf16[256,768]{1,0:T(8,128)(2,1)} %get-tuple-element.116), channel_id=1, source_target_pairs={{0,2},{1,3},{2,0},{3,1},{4,6},{5,7},{6,4},{7,5},{8,10},{9,11},{10,... | collective-permute-start | bytes 1179656 | tf_op jit(solution)/shard_map/ppermute | solution.py:35
  225.2 18.5 %collective-permute-start.39 = (bf16[256,768]{1,0:T(8,128)(2,1)}, bf16[256,768]{1,0:T(8,128)(2,1)}, u32[]{:S(2)}, u32[]{:S(2)}) collective-permute-start(bf16[256,768]{1,0:T(8,128)(2,1)} %get-tuple-element.118), channel_id=1, source_target_pairs={{0,2},{1,3},{2,0},{3,1},{4,6},{5,7},{6,4},{7,5},{8,10},{9,11},{10,... | collective-permute-start | bytes 1179656 | tf_op jit(solution)/shard_map/ppermute | solution.py:35
  231.2 20.8 %collective-permute-start.44 = (bf16[3,96,768]{2,1,0:T(8,128)(2,1)}, bf16[3,96,768]{2,1,0:T(8,128)(2,1)}, u32[]{:S(2)}, u32[]{:S(2)}) collective-permute-start(bf16[3,96,768]{2,1,0:T(8,128)(2,1)} %dynamic-slice_bitcast_fusion.4), channel_id=1, source_target_pairs={{0,16},{16,0},{1,17},{17,1},{2,18},{18,2},{3,19},{19,3},{4,20},{20... | collective-permute-start | bytes 1327112 | tf_op jit(solution)/shard_map/ppermute | solution.py:35
  240.0 17.5 %collective-permute-start.46 = (bf16[216,768]{1,0:T(8,128)(2,1)}, bf16[216,768]{1,0:T(8,128)(2,1)}, u32[]{:S(2)}, u32[]{:S(2)}) collective-permute-start(bf16[216,768]{1,0:T(8,128)(2,1)} %dynamic-slice_bitcast_fusion.5), channel_id=1, source_target_pairs={{0,8},{4,12},{8,0},{12,4},{1,9},{5,13},{9,1},{13,5},{2,10},{6,14},... | collective-permute-start | bytes 995336 | tf_op jit(solution)/shard_map/ppermute | solution.py:35
  245.8 4.0 %collective-permute-start.41 = (f32[72,128]{1,0:T(8,128)S(1)}, f32[72,128]{1,0:T(8,128)S(1)}, u32[]{:S(2)}, u32[]{:S(2)}) collective-permute-start(f32[72,128]{1,0:T(8,128)S(1)} %pad_maximum_fusion.12), channel_id=1, source_target_pairs={{0,2},{1,3},{2,0},{3,1},{4,6},{5,7},{6,4},{7,5},{8,10},{9,11},{10,... | collective-permute-start | bytes 110600 | tf_op jit(solution)/shard_map/ppermute | solution.py:35
  246.9 3.7 %collective-permute-start.42 = (f32[72,128]{1,0:T(8,128)S(1)}, f32[72,128]{1,0:T(8,128)S(1)}, u32[]{:S(2)}, u32[]{:S(2)}) collective-permute-start(f32[72,128]{1,0:T(8,128)S(1)} %pad_maximum_fusion.12), channel_id=1, source_target_pairs={{0,3},{1,2},{2,1},{3,0},{4,7},{5,6},{6,5},{7,4},{8,11},{9,10},{10,... | collective-permute-start | bytes 110600 | tf_op jit(solution)/shard_map/ppermute | solution.py:35
  247.0 3.7 %collective-permute-start.40 = (f32[72,128]{1,0:T(8,128)S(1)}, f32[72,128]{1,0:T(8,128)S(1)}, u32[]{:S(2)}, u32[]{:S(2)}) collective-permute-start(f32[72,128]{1,0:T(8,128)S(1)} %pad_maximum_fusion.12), channel_id=1, source_target_pairs={{0,1},{1,0},{2,3},{3,2},{4,5},{5,4},{6,7},{7,6},{8,9},{9,8},{10,11... | collective-permute-start | bytes 110600 | tf_op jit(solution)/shard_map/ppermute | solution.py:35
  250.7 9.3 %collective-permute-start.43 = (f32[72,128]{1,0:T(8,128)S(1)}, f32[72,128]{1,0:T(8,128)S(1)}, u32[]{:S(2)}, u32[]{:S(2)}) collective-permute-start(f32[72,128]{1,0:T(8,128)S(1)} %add_add_fusion.1), channel_id=1, source_target_pairs={{0,16},{16,0},{1,17},{17,1},{2,18},{18,2},{3,19},{19,3},{4,20},{20... | collective-permute-start | bytes 110600 | tf_op jit(solution)/shard_map/ppermute | solution.py:35
  258.6 10.3 %collective-permute-start.54 = (bf16[2,72,768]{2,1,0:T(8,128)(2,1)S(1)}, bf16[2,72,768]{2,1,0:T(8,128)(2,1)S(1)}, u32[]{:S(2)}, u32[]{:S(2)}) collective-permute-start(bf16[2,72,768]{2,1,0:T(8,128)(2,1)S(1)} %dynamic-slice_bitcast_fusion.6), channel_id=1, source_target_pairs={{0,4},{4,0},{8,12},{12,8},{1,5},{5,1},{9,13},{13,9},{2,6},{6,2},{1... | collective-permute-start | bytes 663560 | tf_op jit(solution)/shard_map/ppermute | solution.py:35
  260.0 21.6 %collective-permute-start.47 = (bf16[216,768]{1,0:T(8,128)(2,1)S(1)}, bf16[216,768]{1,0:T(8,128)(2,1)S(1)}, u32[]{:S(2)}, u32[]{:S(2)}) collective-permute-start(bf16[216,768]{1,0:T(8,128)(2,1)S(1)} %fusion.22), channel_id=1, source_target_pairs={{0,8},{4,12},{8,0},{12,4},{1,9},{5,13},{9,1},{13,5},{2,10},{6,14},... | collective-permute-start | bytes 995336 | tf_op jit(solution)/shard_map/ppermute | solution.py:35
  269.0 14.0 %collective-permute-start.55 = (bf16[72,768]{1,0:T(8,128)(2,1)S(1)}, bf16[72,768]{1,0:T(8,128)(2,1)S(1)}, u32[]{:S(2)}, u32[]{:S(2)}) collective-permute-start(bf16[72,768]{1,0:T(8,128)(2,1)S(1)} %dynamic-slice_bitcast_fusion.9), channel_id=1, source_target_pairs={{0,8},{4,12},{8,0},{12,4},{1,9},{5,13},{9,1},{13,5},{2,10},{6,14},... | collective-permute-start | bytes 331784 | tf_op jit(solution)/shard_map/ppermute | solution.py:35
  283.0 7.8 %collective-permute-start.56 = (bf16[72,768]{1,0:T(8,128)(2,1)S(1)}, bf16[72,768]{1,0:T(8,128)(2,1)S(1)}, u32[]{:S(2)}, u32[]{:S(2)}) collective-permute-start(bf16[72,768]{1,0:T(8,128)(2,1)S(1)} %fusion.26), channel_id=1, source_target_pairs={{0,8},{4,12},{8,0},{12,4},{1,9},{5,13},{9,1},{13,5},{2,10},{6,14},... | collective-permute-start | bytes 331784 | tf_op jit(solution)/shard_map/ppermute | solution.py:35
  283.3 10.5 %collective-permute-start.48 = (bf16[1,128,768]{2,1,0:T(8,128)(2,1)S(1)}, bf16[1,128,768]{2,1,0:T(8,128)(2,1)S(1)}, u32[]{:S(2)}, u32[]{:S(2)}) collective-permute-start(bf16[1,128,768]{2,1,0:T(8,128)(2,1)S(1)} %get-tuple-element.180), channel_id=1, source_target_pairs={{4,0},{8,4},{12,8},{0,12},{5,1},{9,5},{13,9},{1,13},{6,2},{10,6},{... | collective-permute-start | bytes 589832 | tf_op jit(solution)/shard_map/ppermute | solution.py:158
  285.7 21.5 %collective-permute-start.49 = (bf16[1,128,768]{2,1,0:T(8,128)(2,1)S(1)}, bf16[1,128,768]{2,1,0:T(8,128)(2,1)S(1)}, u32[]{:S(2)}, u32[]{:S(2)}) collective-permute-start(bf16[1,128,768]{2,1,0:T(8,128)(2,1)S(1)} %get-tuple-element.179), channel_id=1, source_target_pairs={{8,0},{12,4},{0,8},{4,12},{9,1},{13,5},{1,9},{5,13},{10,2},{14,6},... | collective-permute-start | bytes 589832 | tf_op jit(solution)/shard_map/ppermute | solution.py:158
  287.7 19.5 %collective-permute-start.50 = (bf16[1,128,768]{2,1,0:T(8,128)(2,1)S(1)}, bf16[1,128,768]{2,1,0:T(8,128)(2,1)S(1)}, u32[]{:S(2)}, u32[]{:S(2)}) collective-permute-start(bf16[1,128,768]{2,1,0:T(8,128)(2,1)S(1)} %get-tuple-element.178), channel_id=1, source_target_pairs={{12,0},{0,4},{4,8},{8,12},{13,1},{1,5},{5,9},{9,13},{14,2},{2,6},{... | collective-permute-start | bytes 589832 | tf_op jit(solution)/shard_map/ppermute | solution.py:158
  288.2 35.2 %collective-permute-start.58 = (bf16[2,216,768]{2,1,0:T(8,128)(2,1)S(1)}, bf16[2,216,768]{2,1,0:T(8,128)(2,1)S(1)}, u32[]{:S(2)}, u32[]{:S(2)}) collective-permute-start(bf16[2,216,768]{2,1,0:T(8,128)(2,1)S(1)} %pad_maximum_fusion.10), channel_id=1, source_target_pairs={{0,4},{4,0},{8,12},{12,8},{1,5},{5,1},{9,13},{13,9},{2,6},{6,2},{1... | collective-permute-start | bytes 1990664 | tf_op jit(solution)/shard_map/ppermute | solution.py:35
  307.2 7.3 %collective-permute-start.52 = (f32[72,128]{1,0:T(8,128)S(1)}, f32[72,128]{1,0:T(8,128)S(1)}, u32[]{:S(2)}, u32[]{:S(2)}) collective-permute-start(f32[72,128]{1,0:T(8,128)S(1)} %add.435), channel_id=1, source_target_pairs={{0,8},{4,12},{8,0},{12,4},{1,9},{5,13},{9,1},{13,5},{2,10},{6,14},... | collective-permute-start | bytes 110600 | tf_op jit(solution)/shard_map/ppermute | solution.py:35
  307.8 10.0 %collective-permute-start.53 = (f32[72,128]{1,0:T(8,128)S(1)}, f32[72,128]{1,0:T(8,128)S(1)}, u32[]{:S(2)}, u32[]{:S(2)}) collective-permute-start(f32[72,128]{1,0:T(8,128)S(1)} %add.435), channel_id=1, source_target_pairs={{0,12},{4,8},{8,4},{12,0},{1,13},{5,9},{9,5},{13,1},{2,14},{6,10},... | collective-permute-start | bytes 110600 | tf_op jit(solution)/shard_map/ppermute | solution.py:35
  308.3 10.5 %collective-permute-start.51 = (f32[72,128]{1,0:T(8,128)S(1)}, f32[72,128]{1,0:T(8,128)S(1)}, u32[]{:S(2)}, u32[]{:S(2)}) collective-permute-start(f32[72,128]{1,0:T(8,128)S(1)} %add.435), channel_id=1, source_target_pairs={{0,4},{4,0},{8,12},{12,8},{1,5},{5,1},{9,13},{13,9},{2,6},{6,2},{1... | collective-permute-start | bytes 110600 | tf_op jit(solution)/shard_map/ppermute | solution.py:35
  310.8 11.5 %collective-permute-start.57 = (bf16[2,72,768]{2,1,0:T(8,128)(2,1)S(1)}, bf16[2,72,768]{2,1,0:T(8,128)(2,1)S(1)}, u32[]{:S(2)}, u32[]{:S(2)}) collective-permute-start(bf16[2,72,768]{2,1,0:T(8,128)(2,1)S(1)} %pad_maximum_fusion.11), channel_id=1, source_target_pairs={{0,4},{4,0},{8,12},{12,8},{1,5},{5,1},{9,13},{13,9},{2,6},{6,2},{1... | collective-permute-start | bytes 663560 | tf_op jit(solution)/shard_map/ppermute | solution.py:35
  (34 other events, 237.0 us)

commit v5 on v4

--- a/solution.py
+++ b/solution.py
@@ -158,17 +158,21 @@
     return lax.ppermute(value, "ctx", pairs)
 
 
-def to_sequence(value):
+def to_sequence(value, later=()):
     seqs = value.shape[0]
     size = lax.axis_size("ctx")
     base = lax.axis_index("ctx") % seqs
     owner = lax.axis_index("ctx") // (size // seqs)
     out = jnp.zeros_like(value)
+    blocks = [
+        lax.dynamic_index_in_dim(value, (base + step) % seqs, 0, keepdims=True)
+        for step in range(seqs)
+    ]
+    blocks, later = lax.optimization_barrier((blocks, later))
     for step, pairs in enumerate(seq_steps(seqs)):
-        block = lax.dynamic_index_in_dim(value, (base + step) % seqs, 0, keepdims=True)
         place = (owner - step + seqs) % seqs
-        out = lax.dynamic_update_slice_in_dim(out, send(block, pairs), place, 0)
-    return out
+        out = lax.dynamic_update_slice_in_dim(out, send(blocks[step], pairs), place, 0)
+    return out, later
 
 
 def from_sequence(value):
@@ -673,12 +677,12 @@
     tokens = ranks * own
     shard = ln1_gain.shape[0]
 
-    x_blocks = to_sequence(block_in)
+    vectors = [ln1_gain, ln1_shift, b_out, ln2_gain, ln2_shift, b_down, b_qv.reshape(-1), b_up.reshape(-1)]
+    x_blocks, vectors = to_sequence(block_in, vectors)
     down_far = swap(w_down, "tp", 2)
     x_blocks, down_far = lax.optimization_barrier((x_blocks, down_far))
     x_own = x_blocks.reshape(own, width)
 
-    vectors = [ln1_gain, ln1_shift, b_out, ln2_gain, ln2_shift, b_down, b_qv.reshape(-1), b_up.reshape(-1)]
     rows = jnp.stack([jnp.pad(v, (0, shard - v.shape[0])) for v in vectors])
     (small,) = gather_fsdp([rows[None]], 0)
     (qkv_mat,) = gather_fsdp([w_qkv], 1)
@@ -703,7 +707,7 @@
     xhat_one, rstd_one = norm_parts(x_float)
     normed_own = (xhat_one * gain_one + shift_one).astype(BF)
     normed_own, cotangent = lax.optimization_barrier((normed_own, cotangent))
-    cot_rows = to_sequence(cotangent)
+    cot_rows, _ = to_sequence(cotangent)
     normed_one = jnp.concatenate(gather_tp(normed_own), axis=0)
     normed_one, up_own, down_pair, cot_rows = lax.optimization_barrier(
         (normed_one, up_own, down_pair, cot_rows)

time: 331 us -> 326 us (0.985)
  Pallas kernels: 83.2 us -> 94.3 us
  waiting for transfers between devices: 102 us -> 92.6 us
  starting transfers between devices: 58.4 us -> 54.4 us
    ppermute x47, waiting for transfers between devices: 85.6 us -> 76.4 us  [swap(): return lax.ppermute(value, axis, [(i, i ^ bit) for i in range(size)])]
    pallas_call x2, Pallas kernels: 30.2 us -> 36.7 us  [attend_back(): pl.pallas_call(functools.partial(attend_back_kernel, gathered, q_range, k...]
    pallas_call x1, Pallas kernels: 22.1 us -> 27.1 us  [attend(): pl.pallas_call(functools.partial(attend_kernel, gathered), out_shape=(jax...]
    another operation x8 -> x9, local copies, waits for them, and re-layouts: 4.79 us -> 0.66 us  [on_device(): rows = jnp.stack([jnp.pad(v, (0, shard - v.shape[0])) for v in vectors])]
    ppermute x47, starting transfers between devices: 41.6 us -> 37.7 us  [swap(): return lax.ppermute(value, axis, [(i, i ^ bit) for i in range(size)])]
  transfers between devices with their start and end apart: 59 -> 59, of which waited for: 29 -> 26; matrix products, arithmetic and copies ran while one was open for 19% -> 19% of each run, Pallas kernels for 16% -> 20%
where the time goes in v5:
time: 326 us; the launch traced here: 322 us
  Pallas kernels  94.3 us (29%)
  waiting for transfers between devices  92.6 us (28%)
  starting transfers between devices  54.4 us (17%)
  local copies, waits for them, and re-layouts  37.7 us (12%)
  other arithmetic  30.3 us (9%)
  matrix products  10.2 us (3%)
    ppermute x47, waiting for transfers between devices, swap(): return lax.ppermute(value, axis, [(i, i ^ bit) for i in range(size)])  76.4 us
    ppermute x47, starting transfers between devices, swap(): return lax.ppermute(value, axis, [(i, i ^ bit) for i in range(size)])  37.7 us
    pallas_call x2, Pallas kernels, attend_back(): pl.pallas_call(functools.partial(attend_back_kernel, gathered, q_range, k...  36.7 us
    pallas_call x1, Pallas kernels, middle(): pl.pallas_call(functools.partial(middle_kernel, head_width), grid=(4,), o...  30.5 us
    pallas_call x1, Pallas kernels, attend(): pl.pallas_call(functools.partial(attend_kernel, gathered), out_shape=(jax...  27.1 us
    ppermute x12, starting transfers between devices, send(): return lax.ppermute(value, 'ctx', pairs)  16.7 us
    ppermute x12, waiting for transfers between devices, send(): return lax.ppermute(value, 'ctx', pairs)  16.3 us
  transfers between devices with their start and end apart: 59, of which 26 were waited for; matrix products, arithmetic and copies ran while one was open for 19% of the time, Pallas kernels for 20%

profile of v5, /device:TPU:0, one launch (start us, length us, event | category | flops | bytes accessed | tf_op | source)
XLA Modules:
  0.0 322.0 jit_solution(1658277574492806570)
XLA Ops:
  1.7 2.0 constant_dynamic-slice_fusion.16
  4.5 3.0 collective-permute-start.4
  7.5 1.6 collective-permute-start
  9.0 2.6 collective-permute-start.1
  11.6 1.3 collective-permute-start.2
  13.0 1.5 collective-permute-start.3
  20.7 1.3 stack_reshape.7
  22.1 1.3 stack_reshape.6
  24.8 1.3 reshape.405
  26.7 2.1 fusion.39
  29.5 1.6 collective-permute-start.8
  34.0 1.2 broadcast_select_fusion.3
  38.1 1.4 pad_maximum_fusion.6
  39.5 6.7 %collective-permute-done.8 = bf16[480,768]{1,0:T(8,128)(2,1)S(1)} collective-permute-done((bf16[480,768]{1,0:T(8,128)(2,1)S(1)}, bf16[480,768]{1,0:T(8,128)(2,1)S(1)}, u32[]{:S(2)}, u32[]{:S(2)}) %collective-permute-start.8) | collective-permute-done | bytes 737312 | tf_op jit(solution)/shard_map/ppermute | solution.py:35
  48.7 4.9 %collective-permute-done.6 = bf16[512,768]{1,0:T(8,128)(2,1)S(1)} collective-permute-done((bf16[512,768]{1,0:T(8,128)(2,1)S(1)}, bf16[512,768]{1,0:T(8,128)(2,1)S(1)}, u32[]{:S(2)}, u32[]{:S(2)}) %collective-permute-start.6) | collective-permute-done | bytes 786464 | tf_op jit(solution)/shard_map/ppermute | solution.py:35
  58.1 2.9 add_convert_fusion
  61.0 27.1 %attend.1 = (bf16[4,4,128,256]{3,2,1,0:T(8,128)(2,1)S(1)}, f32[4,3,8,512]{3,2,1,0:T(8,128)S(1)}) custom-call(s32[2]{0:T(128)S(1)} %pad_add_fusion.where_ref, s32[4]{0:T(128)S(1)} %get-tuple-element.175.low_ref, s32[4]{0:T(128)S(1)} %max.3.full_ref, s32[2048,1]{1,0:T(8,128)S(1)} %copy.56.seg_q_ref.seg_k_ref, ...), custom_call_target="tpu_custom_call" | custom-call | flops 17179869184 | bytes 16777216 | tf_op jit(solution)/shard_map/attend/pallas_call | solution.py:421
  89.0 2.7 collective-permute-done.13.up2
  93.0 1.3 collective-permute-start.18
  94.3 4.5 %collective-permute-done.16.m1 = bf16[512,256]{1,0:T(8,128)(2,1)S(1)} collective-permute-done((bf16[512,256]{1,0:T(8,128)(2,1)S(1)}, bf16[512,256]{1,0:T(8,128)(2,1)S(1)}, u32[]{:S(2)}, u32[]{:S(2)}) %collective-permute-start.16) | collective-permute-done | bytes 262176 | tf_op jit(solution)/shard_map/ppermute | solution.py:35
  98.8 2.8 collective-permute-done.17.m2
  101.6 4.7 %collective-permute-done.18.m3 = bf16[512,256]{1,0:T(8,128)(2,1)S(1)} collective-permute-done((bf16[512,256]{1,0:T(8,128)(2,1)S(1)}, bf16[512,256]{1,0:T(8,128)(2,1)S(1)}, u32[]{:S(2)}, u32[]{:S(2)}) %collective-permute-start.18) | collective-permute-done | bytes 262176 | tf_op jit(solution)/shard_map/ppermute | solution.py:35
  108.2 30.5 %middle.1 = (bf16[512,768]{1,0:T(8,128)(2,1)S(1)}, f32[512,768]{1,0:T(8,128)}, bf16[4,512,256]{2,1,0:T(8,128)(2,1)S(1)}, bf16[2,768,768]{2,1,0:T(8,128)(2,1)}, b...) custom-call(bf16[512,768]{1,0:T(8,128)(2,1)S(1)} %bitcast.161, ...), custom_call_target="tpu_custom_call" | custom-call | flops 18119393280 | bytes 7077888 | tf_op jit(solution)/shard_map/middle/pallas_call | solution.py:602
  140.8 1.5 collective-permute-start.25
  142.3 2.7 collective-permute-done.22
  145.9 1.8 pad_maximum_fusion.3
  148.6 2.2 add_convert_fusion.1
  151.8 3.2 collective-permute-done.25
  155.0 1.2 pad_maximum_fusion.7.do_ref
  156.7 1.3 dynamic-slice_bitcast_fusion
  160.4 2.8 collective-permute-start.29
  163.1 1.8 collective-permute-start.30
  164.9 24.1 %attend_back_2_4.1 = (bf16[4,2,128,768]{3,2,1,0:T(8,128)(2,1)S(1)}, f32[1024,512]{1,0:T(8,128)}) custom-call(s32[2]{0:T(128)S(1)} %pad_add_fusion.where_ref, s32[4]{0:T(128)S(1)} %get-tuple-element.177.full_ref, s32[4]{0:T(128)S(1)} %get-tuple-element.176.high_ref, s32[4,1,512]{2,1,0:T(1,128)S(1)} %bitcast.169, s32[2048,1]{1,0:T(8,128)S(1)} %copy.56.seg_q_ref.seg_k_ref, ...), custom_call_target="tpu_custom_call" | custom-call | flops 12884901888 | bytes 33554432 | tf_op jit(solution)/shard_map/attend_back_2_4/pallas_call | solution.py:458
  194.1 1.4 convolution_convert_fusion.1
  196.4 12.6 %attend_back_0_2.1 = bf16[4,2,128,768]{3,2,1,0:T(8,128)(2,1)S(1)} custom-call(s32[2]{0:T(128)S(1)} %pad_add_fusion.where_ref, s32[4]{0:T(128)S(1)} %get-tuple-element.177.full_ref, s32[4]{0:T(128)S(1)} %get-tuple-element.176.high_ref, s32[4,1,512]{2,1,0:T(1,128)S(1)} %bitcast.170, s32[2048,1]{1,0:T(8,128)S(1)} %copy.56.seg_q_ref.seg_k_ref, ...), custom_call_target="tpu_custom_call" | custom-call | flops 12884901888 | bytes 33554432 | tf_op jit(solution)/shard_map/attend_back_0_2/pallas_call | solution.py:458
  209.9 2.9 collective-permute-done.32
  213.0 1.4 convolution_convert_fusion
  216.7 1.4 collective-permute-start.45
  221.7 1.5 collective-permute-start.39
  223.2 3.0 fusion.12
  226.2 1.5 fusion.2
  228.7 1.5 collective-permute-start.44
  230.3 3.6 %collective-permute-done.45 = bf16[2,216,768]{2,1,0:T(8,128)(2,1)} collective-permute-done((bf16[2,216,768]{2,1,0:T(8,128)(2,1)}, bf16[2,216,768]{2,1,0:T(8,128)(2,1)}, u32[]{:S(2)}, u32[]{:S(2)}) %collective-permute-start.45) | collective-permute-done | bytes 663584 | tf_op jit(solution)/shard_map/ppermute | solution.py:35
  233.9 1.2 fusion.14
  235.9 2.1 collective-permute-start.46
  239.2 1.5 collective-permute-done.39
  243.4 1.6 collective-permute-start.40
  245.0 2.1 collective-permute-done.41
  247.2 1.6 collective-permute-start.43
  249.9 3.3 %collective-permute-done.46 = bf16[216,768]{1,0:T(8,128)(2,1)} collective-permute-done((bf16[216,768]{1,0:T(8,128)(2,1)}, bf16[216,768]{1,0:T(8,128)(2,1)}, u32[]{:S(2)}, u32[]{:S(2)}) %collective-permute-start.46) | collective-permute-done | bytes 331808 | tf_op jit(solution)/shard_map/ppermute | solution.py:35
  255.5 3.5 %collective-permute-start.47 = (bf16[216,768]{1,0:T(8,128)(2,1)S(1)}, bf16[216,768]{1,0:T(8,128)(2,1)S(1)}, u32[]{:S(2)}, u32[]{:S(2)}) collective-permute-start(bf16[216,768]{1,0:T(8,128)(2,1)S(1)} %fusion.22), channel_id=1, source_target_pairs={{0,8},{4,12},{8,0},{12,4},{1,9},{5,13},{9,1},{13,5},{2,10},{6,14},... | collective-permute-start | bytes 995336 | tf_op jit(solution)/shard_map/ppermute | solution.py:35
  259.0 5.6 %collective-permute-done.54 = bf16[2,72,768]{2,1,0:T(8,128)(2,1)S(1)} collective-permute-done((bf16[2,72,768]{2,1,0:T(8,128)(2,1)S(1)}, bf16[2,72,768]{2,1,0:T(8,128)(2,1)S(1)}, u32[]{:S(2)}, u32[]{:S(2)}) %collective-permute-start.54) | collective-permute-done | bytes 221216 | tf_op jit(solution)/shard_map/ppermute | solution.py:35
  265.4 11.7 %collective-permute-done.47 = bf16[216,768]{1,0:T(8,128)(2,1)S(1)} collective-permute-done((bf16[216,768]{1,0:T(8,128)(2,1)S(1)}, bf16[216,768]{1,0:T(8,128)(2,1)S(1)}, u32[]{:S(2)}, u32[]{:S(2)}) %collective-permute-start.47) | collective-permute-done | bytes 331808 | tf_op jit(solution)/shard_map/ppermute | solution.py:35
  277.2 1.3 collective-permute-done.55
  278.8 2.4 collective-permute-start.48
  281.2 2.0 collective-permute-start.49
  284.7 1.7 collective-permute-done.56
  286.4 2.9 collective-permute-done.48
  289.3 13.4 %collective-permute-done.49 = bf16[1,128,768]{2,1,0:T(8,128)(2,1)S(1)} collective-permute-done((bf16[1,128,768]{2,1,0:T(8,128)(2,1)S(1)}, bf16[1,128,768]{2,1,0:T(8,128)(2,1)S(1)}, u32[]{:S(2)}, u32[]{:S(2)}) %collective-permute-start.49) | collective-permute-done | bytes 196640 | tf_op jit(solution)/shard_map/ppermute | solution.py:158
  303.8 2.5 collective-permute-start.51
  306.4 3.6 %collective-permute-done.52 = f32[72,128]{1,0:T(8,128)S(1)} collective-permute-done((f32[72,128]{1,0:T(8,128)S(1)}, f32[72,128]{1,0:T(8,128)S(1)}, u32[]{:S(2)}, u32[]{:S(2)}) %collective-permute-start.52) | collective-permute-done | bytes 36896 | tf_op jit(solution)/shard_map/ppermute | solution.py:35
  310.0 3.3 %collective-permute-done.53 = f32[72,128]{1,0:T(8,128)S(1)} collective-permute-done((f32[72,128]{1,0:T(8,128)S(1)}, f32[72,128]{1,0:T(8,128)S(1)}, u32[]{:S(2)}, u32[]{:S(2)}) %collective-permute-start.53) | collective-permute-done | bytes 36896 | tf_op jit(solution)/shard_map/ppermute | solution.py:35
  316.3 1.5 collective-permute-done.57
  320.2 1.6 fusion.55
  (322 shorter events, 65.6 us)
Async XLA Ops:
  4.5 11.7 %collective-permute-start.4 = (bf16[1,8,384]{2,1,0:T(8,128)(2,1)}, bf16[1,8,384]{2,1,0:T(8,128)(2,1)}, u32[]{:S(2)}, u32[]{:S(2)}) collective-permute-start(bf16[1,8,384]{2,1,0:T(8,128)(2,1)} %bitcast.8), channel_id=1, source_target_pairs={{0,16},{16,0},{1,17},{17,1},{2,18},{18,2},{3,19},{19,3},{4,20},{20... | collective-permute-start | bytes 18440 | tf_op jit(solution)/shard_map/ppermute | solution.py:35
  7.5 22.1 %collective-permute-start = (bf16[1,128,768]{2,1,0:T(8,128)(2,1)}, bf16[1,128,768]{2,1,0:T(8,128)(2,1)}, u32[]{:S(2)}, u32[]{:S(2)}) collective-permute-start(bf16[1,128,768]{2,1,0:T(8,128)(2,1)} %get-tuple-element.89), channel_id=1, source_target_pairs={{0,4},{4,8},{8,12},{12,0},{1,5},{5,9},{9,13},{13,1},{2,6},{6,10},{... | collective-permute-start | bytes 589832 | tf_op jit(solution)/shard_map/ppermute | solution.py:158
  9.0 23.0 %collective-permute-start.1 = (bf16[1,128,768]{2,1,0:T(8,128)(2,1)}, bf16[1,128,768]{2,1,0:T(8,128)(2,1)}, u32[]{:S(2)}, u32[]{:S(2)}) collective-permute-start(bf16[1,128,768]{2,1,0:T(8,128)(2,1)} %get-tuple-element.90), channel_id=1, source_target_pairs={{0,8},{4,12},{8,0},{12,4},{1,9},{5,13},{9,1},{13,5},{2,10},{6,14},... | collective-permute-start | bytes 589832 | tf_op jit(solution)/shard_map/ppermute | solution.py:158
  11.6 21.4 %collective-permute-start.2 = (bf16[1,128,768]{2,1,0:T(8,128)(2,1)S(1)}, bf16[1,128,768]{2,1,0:T(8,128)(2,1)}, u32[]{:S(2)}, u32[]{:S(2)}) collective-permute-start(bf16[1,128,768]{2,1,0:T(8,128)(2,1)S(1)} %get-tuple-element.91), channel_id=1, source_target_pairs={{0,12},{4,0},{8,4},{12,8},{1,13},{5,1},{9,5},{13,9},{2,14},{6,2},{... | collective-permute-start | bytes 589832 | tf_op jit(solution)/shard_map/ppermute | solution.py:158
  13.0 22.4 %collective-permute-start.3 = (bf16[384,768]{1,0:T(8,128)(2,1)}, bf16[384,768]{1,0:T(8,128)(2,1)}, u32[]{:S(2)}, u32[]{:S(2)}) collective-permute-start(bf16[384,768]{1,0:T(8,128)(2,1)} %param.27), channel_id=1, source_target_pairs={{0,2},{1,3},{2,0},{3,1},{4,6},{5,7},{6,4},{7,5},{8,10},{9,11},{10,... | collective-permute-start | bytes 1769480 | tf_op jit(solution)/shard_map/ppermute | solution.py:35
  16.2 17.8 %collective-permute-start.12 = (bf16[3,96,768]{2,1,0:T(8,128)(2,1)}, bf16[3,96,768]{2,1,0:T(8,128)(2,1)}, u32[]{:S(2)}, u32[]{:S(2)}) collective-permute-start(bf16[3,96,768]{2,1,0:T(8,128)(2,1)} %param.19), channel_id=1, source_target_pairs={{0,16},{16,0},{1,17},{17,1},{2,18},{18,2},{3,19},{19,3},{4,20},{20... | collective-permute-start | bytes 1327112 | tf_op jit(solution)/shard_map/ppermute | solution.py:35
  29.5 16.6 %collective-permute-start.8 = (bf16[480,768]{1,0:T(8,128)(2,1)S(1)}, bf16[480,768]{1,0:T(8,128)(2,1)S(1)}, u32[]{:S(2)}, u32[]{:S(2)}) collective-permute-start(bf16[480,768]{1,0:T(8,128)(2,1)S(1)} %pad_maximum_fusion.8), channel_id=1, source_target_pairs={{0,16},{16,0},{1,17},{17,1},{2,18},{18,2},{3,19},{19,3},{4,20},{20... | collective-permute-start | bytes 2211848 | tf_op jit(solution)/shard_map/ppermute | solution.py:35
  35.3 22.8 %copy-start.26 = (bf16[3,256,768]{2,1,0:T(8,128)(2,1)}, bf16[3,256,768]{2,1,0:T(8,128)(2,1)S(1)}, u32[]{:S(2)}) copy-start(bf16[3,256,768]{2,1,0:T(8,128)(2,1)S(1)} %fusion.17) | copy-start | bytes 3538948
  36.3 17.4 %collective-permute-start.6 = (bf16[512,768]{1,0:T(8,128)(2,1)S(1)}, bf16[512,768]{1,0:T(8,128)(2,1)S(1)}, u32[]{:S(2)}, u32[]{:S(2)}) collective-permute-start(bf16[512,768]{1,0:T(8,128)(2,1)S(1)} %add_convert_fusion.6), channel_id=1, source_target_pairs={{0,2},{1,3},{2,0},{3,1},{4,6},{5,7},{6,4},{7,5},{8,10},{9,11},{10,... | collective-permute-start | bytes 2359304 | tf_op jit(solution)/shard_map/ppermute | solution.py:35
  36.9 18.9 %collective-permute-start.5 = (bf16[512,768]{1,0:T(8,128)(2,1)S(1)}, bf16[512,768]{1,0:T(8,128)(2,1)S(1)}, u32[]{:S(2)}, u32[]{:S(2)}) collective-permute-start(bf16[512,768]{1,0:T(8,128)(2,1)S(1)} %add_convert_fusion.6), channel_id=1, source_target_pairs={{0,1},{1,0},{2,3},{3,2},{4,5},{5,4},{6,7},{7,6},{8,9},{9,8},{10,11... | collective-permute-start | bytes 2359304 | tf_op jit(solution)/shard_map/ppermute | solution.py:35
  37.0 18.7 %collective-permute-start.9 = (bf16[1,128,768]{2,1,0:T(8,128)(2,1)S(1)}, bf16[1,128,768]{2,1,0:T(8,128)(2,1)S(1)}, u32[]{:S(2)}, u32[]{:S(2)}) collective-permute-start(bf16[1,128,768]{2,1,0:T(8,128)(2,1)S(1)} %get-tuple-element.105), channel_id=1, source_target_pairs={{0,4},{4,8},{8,12},{12,0},{1,5},{5,9},{9,13},{13,1},{2,6},{6,10},{... | collective-permute-start | bytes 589832 | tf_op jit(solution)/shard_map/ppermute | solution.py:158
  37.7 18.0 %collective-permute-start.10 = (bf16[1,128,768]{2,1,0:T(8,128)(2,1)S(1)}, bf16[1,128,768]{2,1,0:T(8,128)(2,1)S(1)}, u32[]{:S(2)}, u32[]{:S(2)}) collective-permute-start(bf16[1,128,768]{2,1,0:T(8,128)(2,1)S(1)} %get-tuple-element.106), channel_id=1, source_target_pairs={{0,8},{4,12},{8,0},{12,4},{1,9},{5,13},{9,1},{13,5},{2,10},{6,14},... | collective-permute-start | bytes 589832 | tf_op jit(solution)/shard_map/ppermute | solution.py:158
  46.2 9.6 %collective-permute-start.11 = (bf16[1,128,768]{2,1,0:T(8,128)(2,1)S(1)}, bf16[1,128,768]{2,1,0:T(8,128)(2,1)S(1)}, u32[]{:S(2)}, u32[]{:S(2)}) collective-permute-start(bf16[1,128,768]{2,1,0:T(8,128)(2,1)S(1)} %get-tuple-element.107), channel_id=1, source_target_pairs={{0,12},{4,0},{8,4},{12,8},{1,13},{5,1},{9,5},{13,9},{2,14},{6,2},{... | collective-permute-start | bytes 589832 | tf_op jit(solution)/shard_map/ppermute | solution.py:158
  53.7 2.3 collective-permute-start.7
  56.3 35.4 %collective-permute-start.13 = (bf16[976,768]{1,0:T(8,128)(2,1)}, bf16[976,768]{1,0:T(8,128)(2,1)S(1)}, u32[]{:S(2)}, u32[]{:S(2)}) collective-permute-start(bf16[976,768]{1,0:T(8,128)(2,1)} %pad_dynamic-update-slice_fusion.up0), channel_id=1, source_target_pairs={{0,2},{1,3},{2,0},{3,1},{4,6},{5,7},{6,4},{7,5},{8,10},{9,11},{10,... | collective-permute-start | bytes 4497416 | tf_op jit(solution)/shard_map/ppermute | solution.py:35
  56.9 34.8 %collective-permute-start.14 = (bf16[976,768]{1,0:T(8,128)(2,1)}, bf16[976,768]{1,0:T(8,128)(2,1)}, u32[]{:S(2)}, u32[]{:S(2)}) collective-permute-start(bf16[976,768]{1,0:T(8,128)(2,1)} %pad_dynamic-update-slice_fusion.up0), channel_id=1, source_target_pairs={{0,1},{1,0},{2,3},{3,2},{4,5},{5,4},{6,7},{7,6},{8,9},{9,8},{10,11... | collective-permute-start | bytes 4497416 | tf_op jit(solution)/shard_map/ppermute | solution.py:35
  57.0 31.2 %collective-permute-start.15 = (bf16[2,384,768]{2,1,0:T(8,128)(2,1)S(1)}, bf16[2,384,768]{2,1,0:T(8,128)(2,1)S(1)}, u32[]{:S(2)}, u32[]{:S(2)}) collective-permute-start(bf16[2,384,768]{2,1,0:T(8,128)(2,1)S(1)} %pad_maximum_fusion.6), channel_id=1, source_target_pairs={{0,16},{16,0},{1,17},{17,1},{2,18},{18,2},{3,19},{19,3},{4,20},{20... | collective-permute-start | bytes 3538952 | tf_op jit(solution)/shard_map/ppermute | solution.py:35
  61.0 27.1 %copy-start.6 = (bf16[2048,768]{1,0:T(8,128)(2,1)}, bf16[2048,768]{1,0:T(8,128)(2,1)S(1)}, u32[]{:S(2)}) copy-start(bf16[2048,768]{1,0:T(8,128)(2,1)S(1)} %add_convert_fusion) | copy-start | bytes 9437188
  89.0 17.3 %copy-start.20 = (bf16[2,768,768]{2,1,0:T(8,128)(2,1)}, bf16[2,768,768]{2,1,0:T(8,128)(2,1)S(1)}, u32[]{:S(2)}) copy-start(bf16[2,768,768]{2,1,0:T(8,128)(2,1)S(1)} %pad_maximum_fusion.1.down_even) | copy-start | bytes 7077892
  91.7 14.6 %collective-permute-start.20 = (bf16[2,768,768]{2,1,0:T(8,128)(2,1)S(1)}, bf16[2,768,768]{2,1,0:T(8,128)(2,1)S(1)}, u32[]{:S(2)}, u32[]{:S(2)}) collective-permute-start(bf16[2,768,768]{2,1,0:T(8,128)(2,1)S(1)} %pad_maximum_fusion.1.down_even), channel_id=1, source_target_pairs={{0,1},{1,0},{2,3},{3,2},{4,5},{5,4},{6,7},{7,6},{8,9},{9,8},{10,11... | collective-permute-start | bytes 7077896 | tf_op jit(solution)/shard_map/ppermute | solution.py:35
  91.7 14.6 %collective-permute-start.19 = (bf16[976,768]{1,0:T(8,128)(2,1)S(1)}, bf16[976,768]{1,0:T(8,128)(2,1)S(1)}, u32[]{:S(2)}, u32[]{:S(2)}) collective-permute-start(bf16[976,768]{1,0:T(8,128)(2,1)S(1)} %collective-permute-done.13.up2), channel_id=1, source_target_pairs={{0,1},{1,0},{2,3},{3,2},{4,5},{5,4},{6,7},{7,6},{8,9},{9,8},{10,11... | collective-permute-start | bytes 4497416 | tf_op jit(solution)/shard_map/ppermute | solution.py:35
  92.3 6.4 %collective-permute-start.16 = (bf16[512,256]{1,0:T(8,128)(2,1)S(1)}, bf16[512,256]{1,0:T(8,128)(2,1)S(1)}, u32[]{:S(2)}, u32[]{:S(2)}) collective-permute-start(bf16[512,256]{1,0:T(8,128)(2,1)S(1)} %bitcast.201), channel_id=1, source_target_pairs={{0,1},{1,0},{2,3},{3,2},{4,5},{5,4},{6,7},{7,6},{8,9},{9,8},{10,11... | collective-permute-start | bytes 786440 | tf_op jit(solution)/shard_map/ppermute | solution.py:35
  92.4 9.1 %collective-permute-start.17 = (bf16[512,256]{1,0:T(8,128)(2,1)S(1)}, bf16[512,256]{1,0:T(8,128)(2,1)S(1)}, u32[]{:S(2)}, u32[]{:S(2)}) collective-permute-start(bf16[512,256]{1,0:T(8,128)(2,1)S(1)} %bitcast.200), channel_id=1, source_target_pairs={{0,2},{1,3},{2,0},{3,1},{4,6},{5,7},{6,4},{7,5},{8,10},{9,11},{10,... | collective-permute-start | bytes 786440 | tf_op jit(solution)/shard_map/ppermute | solution.py:35
  93.0 13.3 %collective-permute-start.18 = (bf16[512,256]{1,0:T(8,128)(2,1)S(1)}, bf16[512,256]{1,0:T(8,128)(2,1)S(1)}, u32[]{:S(2)}, u32[]{:S(2)}) collective-permute-start(bf16[512,256]{1,0:T(8,128)(2,1)S(1)} %bitcast.199), channel_id=1, source_target_pairs={{0,3},{1,2},{2,1},{3,0},{4,7},{5,6},{6,5},{7,4},{8,11},{9,10},{10,... | collective-permute-start | bytes 786440 | tf_op jit(solution)/shard_map/ppermute | solution.py:35
  138.7 6.5 %collective-permute-start.21 = (bf16[2,768,768]{2,1,0:T(8,128)(2,1)}, bf16[2,768,768]{2,1,0:T(8,128)(2,1)S(1)}, u32[]{:S(2)}, u32[]{:S(2)}) collective-permute-start(bf16[2,768,768]{2,1,0:T(8,128)(2,1)} %get-tuple-element.119), channel_id=1, source_target_pairs={{0,1},{1,0},{2,3},{3,2},{4,5},{5,4},{6,7},{7,6},{8,9},{9,8},{10,11... | collective-permute-start | bytes 7077896 | tf_op jit(solution)/shard_map/ppermute | solution.py:35
  139.1 8.7 %collective-permute-start.23 = (bf16[2,768,768]{2,1,0:T(8,128)(2,1)}, bf16[2,768,768]{2,1,0:T(8,128)(2,1)S(1)}, u32[]{:S(2)}, u32[]{:S(2)}) collective-permute-start(bf16[2,768,768]{2,1,0:T(8,128)(2,1)} %get-tuple-element.123), channel_id=1, source_target_pairs={{0,1},{1,0},{2,3},{3,2},{4,5},{5,4},{6,7},{7,6},{8,9},{9,8},{10,11... | collective-permute-start | bytes 7077896 | tf_op jit(solution)/shard_map/ppermute | solution.py:35
  139.3 5.7 %collective-permute-start.22 = (bf16[2,192,768]{2,1,0:T(8,128)(2,1)S(1)}, bf16[2,192,768]{2,1,0:T(8,128)(2,1)S(1)}, u32[]{:S(2)}, u32[]{:S(2)}) collective-permute-start(bf16[2,192,768]{2,1,0:T(8,128)(2,1)S(1)} %get-tuple-element.121), channel_id=1, source_target_pairs={{0,1},{1,0},{2,3},{3,2},{4,5},{5,4},{6,7},{7,6},{8,9},{9,8},{10,11... | collective-permute-start | bytes 1769480 | tf_op jit(solution)/shard_map/ppermute | solution.py:35
  140.4 11.3 %collective-permute-start.26 = (bf16[512,256]{1,0:T(8,128)(2,1)}, bf16[512,256]{1,0:T(8,128)(2,1)S(1)}, u32[]{:S(2)}, u32[]{:S(2)}) collective-permute-start(bf16[512,256]{1,0:T(8,128)(2,1)} %get-tuple-element.201), channel_id=1, source_target_pairs={{0,3},{1,2},{2,1},{3,0},{4,7},{5,6},{6,5},{7,4},{8,11},{9,10},{10,... | collective-permute-start | bytes 786440 | tf_op jit(solution)/shard_map/ppermute | solution.py:35
  140.8 14.2 %collective-permute-start.25 = (bf16[512,256]{1,0:T(8,128)(2,1)}, bf16[512,256]{1,0:T(8,128)(2,1)}, u32[]{:S(2)}, u32[]{:S(2)}) collective-permute-start(bf16[512,256]{1,0:T(8,128)(2,1)} %get-tuple-element.202), channel_id=1, source_target_pairs={{0,2},{1,3},{2,0},{3,1},{4,6},{5,7},{6,4},{7,5},{8,10},{9,11},{10,... | collective-permute-start | bytes 786440 | tf_op jit(solution)/shard_map/ppermute | solution.py:35
  150.8 4.2 %collective-permute-start.24 = (bf16[512,256]{1,0:T(8,128)(2,1)S(1)}, bf16[512,256]{1,0:T(8,128)(2,1)}, u32[]{:S(2)}, u32[]{:S(2)}) collective-permute-start(bf16[512,256]{1,0:T(8,128)(2,1)S(1)} %get-tuple-element.124), channel_id=1, source_target_pairs={{0,1},{1,0},{2,3},{3,2},{4,5},{5,4},{6,7},{7,6},{8,9},{9,8},{10,11... | collective-permute-start | bytes 786440 | tf_op jit(solution)/shard_map/ppermute | solution.py:35
  156.1 35.3 %collective-permute-start.27 = (bf16[960,768]{1,0:T(8,128)(2,1)S(1)}, bf16[960,768]{1,0:T(8,128)(2,1)S(1)}, u32[]{:S(2)}, u32[]{:S(2)}) collective-permute-start(bf16[960,768]{1,0:T(8,128)(2,1)S(1)} %copy-done.24), channel_id=1, source_target_pairs={{0,2},{1,3},{2,0},{3,1},{4,6},{5,7},{6,4},{7,5},{8,10},{9,11},{10,... | collective-permute-start | bytes 4423688 | tf_op jit(solution)/shard_map/ppermute | solution.py:35
  158.1 33.0 %collective-permute-start.28 = (bf16[2,384,768]{2,1,0:T(8,128)(2,1)S(1)}, bf16[2,384,768]{2,1,0:T(8,128)(2,1)S(1)}, u32[]{:S(2)}, u32[]{:S(2)}) collective-permute-start(bf16[2,384,768]{2,1,0:T(8,128)(2,1)S(1)} %dynamic-slice_bitcast_fusion), channel_id=1, source_target_pairs={{0,16},{16,0},{1,17},{17,1},{2,18},{18,2},{3,19},{19,3},{4,20},{20... | collective-permute-start | bytes 3538952 | tf_op jit(solution)/shard_map/ppermute | solution.py:35
  160.4 28.7 %collective-permute-start.29 = (bf16[1,128,768]{2,1,0:T(8,128)(2,1)S(1)}, bf16[1,128,768]{2,1,0:T(8,128)(2,1)S(1)}, u32[]{:S(2)}, u32[]{:S(2)}) collective-permute-start(bf16[1,128,768]{2,1,0:T(8,128)(2,1)S(1)} %get-tuple-element.220), channel_id=1, source_target_pairs={{4,0},{8,4},{12,8},{0,12},{5,1},{9,5},{13,9},{1,13},{6,2},{10,6},{... | collective-permute-start | bytes 589832 | tf_op jit(solution)/shard_map/ppermute | solution.py:158
  163.1 26.6 %collective-permute-start.30 = (bf16[1,128,768]{2,1,0:T(8,128)(2,1)S(1)}, bf16[1,128,768]{2,1,0:T(8,128)(2,1)S(1)}, u32[]{:S(2)}, u32[]{:S(2)}) collective-permute-start(bf16[1,128,768]{2,1,0:T(8,128)(2,1)S(1)} %get-tuple-element.219), channel_id=1, source_target_pairs={{8,0},{12,4},{0,8},{4,12},{9,1},{13,5},{1,9},{5,13},{10,2},{14,6},... | collective-permute-start | bytes 589832 | tf_op jit(solution)/shard_map/ppermute | solution.py:158
  164.9 25.5 %collective-permute-start.31 = (bf16[1,128,768]{2,1,0:T(8,128)(2,1)S(1)}, bf16[1,128,768]{2,1,0:T(8,128)(2,1)S(1)}, u32[]{:S(2)}, u32[]{:S(2)}) collective-permute-start(bf16[1,128,768]{2,1,0:T(8,128)(2,1)S(1)} %get-tuple-element.218), channel_id=1, source_target_pairs={{12,0},{0,4},{4,8},{8,12},{13,1},{1,5},{5,9},{9,13},{14,2},{2,6},{... | collective-permute-start | bytes 589832 | tf_op jit(solution)/shard_map/ppermute | solution.py:158
  164.9 26.2 %copy-start.9 = (bf16[2,768,768]{2,1,0:T(8,128)(2,1)S(1)}, bf16[2,768,768]{2,1,0:T(8,128)(2,1)}, u32[]{:S(2)}) copy-start(bf16[2,768,768]{2,1,0:T(8,128)(2,1)} %add_convert_fusion.1) | copy-start | bytes 7077892
  195.7 17.1 %collective-permute-start.32 = (bf16[480,768]{1,0:T(8,128)(2,1)S(1)}, bf16[480,768]{1,0:T(8,128)(2,1)S(1)}, u32[]{:S(2)}, u32[]{:S(2)}) collective-permute-start(bf16[480,768]{1,0:T(8,128)(2,1)S(1)} %pad_maximum_fusion.9), channel_id=1, source_target_pairs={{0,16},{16,0},{1,17},{17,1},{2,18},{18,2},{3,19},{19,3},{4,20},{20... | collective-permute-start | bytes 2211848 | tf_op jit(solution)/shard_map/ppermute | solution.py:35
  195.8 14.0 %collective-permute-start.33 = (bf16[384,768]{1,0:T(8,128)(2,1)S(1)}, bf16[384,768]{1,0:T(8,128)(2,1)S(1)}, u32[]{:S(2)}, u32[]{:S(2)}) collective-permute-start(bf16[384,768]{1,0:T(8,128)(2,1)S(1)} %slice_bitcast_fusion), channel_id=1, source_target_pairs={{0,2},{1,3},{2,0},{3,1},{4,6},{5,7},{6,4},{7,5},{8,10},{9,11},{10,... | collective-permute-start | bytes 1769480 | tf_op jit(solution)/shard_map/ppermute | solution.py:35
  214.5 3.7 %collective-permute-start.35 = (bf16[256,768]{1,0:T(8,128)(2,1)S(1)}, bf16[256,768]{1,0:T(8,128)(2,1)S(1)}, u32[]{:S(2)}, u32[]{:S(2)}) collective-permute-start(bf16[256,768]{1,0:T(8,128)(2,1)S(1)} %get-tuple-element.192), channel_id=1, source_target_pairs={{0,1},{1,0},{2,3},{3,2},{4,5},{5,4},{6,7},{7,6},{8,9},{9,8},{10,11... | collective-permute-start | bytes 1179656 | tf_op jit(solution)/shard_map/ppermute | solution.py:35
  214.5 3.6 %collective-permute-start.34 = (bf16[256,768]{1,0:T(8,128)(2,1)S(1)}, bf16[256,768]{1,0:T(8,128)(2,1)S(1)}, u32[]{:S(2)}, u32[]{:S(2)}) collective-permute-start(bf16[256,768]{1,0:T(8,128)(2,1)S(1)} %get-tuple-element.193), channel_id=1, source_target_pairs={{0,1},{1,0},{2,3},{3,2},{4,5},{5,4},{6,7},{7,6},{8,9},{9,8},{10,11... | collective-permute-start | bytes 1179656 | tf_op jit(solution)/shard_map/ppermute | solution.py:35
  215.1 4.2 %collective-permute-start.37 = (bf16[256,768]{1,0:T(8,128)(2,1)S(1)}, bf16[256,768]{1,0:T(8,128)(2,1)S(1)}, u32[]{:S(2)}, u32[]{:S(2)}) collective-permute-start(bf16[256,768]{1,0:T(8,128)(2,1)S(1)} %get-tuple-element.188), channel_id=1, source_target_pairs={{0,1},{1,0},{2,3},{3,2},{4,5},{5,4},{6,7},{7,6},{8,9},{9,8},{10,11... | collective-permute-start | bytes 1179656 | tf_op jit(solution)/shard_map/ppermute | solution.py:35
  215.2 4.1 %collective-permute-start.36 = (bf16[256,768]{1,0:T(8,128)(2,1)S(1)}, bf16[256,768]{1,0:T(8,128)(2,1)S(1)}, u32[]{:S(2)}, u32[]{:S(2)}) collective-permute-start(bf16[256,768]{1,0:T(8,128)(2,1)S(1)} %get-tuple-element.189), channel_id=1, source_target_pairs={{0,1},{1,0},{2,3},{3,2},{4,5},{5,4},{6,7},{7,6},{8,9},{9,8},{10,11... | collective-permute-start | bytes 1179656 | tf_op jit(solution)/shard_map/ppermute | solution.py:35
  216.7 17.2 %collective-permute-start.45 = (bf16[2,216,768]{2,1,0:T(8,128)(2,1)}, bf16[2,216,768]{2,1,0:T(8,128)(2,1)}, u32[]{:S(2)}, u32[]{:S(2)}) collective-permute-start(bf16[2,216,768]{2,1,0:T(8,128)(2,1)} %dynamic-slice_bitcast_fusion.1), channel_id=1, source_target_pairs={{0,4},{4,0},{8,12},{12,8},{1,5},{5,1},{9,13},{13,9},{2,6},{6,2},{1... | collective-permute-start | bytes 1990664 | tf_op jit(solution)/shard_map/ppermute | solution.py:35
  221.1 16.9 %collective-permute-start.38 = (bf16[256,768]{1,0:T(8,128)(2,1)}, bf16[256,768]{1,0:T(8,128)(2,1)}, u32[]{:S(2)}, u32[]{:S(2)}) collective-permute-start(bf16[256,768]{1,0:T(8,128)(2,1)} %get-tuple-element.148), channel_id=1, source_target_pairs={{0,2},{1,3},{2,0},{3,1},{4,6},{5,7},{6,4},{7,5},{8,10},{9,11},{10,... | collective-permute-start | bytes 1179656 | tf_op jit(solution)/shard_map/ppermute | solution.py:35
  221.7 19.0 %collective-permute-start.39 = (bf16[256,768]{1,0:T(8,128)(2,1)}, bf16[256,768]{1,0:T(8,128)(2,1)}, u32[]{:S(2)}, u32[]{:S(2)}) collective-permute-start(bf16[256,768]{1,0:T(8,128)(2,1)} %get-tuple-element.150), channel_id=1, source_target_pairs={{0,2},{1,3},{2,0},{3,1},{4,6},{5,7},{6,4},{7,5},{8,10},{9,11},{10,... | collective-permute-start | bytes 1179656 | tf_op jit(solution)/shard_map/ppermute | solution.py:35
  228.7 20.1 %collective-permute-start.44 = (bf16[3,96,768]{2,1,0:T(8,128)(2,1)}, bf16[3,96,768]{2,1,0:T(8,128)(2,1)}, u32[]{:S(2)}, u32[]{:S(2)}) collective-permute-start(bf16[3,96,768]{2,1,0:T(8,128)(2,1)} %dynamic-slice_bitcast_fusion.4), channel_id=1, source_target_pairs={{0,16},{16,0},{1,17},{17,1},{2,18},{18,2},{3,19},{19,3},{4,20},{20... | collective-permute-start | bytes 1327112 | tf_op jit(solution)/shard_map/ppermute | solution.py:35
  235.9 17.3 %collective-permute-start.46 = (bf16[216,768]{1,0:T(8,128)(2,1)}, bf16[216,768]{1,0:T(8,128)(2,1)}, u32[]{:S(2)}, u32[]{:S(2)}) collective-permute-start(bf16[216,768]{1,0:T(8,128)(2,1)} %dynamic-slice_bitcast_fusion.5), channel_id=1, source_target_pairs={{0,8},{4,12},{8,0},{12,4},{1,9},{5,13},{9,1},{13,5},{2,10},{6,14},... | collective-permute-start | bytes 995336 | tf_op jit(solution)/shard_map/ppermute | solution.py:35
  242.8 4.4 %collective-permute-start.41 = (f32[72,128]{1,0:T(8,128)S(1)}, f32[72,128]{1,0:T(8,128)S(1)}, u32[]{:S(2)}, u32[]{:S(2)}) collective-permute-start(f32[72,128]{1,0:T(8,128)S(1)} %pad_maximum_fusion.12), channel_id=1, source_target_pairs={{0,2},{1,3},{2,0},{3,1},{4,6},{5,7},{6,4},{7,5},{8,10},{9,11},{10,... | collective-permute-start | bytes 110600 | tf_op jit(solution)/shard_map/ppermute | solution.py:35
  243.4 3.8 %collective-permute-start.42 = (f32[72,128]{1,0:T(8,128)S(1)}, f32[72,128]{1,0:T(8,128)S(1)}, u32[]{:S(2)}, u32[]{:S(2)}) collective-permute-start(f32[72,128]{1,0:T(8,128)S(1)} %pad_maximum_fusion.12), channel_id=1, source_target_pairs={{0,3},{1,2},{2,1},{3,0},{4,7},{5,6},{6,5},{7,4},{8,11},{9,10},{10,... | collective-permute-start | bytes 110600 | tf_op jit(solution)/shard_map/ppermute | solution.py:35
  243.4 3.8 %collective-permute-start.40 = (f32[72,128]{1,0:T(8,128)S(1)}, f32[72,128]{1,0:T(8,128)S(1)}, u32[]{:S(2)}, u32[]{:S(2)}) collective-permute-start(f32[72,128]{1,0:T(8,128)S(1)} %pad_maximum_fusion.12), channel_id=1, source_target_pairs={{0,1},{1,0},{2,3},{3,2},{4,5},{5,4},{6,7},{7,6},{8,9},{9,8},{10,11... | collective-permute-start | bytes 110600 | tf_op jit(solution)/shard_map/ppermute | solution.py:35
  247.2 8.3 %collective-permute-start.43 = (f32[72,128]{1,0:T(8,128)S(1)}, f32[72,128]{1,0:T(8,128)S(1)}, u32[]{:S(2)}, u32[]{:S(2)}) collective-permute-start(f32[72,128]{1,0:T(8,128)S(1)} %add_add_fusion.1), channel_id=1, source_target_pairs={{0,16},{16,0},{1,17},{17,1},{2,18},{18,2},{3,19},{19,3},{4,20},{20... | collective-permute-start | bytes 110600 | tf_op jit(solution)/shard_map/ppermute | solution.py:35
  254.3 10.3 %collective-permute-start.54 = (bf16[2,72,768]{2,1,0:T(8,128)(2,1)S(1)}, bf16[2,72,768]{2,1,0:T(8,128)(2,1)S(1)}, u32[]{:S(2)}, u32[]{:S(2)}) collective-permute-start(bf16[2,72,768]{2,1,0:T(8,128)(2,1)S(1)} %dynamic-slice_bitcast_fusion.6), channel_id=1, source_target_pairs={{0,4},{4,0},{8,12},{12,8},{1,5},{5,1},{9,13},{13,9},{2,6},{6,2},{1... | collective-permute-start | bytes 663560 | tf_op jit(solution)/shard_map/ppermute | solution.py:35
  255.5 21.6 %collective-permute-start.47 = (bf16[216,768]{1,0:T(8,128)(2,1)S(1)}, bf16[216,768]{1,0:T(8,128)(2,1)S(1)}, u32[]{:S(2)}, u32[]{:S(2)}) collective-permute-start(bf16[216,768]{1,0:T(8,128)(2,1)S(1)} %fusion.22), channel_id=1, source_target_pairs={{0,8},{4,12},{8,0},{12,4},{1,9},{5,13},{9,1},{13,5},{2,10},{6,14},... | collective-permute-start | bytes 995336 | tf_op jit(solution)/shard_map/ppermute | solution.py:35
  264.7 13.8 %collective-permute-start.55 = (bf16[72,768]{1,0:T(8,128)(2,1)S(1)}, bf16[72,768]{1,0:T(8,128)(2,1)S(1)}, u32[]{:S(2)}, u32[]{:S(2)}) collective-permute-start(bf16[72,768]{1,0:T(8,128)(2,1)S(1)} %dynamic-slice_bitcast_fusion.9), channel_id=1, source_target_pairs={{0,8},{4,12},{8,0},{12,4},{1,9},{5,13},{9,1},{13,5},{2,10},{6,14},... | collective-permute-start | bytes 331784 | tf_op jit(solution)/shard_map/ppermute | solution.py:35
  278.5 7.8 %collective-permute-start.56 = (bf16[72,768]{1,0:T(8,128)(2,1)S(1)}, bf16[72,768]{1,0:T(8,128)(2,1)S(1)}, u32[]{:S(2)}, u32[]{:S(2)}) collective-permute-start(bf16[72,768]{1,0:T(8,128)(2,1)S(1)} %fusion.26), channel_id=1, source_target_pairs={{0,8},{4,12},{8,0},{12,4},{1,9},{5,13},{9,1},{13,5},{2,10},{6,14},... | collective-permute-start | bytes 331784 | tf_op jit(solution)/shard_map/ppermute | solution.py:35
  278.8 10.5 %collective-permute-start.48 = (bf16[1,128,768]{2,1,0:T(8,128)(2,1)S(1)}, bf16[1,128,768]{2,1,0:T(8,128)(2,1)S(1)}, u32[]{:S(2)}, u32[]{:S(2)}) collective-permute-start(bf16[1,128,768]{2,1,0:T(8,128)(2,1)S(1)} %get-tuple-element.212), channel_id=1, source_target_pairs={{4,0},{8,4},{12,8},{0,12},{5,1},{9,5},{13,9},{1,13},{6,2},{10,6},{... | collective-permute-start | bytes 589832 | tf_op jit(solution)/shard_map/ppermute | solution.py:158
  281.2 21.5 %collective-permute-start.49 = (bf16[1,128,768]{2,1,0:T(8,128)(2,1)S(1)}, bf16[1,128,768]{2,1,0:T(8,128)(2,1)S(1)}, u32[]{:S(2)}, u32[]{:S(2)}) collective-permute-start(bf16[1,128,768]{2,1,0:T(8,128)(2,1)S(1)} %get-tuple-element.211), channel_id=1, source_target_pairs={{8,0},{12,4},{0,8},{4,12},{9,1},{13,5},{1,9},{5,13},{10,2},{14,6},... | collective-permute-start | bytes 589832 | tf_op jit(solution)/shard_map/ppermute | solution.py:158
  283.2 19.5 %collective-permute-start.50 = (bf16[1,128,768]{2,1,0:T(8,128)(2,1)S(1)}, bf16[1,128,768]{2,1,0:T(8,128)(2,1)S(1)}, u32[]{:S(2)}, u32[]{:S(2)}) collective-permute-start(bf16[1,128,768]{2,1,0:T(8,128)(2,1)S(1)} %get-tuple-element.210), channel_id=1, source_target_pairs={{12,0},{0,4},{4,8},{8,12},{13,1},{1,5},{5,9},{9,13},{14,2},{2,6},{... | collective-permute-start | bytes 589832 | tf_op jit(solution)/shard_map/ppermute | solution.py:158
  283.8 35.1 %collective-permute-start.58 = (bf16[2,216,768]{2,1,0:T(8,128)(2,1)S(1)}, bf16[2,216,768]{2,1,0:T(8,128)(2,1)S(1)}, u32[]{:S(2)}, u32[]{:S(2)}) collective-permute-start(bf16[2,216,768]{2,1,0:T(8,128)(2,1)S(1)} %pad_maximum_fusion.10), channel_id=1, source_target_pairs={{0,4},{4,0},{8,12},{12,8},{1,5},{5,1},{9,13},{13,9},{2,6},{6,2},{1... | collective-permute-start | bytes 1990664 | tf_op jit(solution)/shard_map/ppermute | solution.py:35
  302.7 16.2 %copy-start.29 = (bf16[4,128,768]{2,1,0:T(8,128)(2,1)}, bf16[4,128,768]{2,1,0:T(8,128)(2,1)S(1)}, u32[]{:S(2)}) copy-start(bf16[4,128,768]{2,1,0:T(8,128)(2,1)S(1)} %constant_dynamic-update-slice_fusion) | copy-start | bytes 2359300
  302.7 7.3 %collective-permute-start.52 = (f32[72,128]{1,0:T(8,128)S(1)}, f32[72,128]{1,0:T(8,128)S(1)}, u32[]{:S(2)}, u32[]{:S(2)}) collective-permute-start(f32[72,128]{1,0:T(8,128)S(1)} %add.435), channel_id=1, source_target_pairs={{0,8},{4,12},{8,0},{12,4},{1,9},{5,13},{9,1},{13,5},{2,10},{6,14},... | collective-permute-start | bytes 110600 | tf_op jit(solution)/shard_map/ppermute | solution.py:35
  303.3 10.0 %collective-permute-start.53 = (f32[72,128]{1,0:T(8,128)S(1)}, f32[72,128]{1,0:T(8,128)S(1)}, u32[]{:S(2)}, u32[]{:S(2)}) collective-permute-start(f32[72,128]{1,0:T(8,128)S(1)} %add.435), channel_id=1, source_target_pairs={{0,12},{4,8},{8,4},{12,0},{1,13},{5,9},{9,5},{13,1},{2,14},{6,10},... | collective-permute-start | bytes 110600 | tf_op jit(solution)/shard_map/ppermute | solution.py:35
  303.8 10.5 %collective-permute-start.51 = (f32[72,128]{1,0:T(8,128)S(1)}, f32[72,128]{1,0:T(8,128)S(1)}, u32[]{:S(2)}, u32[]{:S(2)}) collective-permute-start(f32[72,128]{1,0:T(8,128)S(1)} %add.435), channel_id=1, source_target_pairs={{0,4},{4,0},{8,12},{12,8},{1,5},{5,1},{9,13},{13,9},{2,6},{6,2},{1... | collective-permute-start | bytes 110600 | tf_op jit(solution)/shard_map/ppermute | solution.py:35
  306.3 11.5 %collective-permute-start.57 = (bf16[2,72,768]{2,1,0:T(8,128)(2,1)S(1)}, bf16[2,72,768]{2,1,0:T(8,128)(2,1)S(1)}, u32[]{:S(2)}, u32[]{:S(2)}) collective-permute-start(bf16[2,72,768]{2,1,0:T(8,128)(2,1)S(1)} %pad_maximum_fusion.11), channel_id=1, source_target_pairs={{0,4},{4,0},{8,12},{12,8},{1,5},{5,1},{9,13},{13,9},{2,6},{6,2},{1... | collective-permute-start | bytes 663560 | tf_op jit(solution)/shard_map/ppermute | solution.py:35
  (41 other events, 226.3 us)
